TPU v7x, 128 devices: a whole 4x4x4 slice. The times are simulated.
128 devices in a mesh: ctx: 8 (over x, core), head: 16 (over z, y).
Axes of the slice: x: 4, y: 4, z: 4, core: 2. Of those that a mesh axis runs over, the one named last changes fastest.
Arguments:
- features: bfloat16 [2048, 6144], P('ctx', 'head'), may hold values from -6 to 6
- w_query: bfloat16 [6144, 8192], P(None, 'head'), may hold values from -0.078125 to 0.078125
- w_key: bfloat16 [6144, 8192], P(None, 'head'), may hold values from -0.078125 to 0.078125
- w_value: bfloat16 [6144, 8192], P(None, 'head'), may hold values from -0.078125 to 0.078125
- log_decay: float32 [64, 2048], P('head', 'ctx'), may hold values from -1 to 0, as said below
- d_out: bfloat16 [2048, 8192], P('ctx', 'head'), may hold values from -0.011962891 to 0.011962891
Outputs:
- d_features: bfloat16 [2048, 6144], P(('ctx', 'head'))
Inputs may be any that keep to these rules, and one draw needn't show every extreme that they name: `log_decay`: entries are negative or zero.
All inputs are finite; a program needn't handle non-finite values.
Results may differ from a plain program's by a relative error of at most 0.023.
Values may be sent and summed in bfloat16 or wider, within the bound.
No kernel may reach another device: no remote copies, remote signals or barrier semaphores. Data moves between devices by JAX's collectives and lax.ppermute only.
A program may use at most 128 MiB of HBM per device.

v0:
```python
import jax
import jax.numpy as jnp
from jax import lax
from jax.sharding import PartitionSpec as P

HI = lax.Precision.HIGHEST


def prefix(shard, axis, combine, identity, reverse):
    count, index = (lax.axis_size(axis), lax.axis_index(axis))
    everything = jax.tree.map(
        lambda part, kind: lax.all_gather(part.astype(kind), axis),
        shard,
        (jnp.bfloat16, jnp.bfloat16),
    )
    start = jax.tree.map(
        lambda part, zero: jnp.broadcast_to(jnp.asarray(zero, part.dtype), part.shape),
        shard,
        identity,
    )

    def lap(k, before):
        at = count - 1 - k if reverse else k
        reached = at > index if reverse else at < index
        new = combine(
            before, jax.tree.map(lambda part, own: part[at].astype(own.dtype), everything, shard)
        )
        return jax.tree.map(lambda a, b: jnp.where(reached, a, b), new, before)

    return lax.fori_loop(0, count, lap, start)


def split_heads(flat, head_count):
    return flat.reshape(flat.shape[0], head_count, -1).transpose(1, 0, 2)


def merge_heads(stacked):
    return stacked.transpose(1, 0, 2).reshape(stacked.shape[1], -1)


def forward_combine(earlier, later):
    return (earlier[0] + later[0], jnp.exp(later[0])[:, None, None] * earlier[1] + later[1])


def backward_combine(earlier, later):
    return (later[0] + earlier[0], later[1] + jnp.exp(later[0])[:, None, None] * earlier[1])


def shards(features, w_query, w_key, w_value, log_decay, d_out):
    f32 = jnp.float32
    row_count = features.shape[0]
    head_count = log_decay.shape[0]
    column_piece = lax.all_gather(features, "head", axis=1, tiled=True)
    query_sum = jnp.dot(column_piece, w_query, preferred_element_type=f32)
    key_sum = jnp.dot(column_piece, w_key, preferred_element_type=f32)
    value_sum = jnp.dot(column_piece, w_value, preferred_element_type=f32)
    queries = split_heads(query_sum.astype(jnp.bfloat16), head_count)
    keys_local = split_heads(key_sum.astype(jnp.bfloat16), head_count)
    values_local = split_heads(value_sum.astype(jnp.bfloat16), head_count)
    grads_out = split_heads(d_out, head_count)
    cumul = jnp.cumsum(log_decay, axis=1)
    total = cumul[:, -1]
    causal = jnp.tril(jnp.ones((row_count, row_count), dtype=bool))
    differ = cumul[:, :, None] - cumul[:, None, :]
    weights = jnp.where(causal[None], jnp.exp(jnp.minimum(differ, 0.0)), 0.0)
    tail = jnp.exp(total[:, None] - cumul)
    leading = jnp.exp(cumul)
    local_state = jnp.einsum(
        "hsi,hsj->hij",
        keys_local.astype(f32) * tail[:, :, None],
        values_local.astype(f32),
        precision=HI,
    )
    local_grad = jnp.einsum(
        "hti,htj->hij",
        queries.astype(f32) * leading[:, :, None],
        grads_out.astype(f32),
        precision=HI,
    )
    zero_total = jnp.zeros_like(total)
    zero_state = jnp.zeros_like(local_state)
    prefix_unused, state_in = prefix(
        (total, local_state), "ctx", forward_combine, (zero_total, zero_state), False
    )
    suffix_unused, grad_in = prefix(
        (total, local_grad), "ctx", backward_combine, (zero_total, zero_state), True
    )
    state_low = state_in.astype(jnp.bfloat16)
    grad_low = grad_in.astype(jnp.bfloat16)
    scores = (
        jnp.einsum("hti,hsi->hts", queries, keys_local, preferred_element_type=f32) * weights
    ).astype(jnp.bfloat16)
    mixing = (
        jnp.einsum("htj,hsj->hts", grads_out, values_local, preferred_element_type=f32) * weights
    ).astype(jnp.bfloat16)
    grad_query = jnp.einsum("hts,hsi->hti", mixing, keys_local, preferred_element_type=f32)
    grad_query = grad_query + leading[:, :, None] * jnp.einsum(
        "htj,hij->hti", grads_out, state_low, preferred_element_type=f32
    )
    grad_key = jnp.einsum("hts,hti->hsi", mixing, queries, preferred_element_type=f32)
    grad_key = grad_key + tail[:, :, None] * jnp.einsum(
        "hsj,hij->hsi", values_local, grad_low, preferred_element_type=f32
    )
    grad_value = jnp.einsum("hts,htj->hsj", scores, grads_out, preferred_element_type=f32)
    grad_value = grad_value + tail[:, :, None] * jnp.einsum(
        "hsi,hij->hsj", keys_local, grad_low, preferred_element_type=f32
    )
    query_grad_flat = merge_heads(grad_query.astype(jnp.bfloat16))
    key_grad_flat = merge_heads(grad_key.astype(jnp.bfloat16))
    value_grad_flat = merge_heads(grad_value.astype(jnp.bfloat16))
    summed = jnp.einsum("tc,dc->td", query_grad_flat, w_query, preferred_element_type=f32)
    summed = summed + jnp.einsum("tc,dc->td", key_grad_flat, w_key, preferred_element_type=f32)
    return lax.psum_scatter(
        (
            summed + jnp.einsum("tc,dc->td", value_grad_flat, w_value, preferred_element_type=f32)
        ).astype(jnp.bfloat16),
        "head",
        scatter_dimension=0,
        tiled=True,
    )


def solution(mesh):
    return jax.shard_map(
        shards,
        mesh=mesh,
        in_specs=(
            P("ctx", "head"),
            P(None, "head"),
            P(None, "head"),
            P(None, "head"),
            P("head", "ctx"),
            P("ctx", "head"),
        ),
        out_specs=P(("ctx", "head"), None),
        check_vma=False,
    )
```

profile of v0, /device:TPU:0, one launch (start us, length us, event | category | flops | bytes accessed | tf_op | source)
XLA Modules:
  0.0 224.2 jit_solution(17450735024143367338)
XLA Ops:
  6.5 0.0 all-gather.7.cloned.1.call-start
  6.5 0.7 all-gather.7.cloned.1.call-update
  7.3 0.0 all-gather.11.cloned.1.call-start
  7.3 0.7 reshape.133
  8.0 1.2 reduce-window.6
  9.2 0.1 slice.15
  9.3 0.1 copy.42
  9.5 0.1 copy.43
  9.6 0.1 add_bitcast_fusion
  9.6 0.1 slice.16
  9.7 0.1 copy.75
  9.8 1.2 dynamic-slice
  11.7 0.2 dynamic-update-slice
  12.0 14.7 %all-reduce = bf16[32]{0:T(256)(128)(2,1)S(1)} all-reduce(bf16[32]{0:T(256)(128)(2,1)S(1)} %dynamic-update-slice), channel_id=2, replica_groups=mesh['ctx'=8,'head'=16] {'ctx'}, use_global_device_ids=true, to_apply=%add | all-reduce | flops 32 | bytes 128
  26.7 0.1 reshape.142
  26.8 1.1 copy.70
  27.9 0.1 fusion.44
  28.0 36.8 %all-gather.7.cloned.1.call-done = bf16[256,6144]{1,0:T(8,128)(2,1)} async-done(((bf16[256,384]{1,0:T(8,128)(2,1)}), bf16[256,6144]{1,0:T(8,128)(2,1)}) %all-gather.7.cloned.1.call-update) | async-done | bytes 3145744 | tf_op jit(solution)/shard_map/all_gather | solution.py:53
  64.7 5.5 %fusion.17 = bf16[32,4,8,128]{3,2,1,0:T(8,128)(2,1)S(1)} fusion(bf16[256,6144]{1,0:T(8,128)(2,1)} %all-gather.7.cloned.1.call-done, bf16[6144,512]{1,0:T(8,128)(2,1)} %param.11), kind=kOutput, calls=%fused_computation.34 | convolution fusion | flops 1610743808 | bytes 9699328 | tf_op jit(solution)/shard_map/dot_general | solution.py:54
  70.2 1.4 convolution_convert_fusion.3
  71.7 0.0 all-gather.11.cloned.1.call-update
  71.7 0.0 all-gather.9.cloned.1.call-start
  71.8 0.0 copy-start
  71.8 5.7 %fusion.16 = bf16[32,4,8,128]{3,2,1,0:T(8,128)(2,1)S(1)} fusion(bf16[256,6144]{1,0:T(8,128)(2,1)} %all-gather.7.cloned.1.call-done, bf16[6144,512]{1,0:T(8,128)(2,1)} %param.12), kind=kOutput, calls=%fused_computation.33 | convolution fusion | flops 1610743808 | bytes 9699328 | tf_op jit(solution)/shard_map/dot_general | solution.py:55
  77.4 0.0 copy-done
  77.4 4.6 %fusion.15 = bf16[32,4,8,128]{3,2,1,0:T(8,128)(2,1)S(1)} fusion(bf16[256,6144]{1,0:T(8,128)(2,1)S(1)} %copy-done, bf16[6144,512]{1,0:T(8,128)(2,1)} %param.13), kind=kOutput, calls=%fused_computation.32 | convolution fusion | flops 1610743808 | bytes 9699328 | tf_op jit(solution)/shard_map/dot_general | solution.py:56
  82.1 1.5 convolution_convert_fusion.4
  83.5 0.4 fusion.5
  83.9 0.3 convolution_bitcast_fusion.6
  84.2 0.3 convolution_bitcast_fusion.4
  84.5 0.6 convolution_bitcast_fusion.2
  85.1 0.0 all-gather.9.cloned.1.call-update
  85.1 0.2 reduce-scatter.2.cloned.1.call-start
  85.3 9.1 %all-gather.11.cloned.1.call-done = bf16[32,128,128]{2,1,0:T(8,128)(2,1)} async-done(((bf16[4,128,128]{2,1,0:T(8,128)(2,1)}), bf16[32,128,128]{2,1,0:T(8,128)(2,1)}) %all-gather.11.cloned.1.call-update) | async-done | bytes 1048592 | tf_op jit(solution)/shard_map/all_gather | solution.py:12
  94.4 8.5 %while.31 = (s32[]{:T(128)}, f32[4,128,128]{2,1,0:T(8,128)S(1)}, s32[]{:T(128)}, bf16[8,4,128,128]{3,2,1,0:T(8,128)(2,1)}, bf16[8,4]{1,0:T(8,128)(2,1)S(1)}, /*index=5*/s32[]{:T(128)}, s32[]{:T(128)}, s32[]{:T(128)}, s32[]{:T(128)}) while((s32[]{:T(128)}, f32[4,128,128]{2,1,0:T(8,128)S(1)}, s32[]{:T(128)}, ...), condition=%wide.region_5.6_spmd.clone, body=%wide.region_4.5_spmd.clone.sunk | while | flops 327692 | bytes 655575 | solution.py:30
  94.4 1.0 fusion.67
  95.5 1.0 fusion.67
  96.6 1.0 fusion.67
  97.6 1.0 fusion.67
  98.7 1.0 fusion.67
  99.8 1.0 fusion.67
  100.8 1.0 fusion.67
  101.9 1.0 fusion.67
  102.9 16.5 %all-gather.9.cloned.1.call-done = bf16[32,128,128]{2,1,0:T(8,128)(2,1)} async-done(((bf16[4,128,128]{2,1,0:T(8,128)(2,1)}), bf16[32,128,128]{2,1,0:T(8,128)(2,1)}) %all-gather.9.cloned.1.call-update) | async-done | bytes 1048592 | tf_op jit(solution)/shard_map/all_gather | solution.py:12
  119.4 8.4 %while.30 = (s32[]{:T(128)}, f32[4,128,128]{2,1,0:T(8,128)S(1)}, s32[]{:T(128)}, bf16[8,4]{1,0:T(8,128)(2,1)S(1)}, bf16[8,4,128,128]{3,2,1,0:T(8,128)(2,1)}, /*index=5*/s32[]{:T(128)}, s32[]{:T(128)}) while((s32[]{:T(128)}, f32[4,128,128]{2,1,0:T(8,128)S(1)}, s32[]{:T(128)}, bf16[8,4]{1,0:T(8,128)(2,1)S(1)}, ...), condition=%wide.region_3.4_spmd.clone, body=%wide.region_2.3_spmd.clone.sunk | while | flops 327688 | bytes 655513 | solution.py:30
  119.4 1.0 fusion.66
  120.4 1.0 fusion.66
  121.5 1.0 fusion.66
  122.6 1.0 fusion.66
  123.6 1.0 fusion.66
  124.7 1.0 fusion.66
  125.7 1.0 fusion.66
  126.8 1.0 fusion.66
  127.8 0.3 fusion.12
  128.1 0.2 fusion.13
  128.3 0.0 slice-start
  128.3 0.2 fusion.14
  128.6 0.0 slice-start.1
  128.6 4.8 %fusion.45 = f32[256,6144]{1,0:T(8,128)S(1)} fusion(bf16[256,512]{0,1:T(8,128)(2,1)S(1)} %bitcast.157, bf16[6144,512]{1,0:T(8,128)(2,1)} %param.11), kind=kOutput, calls=%fused_computation.72 | convolution fusion | flops 1610612736 | bytes 12845056 | tf_op jit(solution)/shard_map/tc,dc->td/dot_general | solution.py:111
  133.4 0.0 slice-done
  133.4 1.9 convolution_add_fusion.1
  135.3 6.3 %fusion.2 = bf16[256,6144]{1,0:T(8,128)(2,1)} fusion(f32[256,6144]{1,0:T(8,128)S(1)} %convolution_add_fusion.1, bf16[256,512]{0,1:T(8,128)(2,1)S(1)} %bitcast.155, bf16[6144,512]{1,0:T(8,128)(2,1)} %param.13), kind=kOutput, calls=%fused_computation.8 | convolution fusion | flops 1613758464 | bytes 15990784 | tf_op jit(solution)/shard_map/tc,dc->td/dot_general | solution.py:115
  141.6 0.0 reduce-scatter.2.cloned.1.call-update
  141.6 76.0 %reduce-scatter.2.cloned.1.call-done = bf16[16,6144]{1,0:T(8,128)(2,1)} async-done(((bf16[256,6144]{1,0:T(8,128)(2,1)}), bf16[16,6144]{1,0:T(8,128)(2,1)}) %reduce-scatter.2.cloned.1.call-update) | async-done | bytes 196624 | tf_op jit(solution)/shard_map/reduce_scatter | solution.py:113
  (26 shorter events, 0.2 us)
Async XLA Ops:
  6.5 58.2 %all-gather.7.cloned.1.call-start = ((), (), s32[]{:S(2)}) async-start(), calls=%async_computation.1 | async-start | bytes 3342336 | tf_op jit(solution)/shard_map/all_gather | solution.py:53
  7.3 87.2 %all-gather.11.cloned.1.call-start = ((), (), s32[]{:S(2)}) async-start(), calls=%async_computation.4 | async-start | bytes 1179648 | tf_op jit(solution)/shard_map/all_gather | solution.py:12
  71.7 47.7 %all-gather.9.cloned.1.call-start = ((), (), s32[]{:S(2)}) async-start(), calls=%async_computation.3 | async-start | bytes 1179648 | tf_op jit(solution)/shard_map/all_gather | solution.py:12
  71.8 5.7 %copy-start = (bf16[256,6144]{1,0:T(8,128)(2,1)S(1)}, bf16[256,6144]{1,0:T(8,128)(2,1)}, u32[]{:S(2)}) copy-start(bf16[256,6144]{1,0:T(8,128)(2,1)} %all-gather.7.cloned.1.call-done) | copy-start | bytes 9437188
  85.1 132.6 %reduce-scatter.2.cloned.1.call-start = ((), (), s32[]{:S(2)}) async-start(), calls=%async_computation.2 | async-start | bytes 3342336 | tf_op jit(solution)/shard_map/reduce_scatter | solution.py:113
  128.3 5.1 %slice-start = ((s8[6291456]{0:T(1024)(128)(4,1)}), s8[4194304]{0:T(1024)(128)(4,1)S(1)}, s32[]{:S(2)}) async-start(s8[6291456]{0:T(1024)(128)(4,1)} %bitcast.153), calls=%async_computation.5 | async-start | bytes 8388608
  128.6 4.8 %slice-start.1 = ((s8[6291456]{0:T(1024)(128)(4,1)}), s8[2097152]{0:T(1024)(128)(4,1)S(1)}, s32[]{:S(2)}) async-start(s8[6291456]{0:T(1024)(128)(4,1)} %bitcast.153), calls=%async_computation.6 | async-start | bytes 4194304
Sparse Core Ops, SparseCore 0:
  9.5 55.1 all-gather.6
  71.8 22.5 all-gather.10
  96.1 23.1 all-gather.8
  141.8 75.8 reduce-scatter.1
where the time goes:
time: 225 us; the launch traced here: 224 us
  waiting for transfers between devices  139 us (62%)
  matrix products  33.9 us (15%)
  other arithmetic  17.8 us (8%)
  blocking collectives  14.7 us (7%)
  between operations  14 us (6%)
  local copies, waits for them, and re-layouts  3.84 us (2%)
    reduce_scatter x1, waiting for transfers between devices, shards(): lax.psum_scatter((summed + jnp.einsum('tc,dc->td', value_grad_flat, w_val...  76 us
    all_gather x1, waiting for transfers between devices, shards(): column_piece = lax.all_gather(features, 'head', axis=1, tiled=True)  36.8 us
    all_gather x2, waiting for transfers between devices, prefix(): lax.all_gather(part.astype(kind), axis)  25.6 us
    select_n x16, other arithmetic, lap(): return jax.tree.map(lambda a, b: jnp.where(reached, a, b), new, before)  16.2 us
    unnamed x1, blocking collectives  14.7 us
    dot_general x1, matrix products, shards(): jnp.einsum('tc,dc->td', value_grad_flat, w_value, preferred_element_type=...  6.29 us
    dot_general x1, matrix products, shards(): key_sum = jnp.dot(column_piece, w_key, preferred_element_type=f32)  5.67 us
    dot_general x1, matrix products, shards(): query_sum = jnp.dot(column_piece, w_query, preferred_element_type=f32)  5.52 us
  transfers between devices with their start and end apart: 4, of which 4 were waited for; matrix products, arithmetic and copies ran while one was open for 12% of the time, Pallas kernels for 0%

commit v1 on v0

v1 whole, which is shorter than its diff:
```python
import functools

import jax
import jax.numpy as jnp
from jax import lax
from jax.experimental import pallas as pl
from jax.experimental.pallas import tpu as pltpu
from jax.sharding import PartitionSpec as P

F32, BF16 = jnp.float32, jnp.bfloat16
HI = lax.Precision.HIGHEST
AXES = ("ctx", "head")
REL = (0, 1, 3, 2)
SIDE = 4
DH = 128
MIB = 2**20
VMEM = pl.BlockSpec(memory_space=pltpu.VMEM)
SMEM = pl.BlockSpec(memory_space=pltpu.SMEM)


def device(x, core, z, y):
    return (x * 2 + core) * 16 + z * 4 + y


def everywhere():
    for x in range(4):
        for core in range(2):
            for z in range(4):
                for y in range(4):
                    yield x, core, z, y


def plane_perm(first, offset):
    pairs = []
    for x, core, z, y in everywhere():
        along_y = (core == 0) == first
        to = (z, (y + offset) % 4) if along_y else ((z + offset) % 4, y)
        pairs.append((device(x, core, z, y), device(x, core, *to)))
    return pairs


def core_perm():
    return [(device(x, c, z, y), device(x, 1 - c, z, y)) for x, c, z, y in everywhere()]


def chip_perm(offset):
    return [
        (device(x, c, z, y), device((x + offset) % 4, c, z, y)) for x, c, z, y in everywhere()
    ]


def move(array, pairs):
    return lax.ppermute(array, AXES, pairs)


def params(mib):
    return pltpu.CompilerParams(vmem_limit_bytes=mib * MIB)


def cost(flops, moved):
    return pl.CostEstimate(flops=flops, bytes_accessed=moved, transcendentals=0)


def nt(a, b):
    return lax.dot_general(a, b, (((1,), (1,)), ((), ())), preferred_element_type=F32)


def tn(a, b):
    return lax.dot_general(a, b, (((0,), (0,)), ((), ())), preferred_element_type=F32)


def nn(a, b):
    return jnp.dot(a, b, preferred_element_type=F32)


def decay_kernel(decay_ref, weights_ref, lead_ref, tail_ref):
    heads, rows = decay_ref.shape
    decay = decay_ref[...]
    row = lax.broadcasted_iota(jnp.int32, (rows, rows), 0)
    column = lax.broadcasted_iota(jnp.int32, (rows, rows), 1)
    causal = column <= row
    lower = jnp.where(causal, 1.0, 0.0)
    upright = lax.dot_general(
        lower, decay, (((1,), (1,)), ((), ())), precision=HI, preferred_element_type=F32
    )
    flat = lax.dot_general(
        decay, lower, (((1,), (1,)), ((), ())), precision=HI, preferred_element_type=F32
    )
    for h in range(heads):
        at_t = upright[:, h : h + 1]
        at_s = flat[h : h + 1, :]
        weights_ref[h] = jnp.where(causal, jnp.exp(jnp.minimum(at_t - at_s, 0.0)), 0.0)
        total = flat[h : h + 1, rows - 1 : rows]
        span = slice(h * DH, (h + 1) * DH)
        lead_ref[:, span] = jnp.broadcast_to(jnp.exp(at_t), (rows, DH))
        tail_ref[:, span] = jnp.broadcast_to(jnp.exp(total - at_t), (rows, DH))


def decay_factors(log_decay):
    heads, rows = log_decay.shape
    wide = jax.ShapeDtypeStruct((rows, heads * DH), F32)
    return pl.pallas_call(
        decay_kernel,
        out_shape=(jax.ShapeDtypeStruct((heads, rows, rows), F32), wide, wide),
        in_specs=[VMEM],
        out_specs=(VMEM, VMEM, VMEM),
        compiler_params=params(8),
        cost_estimate=cost(2_000_000, 2_000_000),
        name="decay",
    )(log_decay)


def project_kernel(has_sum, slot, ids_ref, x_ref, *refs):
    sums = refs[:3] if has_sum else None
    weights = refs[3:6] if has_sum else refs[:3]
    outs = refs[-3:]
    width = x_ref.shape[1] // SIDE
    x = x_ref[...]
    starts = [pl.multiple_of(ids_ref[slot * SIDE + j] * width, 128) for j in range(SIDE)]
    for n, (w_ref, out_ref) in enumerate(zip(weights, outs)):
        w = jnp.concatenate([w_ref[pl.ds(s, width), :] for s in starts], axis=0)
        total = nn(x, w)
        if has_sum:
            total = total + sums[n][...]
        out_ref[...] = total.astype(out_ref.dtype)


def project(ids, x, sums, weights, slot, kind):
    rows, columns = x.shape[0], weights[0].shape[1]
    has_sum = sums is not None
    out = jax.ShapeDtypeStruct((rows, columns), kind)
    return pl.pallas_call(
        functools.partial(project_kernel, has_sum, slot),
        out_shape=(out,) * 3,
        in_specs=[SMEM] + [VMEM] * (4 + 3 * has_sum),
        out_specs=(VMEM,) * 3,
        compiler_params=params(12),
        cost_estimate=cost(2 * 3 * rows * x.shape[1] * columns, 6_000_000),
        name="project",
    )(ids, x, *(sums or ()), *weights)


def states_kernel(q_ref, k_ref, v_ref, g_ref, lead_ref, tail_ref, l_ref, m_ref, pay_ref):
    rows, columns = q_ref.shape
    heads = columns // DH
    for h in range(heads):
        c = slice(h * DH, (h + 1) * DH)
        s = slice(h * DH, (h + 1) * DH)
        k = (k_ref[:, c].astype(F32) * tail_ref[:, c]).astype(BF16)
        q = (q_ref[:, c].astype(F32) * lead_ref[:, c]).astype(BF16)
        local = tn(k, v_ref[:, c])
        grad = tn(q, g_ref[:, c])
        l_ref[s, :] = local
        m_ref[s, :] = grad
        pay_ref[s, :] = local.astype(BF16)
        pay_ref[pl.ds(columns + h * DH, DH), :] = grad.astype(BF16)
        own = jnp.broadcast_to(lead_ref[rows - 1 : rows, c], (16, DH))
        pay_ref[pl.ds(2 * columns + h * 16, 16), :] = own.astype(BF16)


def states(q, k, v, g, lead, tail):
    columns = q.shape[1]
    state = jax.ShapeDtypeStruct((columns, DH), F32)
    pay = jax.ShapeDtypeStruct((2 * columns + columns // 8, DH), BF16)
    return pl.pallas_call(
        states_kernel,
        out_shape=(state, state, pay),
        in_specs=[VMEM] * 6,
        out_specs=(VMEM,) * 3,
        compiler_params=params(8),
        cost_estimate=cost(70_000_000, 3_000_000),
        name="states",
    )(q, k, v, g, lead, tail)


def intra_kernel(q_ref, k_ref, v_ref, g_ref, weights_ref, dq_ref, dk_ref, dv_ref):
    for h in range(q_ref.shape[1] // DH):
        c = slice(h * DH, (h + 1) * DH)
        q, k, v, g = q_ref[:, c], k_ref[:, c], v_ref[:, c], g_ref[:, c]
        weights = weights_ref[h]
        scores = (nt(q, k) * weights).astype(BF16)
        mixing = (nt(g, v) * weights).astype(BF16)
        dq_ref[:, c] = nn(mixing, k)
        dk_ref[:, c] = tn(mixing, q)
        dv_ref[:, c] = tn(scores, g)


def intra(q, k, v, g, weights):
    out = jax.ShapeDtypeStruct(q.shape, F32)
    return pl.pallas_call(
        intra_kernel,
        out_shape=(out,) * 3,
        in_specs=[VMEM] * 5,
        out_specs=(VMEM,) * 3,
        compiler_params=params(8),
        cost_estimate=cost(340_000_000, 4_000_000),
        name="intra",
    )(q, k, v, g, weights)


def chip_kernel(place_ref, l_ref, m_ref, lead_ref, peer_ref, *pays):
    columns = l_ref.shape[0]
    rows = lead_ref.shape[0]
    heads = columns // DH
    core, x = place_ref[0], place_ref[1]
    first = core == 0
    for h in range(heads):
        s = slice(h * DH, (h + 1) * DH)
        own_decay = lead_ref[rows - 1 : rows, s]
        peer_decay = peer_ref[pl.ds(2 * columns + h * 16, 16), :].astype(F32)[0:1, :]
        peer_l = peer_ref[s, :].astype(F32)
        peer_m = peer_ref[pl.ds(columns + h * DH, DH), :].astype(F32)
        own_l, own_m = l_ref[s, :], m_ref[s, :]
        chip_l = jnp.where(first, peer_decay * own_l + peer_l, own_decay * peer_l + own_l)
        chip_m = jnp.where(first, own_m + own_decay * peer_m, peer_m + peer_decay * own_m)
        decay = jnp.broadcast_to(own_decay * peer_decay, (16, DH)).astype(BF16)
        for d, pay_ref in enumerate(pays, 1):
            pay_ref[s, :] = jnp.where(x + d < 4, chip_l, chip_m).astype(BF16)
            pay_ref[pl.ds(columns + h * 16, 16), :] = decay


def chip_states(place, own_l, own_m, lead, peer):
    columns = own_l.shape[0]
    pay = jax.ShapeDtypeStruct((columns + columns // 8, DH), BF16)
    return pl.pallas_call(
        chip_kernel,
        out_shape=(pay,) * 3,
        in_specs=[SMEM] + [VMEM] * 4,
        out_specs=(VMEM,) * 3,
        compiler_params=params(8),
        cost_estimate=cost(1_000_000, 2_000_000),
        name="chip_states",
    )(place, own_l, own_m, lead, peer)


def inter_kernel(
    place_ref, ids_ref, q_ref, k_ref, v_ref, g_ref, lead_ref, tail_ref, peer_ref, one_ref, two_ref,
    three_ref, dq_ref, dk_ref, dv_ref, out_ref, whole_ref,
):
    rows, columns = q_ref.shape
    core, x = place_ref[0], place_ref[1]
    first = core == 0
    far = (one_ref, two_ref, three_ref)

    def chance(condition):
        return jnp.where(condition, 1.0, 0.0).astype(F32)

    for h in range(columns // DH):
        c = slice(h * DH, (h + 1) * DH)
        peer_decay = peer_ref[pl.ds(2 * columns + h * 16, 16), :].astype(F32)[0:1, :]
        peer_l = peer_ref[c, :].astype(F32)
        peer_m = peer_ref[pl.ds(columns + h * DH, DH), :].astype(F32)
        one, two, three = (r[c, :].astype(F32) for r in far)
        d_one, d_two, d_three = (
            r[pl.ds(columns + h * 16, 16), :].astype(F32)[0:1, :] for r in far
        )
        before = (
            chance(x >= 1) * one
            + (chance(x >= 2) * d_one) * two
            + (chance(x >= 3) * d_one * d_two) * three
        )
        after = (
            chance(x <= 2) * three
            + (chance(x <= 1) * d_three) * two
            + (chance(x <= 0) * d_three * d_two) * one
        )
        state = jnp.where(first, before, peer_decay * before + peer_l).astype(BF16)
        grad = jnp.where(first, peer_decay * after + peer_m, after).astype(BF16)
        k, v, g = k_ref[:, c], v_ref[:, c], g_ref[:, c]
        lead, tail = lead_ref[:, c], tail_ref[:, c]
        dq = dq_ref[:, c] + lead * nt(g, state)
        dk = dk_ref[:, c] + tail * nt(v, grad)
        dv = dv_ref[:, c] + tail * nn(k, grad)
        for n, result in enumerate((dq, dk, dv)):
            whole_ref[:, pl.ds(n * columns + h * DH, DH)] = result.astype(BF16)
    for n in range(16):
        start = pl.multiple_of(ids_ref[n] * 16, 16)
        out_ref[pl.ds(n * 16, 16), :] = whole_ref[pl.ds(start, 16), :]


def inter(place, ids, q, k, v, g, lead, tail, peer, far, within):
    rows, columns = q.shape
    return pl.pallas_call(
        inter_kernel,
        out_shape=jax.ShapeDtypeStruct((rows, 3 * columns), BF16),
        in_specs=[SMEM] * 2 + [VMEM] * 13,
        out_specs=VMEM,
        scratch_shapes=[pltpu.VMEM((rows, 3 * columns), BF16)],
        compiler_params=params(8),
        cost_estimate=cost(150_000_000, 6_000_000),
        name="inter",
    )(place, ids, q, k, v, g, lead, tail, peer, *far, *within)


def output_kernel(start, tile, d_ref, wq_ref, wk_ref, wv_ref, own_ref, *sends):
    rows = d_ref.shape[0]
    piece = rows // SIDE
    inner = wq_ref.shape[1]
    for n in range(own_ref.shape[1] // tile):
        total = jnp.zeros((rows, tile), F32)
        for part, w_ref in enumerate((wq_ref, wk_ref, wv_ref)):
            total += nt(
                d_ref[:, part * inner : (part + 1) * inner],
                w_ref[pl.ds(start + n * tile, tile), :],
            )
        c = slice(n * tile, (n + 1) * tile)
        own_ref[:, c] = total[:piece]
        for slot, send_ref in enumerate(sends, 1):
            send_ref[:, c] = total[slot * piece : (slot + 1) * piece].astype(BF16)


def output(d, weights, start, width):
    rows = d.shape[0]
    piece = rows // SIDE
    send = jax.ShapeDtypeStruct((piece, width), BF16)
    return pl.pallas_call(
        functools.partial(output_kernel, start, 512),
        out_shape=(jax.ShapeDtypeStruct((piece, width), F32),) + (send,) * 3,
        in_specs=[VMEM] * 4,
        out_specs=(VMEM,) * 4,
        compiler_params=params(12),
        cost_estimate=cost(2 * rows * width * d.shape[1], 6_000_000),
        name="output",
    )(d, *weights)


def add_kernel(own_ref, a_ref, b_ref, c_ref, keep_ref, *sends):
    piece = keep_ref.shape[0]
    total = (
        own_ref[...]
        + a_ref[...].astype(F32)
        + b_ref[...].astype(F32)
        + c_ref[...].astype(F32)
    )
    keep_ref[...] = total[:piece].astype(keep_ref.dtype)
    for slot, send_ref in enumerate(sends, 1):
        send_ref[...] = total[slot * piece : (slot + 1) * piece].astype(BF16)


def add(own, parts, last):
    rows, width = own.shape
    piece = rows if last else rows // SIDE
    keep = jax.ShapeDtypeStruct((piece, width), BF16 if last else F32)
    send = jax.ShapeDtypeStruct((piece, width), BF16)
    count = 0 if last else 3
    return pl.pallas_call(
        add_kernel,
        out_shape=(keep,) + (send,) * count,
        in_specs=[VMEM] * 4,
        out_specs=(VMEM,) * (1 + count),
        compiler_params=params(12),
        cost_estimate=cost(2_000_000, 4_000_000),
        name="add",
    )(own, *parts)


def shards(features, w_query, w_key, w_value, log_decay, d_out):
    weights = (w_query, w_key, w_value)
    ctx, head = lax.axis_index("ctx"), lax.axis_index("head")
    x, core = ctx // 2, ctx % 2
    z, y = head // 4, head % 4
    rel = jnp.array(REL, jnp.int32)
    slot, inner = rel[:, None], rel[None, :]
    ids = jnp.where(
        core == 0,
        (z + slot) % 4 * 4 + (y + inner) % 4,
        (z + inner) % 4 * 4 + (y + slot) % 4,
    ).reshape(16)
    place = jnp.stack([core, x])

    near = [move(features, plane_perm(True, -r)) for r in REL[1:]]
    leading, tail, factors = None, None, None
    factors, lead, tail = decay_factors(log_decay)
    mine = jnp.concatenate([features, *near], axis=1)
    blocks = [move(mine, plane_perm(False, -r)) for r in REL[1:]]
    sums = project(ids, mine, None, weights, 0, F32)
    sums = project(ids, blocks[0], sums, weights, 1, F32)
    sums = project(ids, blocks[1], sums, weights, 2, F32)
    q, k, v = project(ids, blocks[2], sums, weights, 3, BF16)

    own_l, own_m, pay = states(q, k, v, d_out, lead, tail)
    peer = move(pay, core_perm())
    chip = chip_states(place, own_l, own_m, lead, peer)
    far = [move(p, chip_perm(d)) for d, p in enumerate(chip, 1)]
    within = intra(q, k, v, d_out, factors)
    d = inter(place, ids, q, k, v, d_out, lead, tail, peer, far, within)

    width = w_query.shape[0] // 2
    kept = []
    for start in (0, width):
        own, *sends = output(d, weights, start, width)
        parts = [move(s, plane_perm(False, r)) for s, r in zip(sends, REL[1:])]
        kept.append((own, parts))
    results = []
    for own, parts in kept:
        keep, *sends = add(own, parts, False)
        parts = [move(s, plane_perm(True, r)) for s, r in zip(sends, REL[1:])]
        results.append((keep, parts))
    return jnp.concatenate([add(keep, parts, True)[0] for keep, parts in results], axis=1)


def solution(mesh):
    return jax.shard_map(
        shards,
        mesh=mesh,
        in_specs=(
            P("ctx", "head"),
            P(None, "head"),
            P(None, "head"),
            P(None, "head"),
            P("head", "ctx"),
            P("ctx", "head"),
        ),
        out_specs=P(("ctx", "head"), None),
        check_vma=False,
    )
```

time: 225 us -> 109 us (0.48)
  waiting for transfers between devices: 139 us -> 30.1 us
  matrix products: 33.9 us -> 0 us
  starting transfers between devices: 0.3 us -> 32.5 us
  Pallas kernels: 0 us -> 21 us
  local copies, waits for them, and re-layouts: 3.84 us -> 23.4 us
  other arithmetic: 17.8 us -> 1.51 us
  blocking collectives: 14.7 us -> 0 us
  between operations: 14 us -> 0.23 us
    reduce_scatter x1 -> x0, waiting for transfers between devices: 76 us -> none  [shards(): lax.psum_scatter((summed + jnp.einsum('tc,dc->td', value_grad_flat, w_val...]
    all_gather x3 -> x0, waiting for transfers between devices: 62.3 us -> none  [the longest x1 36.8 us: shards(): column_piece = lax.all_gather(features, 'head', axis=1, tiled=True)]
    dot_general x15 -> x0, matrix products: 33.9 us -> none  [the longest x1 6.29 us: shards(): jnp.einsum('tc,dc->td', value_grad_flat, w_value, preferred_element_type=...]
    ppermute x0 -> x22, starting transfers between devices: none -> 32.5 us  [move(): return lax.ppermute(array, AXES, pairs)]
    ppermute x0 -> x22, waiting for transfers between devices: none -> 30.1 us  [move(): return lax.ppermute(array, AXES, pairs)]
    unnamed x11 -> x33, local copies, waits for them, and re-layouts: 1.61 us -> 23.2 us
    pallas_call x0 -> x15, Pallas kernels: none -> 21 us  [the longest x4 9.64 us: project(): pl.pallas_call(functools.partial(project_kernel, has_sum, slot), out_shap...]
    select_n x16 -> x1, other arithmetic: 16.2 us -> 0.08 us  [shards(): jnp.where(core == 0, (z + slot) % 4 * 4 + (y + inner) % 4, (z + inner) %...]
  transfers between devices with their start and end apart: 4 -> 22, of which waited for: 4 -> 12; matrix products, arithmetic and copies ran while one was open for 12% -> 2% of each run, Pallas kernels for 0% -> 12%
where the time goes in v1:
time: 109 us
  starting transfers between devices  32.5 us (30%)
  waiting for transfers between devices  30.1 us (28%)
  local copies, waits for them, and re-layouts  23.4 us (21%)
  Pallas kernels  21 us (19%)
  other arithmetic  1.51 us (1%)
    ppermute x22, starting transfers between devices, move(): return lax.ppermute(array, AXES, pairs)  32.5 us
    ppermute x22, waiting for transfers between devices, move(): return lax.ppermute(array, AXES, pairs)  30.1 us
    unnamed x33, local copies, waits for them, and re-layouts  23.2 us
    pallas_call x4, Pallas kernels, project(): pl.pallas_call(functools.partial(project_kernel, has_sum, slot), out_shap...  9.64 us
    pallas_call x2, Pallas kernels, output(): pl.pallas_call(functools.partial(output_kernel, start, 512), out_shape=(j...  5.26 us
  transfers between devices with their start and end apart: 22, of which 12 were waited for; matrix products, arithmetic and copies ran while one was open for 2% of the time, Pallas kernels for 12%

profile of v1, /device:TPU:0, one launch (start us, length us, event | category | flops | bytes accessed | tf_op | source)
XLA Modules:
  0.0 108.8 jit_solution(12280776596365663548)
XLA Ops:
  0.0 3.1 %collective-permute-start = (bf16[256,384]{1,0:T(8,128)(2,1)}, bf16[256,384]{1,0:T(8,128)(2,1)S(1)}, u32[]{:S(2)}, u32[]{:S(2)}) collective-permute-start(bf16[256,384]{1,0:T(8,128)(2,1)} %param.7), channel_id=1, source_target_pairs={{0,3},{1,0},{2,1},{3,2},{4,7},{5,4},{6,5},{7,6},{8,11},{9,8},{10,9... | collective-permute-start | bytes 589832 | tf_op jit(solution)/shard_map/ppermute | solution.py:53
  3.1 0.0 collective-permute-start.1
  3.1 2.2 %collective-permute-start.2 = (bf16[256,384]{1,0:T(8,128)(2,1)}, bf16[256,384]{1,0:T(8,128)(2,1)S(1)}, u32[]{:S(2)}, u32[]{:S(2)}) collective-permute-start(bf16[256,384]{1,0:T(8,128)(2,1)} %param.7), channel_id=1, source_target_pairs={{0,2},{1,3},{2,0},{3,1},{4,6},{5,7},{6,4},{7,5},{8,10},{9,11},{10,... | collective-permute-start | bytes 589832 | tf_op jit(solution)/shard_map/ppermute | solution.py:53
  5.3 1.0 constant_dynamic-update-slice_fusion.3
  6.3 0.3 collective-permute-done
  6.6 5.7 %collective-permute-done.1 = bf16[256,384]{1,0:T(8,128)(2,1)S(1)} collective-permute-done((bf16[256,384]{1,0:T(8,128)(2,1)}, bf16[256,384]{1,0:T(8,128)(2,1)S(1)}, u32[]{:S(2)}, u32[]{:S(2)}) %collective-permute-start.1) | collective-permute-done | bytes 196640 | tf_op jit(solution)/shard_map/ppermute | solution.py:53
  12.4 4.1 %collective-permute-start.5 = (bf16[256,1536]{1,0:T(8,128)(2,1)S(1)}, bf16[256,1536]{1,0:T(8,128)(2,1)}, u32[]{:S(2)}, u32[]{:S(2)}) collective-permute-start(bf16[256,1536]{1,0:T(8,128)(2,1)S(1)} %constant_dynamic-update-slice_fusion.x_ref), channel_id=1, source_target_pairs={{0,12},{1,13},{2,14},{3,15},{4,0},{5,1},{6,2},{7,3},{8,4},{9,5},{1... | collective-permute-start | bytes 2359304 | tf_op jit(solution)/shard_map/ppermute | solution.py:53
  16.5 1.9 %collective-permute-start.3 = (bf16[256,1536]{1,0:T(8,128)(2,1)S(1)}, bf16[256,1536]{1,0:T(8,128)(2,1)}, u32[]{:S(2)}, u32[]{:S(2)}) collective-permute-start(bf16[256,1536]{1,0:T(8,128)(2,1)S(1)} %constant_dynamic-update-slice_fusion.x_ref), channel_id=1, source_target_pairs={{0,8},{1,9},{2,10},{3,11},{4,12},{5,13},{6,14},{7,15},{8,0},{9,1},... | collective-permute-start | bytes 2359304 | tf_op jit(solution)/shard_map/ppermute | solution.py:53
  18.4 0.7 fusion.1
  19.0 0.1 add_select_fusion
  19.1 0.1 select_n.58.ids_ref
  19.2 0.7 copy-done.14
  19.9 1.3 %decay.1 = (f32[4,256,256]{2,1,0:T(8,128)S(1)}, f32[256,512]{1,0:T(8,128)S(1)}, f32[256,512]{1,0:T(8,128)S(1)}) custom-call(f32[4,256]{1,0:T(4,128)S(1)} %copy-done.14), custom_call_target="tpu_custom_call" | custom-call | flops 2000000 | bytes 2000000 | tf_op jit(solution)/shard_map/decay/pallas_call | solution.py:102
  21.2 0.0 copy-start
  21.2 2.8 %copy-done = bf16[6144,512]{1,0:T(8,128)(2,1)S(1)} copy-done((bf16[6144,512]{1,0:T(8,128)(2,1)S(1)}, bf16[6144,512]{1,0:T(8,128)(2,1)}, u32[]{:S(2)}) %copy-start) | copy-done | bytes 6291480
  24.0 2.8 %copy-done.3 = bf16[6144,512]{1,0:T(8,128)(2,1)S(1)} copy-done((bf16[6144,512]{1,0:T(8,128)(2,1)S(1)}, bf16[6144,512]{1,0:T(8,128)(2,1)}, u32[]{:S(2)}) %copy-start.3) | copy-done | bytes 6291480
  26.7 2.8 %copy-done.6 = bf16[6144,512]{1,0:T(8,128)(2,1)S(1)} copy-done((bf16[6144,512]{1,0:T(8,128)(2,1)S(1)}, bf16[6144,512]{1,0:T(8,128)(2,1)}, u32[]{:S(2)}) %copy-start.6) | copy-done | bytes 6291480
  29.5 1.9 %project.4 = (f32[256,512]{1,0:T(8,128)S(1)}, f32[256,512]{1,0:T(8,128)S(1)}, f32[256,512]{1,0:T(8,128)S(1)}) custom-call(s32[16]{0:T(128)S(1)} %select_n.58.ids_ref, bf16[256,1536]{1,0:T(8,128)(2,1)S(1)} %constant_dynamic-update-slice_fusion.x_ref, bf16[6144,512]{1,0:T(8,128)(2,1)S(1)} %copy-done, bf16[6144,512]{1,0:T(8,128)(2,1)S(1)} %copy-done.3, ...), custom_call_target="tpu_custom_call" | custom-call | flops 1207959552 | bytes 6000000 | tf_op jit(solution)/shard_map/project/pallas_call | solution.py:132
  31.5 3.0 %collective-permute-done.5.x_ref = bf16[256,1536]{1,0:T(8,128)(2,1)} collective-permute-done((bf16[256,1536]{1,0:T(8,128)(2,1)S(1)}, bf16[256,1536]{1,0:T(8,128)(2,1)}, u32[]{:S(2)}, u32[]{:S(2)}) %collective-permute-start.5) | collective-permute-done | bytes 786464 | tf_op jit(solution)/shard_map/ppermute | solution.py:53
  34.4 1.5 %copy-done.7 = bf16[6144,512]{1,0:T(8,128)(2,1)S(1)} copy-done((bf16[6144,512]{1,0:T(8,128)(2,1)S(1)}, bf16[6144,512]{1,0:T(8,128)(2,1)}, u32[]{:S(2)}) %copy-start.7) | copy-done | bytes 6291480
  35.9 2.6 %project.5 = (f32[256,512]{1,0:T(8,128)S(1)}, f32[256,512]{1,0:T(8,128)S(1)}, f32[256,512]{1,0:T(8,128)S(1)}) custom-call(s32[16]{0:T(128)S(1)} %select_n.58.ids_ref, bf16[256,1536]{1,0:T(8,128)(2,1)} %collective-permute-done.5.x_ref, f32[256,512]{1,0:T(8,128)S(1)} %get-tuple-element.45.refs_0_, f32[256,512]{1,0:T(8,128)S(1)} %get-tuple-element.46.refs_1_, ...), custom_call_target="tpu_custom_call" | custom-call | flops 1207959552 | bytes 6000000 | tf_op jit(solution)/shard_map/project/pallas_call | solution.py:132
  38.5 2.6 %project.6 = (f32[256,512]{1,0:T(8,128)S(1)}, f32[256,512]{1,0:T(8,128)S(1)}, f32[256,512]{1,0:T(8,128)S(1)}) custom-call(s32[16]{0:T(128)S(1)} %select_n.58.ids_ref, bf16[256,1536]{1,0:T(8,128)(2,1)} %collective-permute-done.4.x_ref, f32[256,512]{1,0:T(8,128)S(1)} %get-tuple-element.48.refs_0_, f32[256,512]{1,0:T(8,128)S(1)} %get-tuple-element.49.refs_1_, ...), custom_call_target="tpu_custom_call" | custom-call | flops 1207959552 | bytes 6000000 | tf_op jit(solution)/shard_map/project/pallas_call | solution.py:132
  41.1 0.0 copy-start.9
  41.1 2.6 %project.7 = (bf16[256,512]{1,0:T(8,128)(2,1)S(1)}, bf16[256,512]{1,0:T(8,128)(2,1)S(1)}, bf16[256,512]{1,0:T(8,128)(2,1)S(1)}) custom-call(s32[16]{0:T(128)S(1)} %select_n.58.ids_ref, bf16[256,1536]{1,0:T(8,128)(2,1)} %collective-permute-done.3.x_ref, f32[256,512]{1,0:T(8,128)S(1)} %get-tuple-element.51.refs_0_, f32[256,512]{1,0:T(8,128)S(1)} %get-tuple-element.52.refs_1_, ...), custom_call_target="tpu_custom_call" | custom-call | flops 1207959552 | bytes 6000000 | tf_op jit(solution)/shard_map/project/pallas_call | solution.py:132
  43.7 1.1 %states.1 = (f32[512,128]{1,0:T(8,128)S(1)}, f32[512,128]{1,0:T(8,128)S(1)}, bf16[1088,128]{1,0:T(8,128)(2,1)}) custom-call(bf16[256,512]{1,0:T(8,128)(2,1)S(1)} %get-tuple-element.54.q_ref, bf16[256,512]{1,0:T(8,128)(2,1)S(1)} %get-tuple-element.55.k_ref, bf16[256,512]{1,0:T(8,128)(2,1)S(1)} %get-tuple-element.56.v_ref, bf16[256,512]{1,0:T(8,128)(2,1)S(1)} %copy-done.9, ...), custom_call_target="tpu_custom_call" | custom-call | flops 70000000 | bytes 3000000 | tf_op jit(solution)/shard_map/states/pallas_call | solution.py:165
  44.8 0.7 copy-done.10
  45.5 0.7 copy-done.12
  46.2 0.1 pad_add_fusion.place_ref
  46.3 1.7 %collective-permute-done.6.peer_ref = bf16[1088,128]{1,0:T(8,128)(2,1)S(1)} collective-permute-done((bf16[1088,128]{1,0:T(8,128)(2,1)}, bf16[1088,128]{1,0:T(8,128)(2,1)S(1)}, u32[]{:S(2)}, u32[]{:S(2)}) %collective-permute-start.6) | collective-permute-done | bytes 278560 | tf_op jit(solution)/shard_map/ppermute | solution.py:53
  48.0 0.9 copy-done.11
  48.9 0.9 copy-done.13
  49.9 0.7 chip_states.1
  50.6 1.6 %collective-permute-start.7 = (bf16[576,128]{1,0:T(8,128)(2,1)S(1)}, bf16[576,128]{1,0:T(8,128)(2,1)S(1)}, u32[]{:S(2)}, u32[]{:S(2)}) collective-permute-start(bf16[576,128]{1,0:T(8,128)(2,1)S(1)} %get-tuple-element.62), channel_id=1, source_target_pairs={{0,32},{1,33},{2,34},{3,35},{4,36},{5,37},{6,38},{7,39},{8,40},{9,... | collective-permute-start | bytes 442376 | tf_op jit(solution)/shard_map/ppermute | solution.py:53
  52.1 2.7 %collective-permute-start.8 = (bf16[576,128]{1,0:T(8,128)(2,1)S(1)}, bf16[576,128]{1,0:T(8,128)(2,1)S(1)}, u32[]{:S(2)}, u32[]{:S(2)}) collective-permute-start(bf16[576,128]{1,0:T(8,128)(2,1)S(1)} %get-tuple-element.63), channel_id=1, source_target_pairs={{0,64},{1,65},{2,66},{3,67},{4,68},{5,69},{6,70},{7,71},{8,72},{9,... | collective-permute-start | bytes 442376 | tf_op jit(solution)/shard_map/ppermute | solution.py:53
  54.9 1.4 %collective-permute-start.9 = (bf16[576,128]{1,0:T(8,128)(2,1)S(1)}, bf16[576,128]{1,0:T(8,128)(2,1)S(1)}, u32[]{:S(2)}, u32[]{:S(2)}) collective-permute-start(bf16[576,128]{1,0:T(8,128)(2,1)S(1)} %get-tuple-element.64), channel_id=1, source_target_pairs={{0,96},{1,97},{2,98},{3,99},{4,100},{5,101},{6,102},{7,103},{8,104... | collective-permute-start | bytes 442376 | tf_op jit(solution)/shard_map/ppermute | solution.py:53
  56.3 1.5 %intra.1 = (f32[256,512]{1,0:T(8,128)S(1)}, f32[256,512]{1,0:T(8,128)S(1)}, f32[256,512]{1,0:T(8,128)S(1)}) custom-call(bf16[256,512]{1,0:T(8,128)(2,1)S(1)} %get-tuple-element.54.q_ref, bf16[256,512]{1,0:T(8,128)(2,1)S(1)} %get-tuple-element.55.k_ref, bf16[256,512]{1,0:T(8,128)(2,1)S(1)} %get-tuple-element.56.v_ref, bf16[256,512]{1,0:T(8,128)(2,1)S(1)} %copy-done.9, ...), custom_call_target="tpu_custom_call" | custom-call | flops 340000000 | bytes 4000000 | tf_op jit(solution)/shard_map/intra/pallas_call | solution.py:190
  57.8 4.1 %collective-permute-done.8.two_ref = bf16[576,128]{1,0:T(8,128)(2,1)S(1)} collective-permute-done((bf16[576,128]{1,0:T(8,128)(2,1)S(1)}, bf16[576,128]{1,0:T(8,128)(2,1)S(1)}, u32[]{:S(2)}, u32[]{:S(2)}) %collective-permute-start.8) | collective-permute-done | bytes 147488 | tf_op jit(solution)/shard_map/ppermute | solution.py:53
  61.9 1.1 %inter.1.d_ref = bf16[256,1536]{1,0:T(8,128)(2,1)S(1)} custom-call(s32[2]{0:T(128)S(1)} %pad_add_fusion.place_ref, s32[16]{0:T(128)S(1)} %select_n.58.ids_ref, bf16[256,512]{1,0:T(8,128)(2,1)S(1)} %get-tuple-element.54.q_ref, bf16[256,512]{1,0:T(8,128)(2,1)S(1)} %get-tuple-element.55.k_ref, bf16[256,512]{1,0:T(8,128)(2,1)S(1)} %get-tuple-element.56.v_ref, ...), custom_call_target="tpu_custom_call" | custom-call | flops 150000000 | bytes 6000000 | tf_op jit(solution)/shard_map/inter/pallas_call | solution.py:283
  63.0 0.0 copy-start.2
  63.0 2.8 %copy-done.2 = bf16[6144,512]{1,0:T(8,128)(2,1)S(1)} copy-done((bf16[6144,512]{1,0:T(8,128)(2,1)S(1)}, bf16[6144,512]{1,0:T(8,128)(2,1)}, u32[]{:S(2)}) %copy-start.2) | copy-done | bytes 6291480
  65.8 2.8 %copy-done.5 = bf16[6144,512]{1,0:T(8,128)(2,1)S(1)} copy-done((bf16[6144,512]{1,0:T(8,128)(2,1)S(1)}, bf16[6144,512]{1,0:T(8,128)(2,1)}, u32[]{:S(2)}) %copy-start.5) | copy-done | bytes 6291480
  68.6 2.8 %copy-done.8 = bf16[6144,512]{1,0:T(8,128)(2,1)S(1)} copy-done((bf16[6144,512]{1,0:T(8,128)(2,1)S(1)}, bf16[6144,512]{1,0:T(8,128)(2,1)}, u32[]{:S(2)}) %copy-start.8) | copy-done | bytes 6291480
  71.4 2.6 %output.2 = (f32[64,3072]{1,0:T(8,128)S(1)}, bf16[64,3072]{1,0:T(8,128)(2,1)S(1)}, bf16[64,3072]{1,0:T(8,128)(2,1)S(1)}, bf16[64,3072]{1,0:T(8,128)(2,1)S(1)}) custom-call(bf16[256,1536]{1,0:T(8,128)(2,1)S(1)} %inter.1.d_ref, bf16[6144,512]{1,0:T(8,128)(2,1)S(1)} %copy-done.2, bf16[6144,512]{1,0:T(8,128)(2,1)S(1)} %copy-done.5, bf16[6144,512]{1,0:T(8,128)(2,1)S(1)} %copy-done.8), custom_call_target="tpu_custom_call" | custom-call | flops 2415919104 | bytes 6000000 | tf_op jit(solution)/shard_map/output/pallas_call | solution.py:316
  74.0 2.3 %collective-permute-start.10 = (bf16[64,3072]{1,0:T(8,128)(2,1)S(1)}, bf16[64,3072]{1,0:T(8,128)(2,1)S(1)}, u32[]{:S(2)}, u32[]{:S(2)}) collective-permute-start(bf16[64,3072]{1,0:T(8,128)(2,1)S(1)} %get-tuple-element.70), channel_id=1, source_target_pairs={{0,4},{1,5},{2,6},{3,7},{4,8},{5,9},{6,10},{7,11},{8,12},{9,13},{1... | collective-permute-start | bytes 1179656 | tf_op jit(solution)/shard_map/ppermute | solution.py:53
  76.3 1.0 collective-permute-start.11
  77.3 1.1 %collective-permute-start.12 = (bf16[64,3072]{1,0:T(8,128)(2,1)S(1)}, bf16[64,3072]{1,0:T(8,128)(2,1)S(1)}, u32[]{:S(2)}, u32[]{:S(2)}) collective-permute-start(bf16[64,3072]{1,0:T(8,128)(2,1)S(1)} %get-tuple-element.72), channel_id=1, source_target_pairs={{0,8},{1,9},{2,10},{3,11},{4,12},{5,13},{6,14},{7,15},{8,0},{9,1},... | collective-permute-start | bytes 1179656 | tf_op jit(solution)/shard_map/ppermute | solution.py:53
  78.5 2.6 %output.3 = (f32[64,3072]{1,0:T(8,128)S(1)}, bf16[64,3072]{1,0:T(8,128)(2,1)S(1)}, bf16[64,3072]{1,0:T(8,128)(2,1)S(1)}, bf16[64,3072]{1,0:T(8,128)(2,1)S(1)}) custom-call(bf16[256,1536]{1,0:T(8,128)(2,1)S(1)} %inter.1.d_ref, bf16[6144,512]{1,0:T(8,128)(2,1)S(1)} %copy-done.2, bf16[6144,512]{1,0:T(8,128)(2,1)S(1)} %copy-done.5, bf16[6144,512]{1,0:T(8,128)(2,1)S(1)} %copy-done.8), custom_call_target="tpu_custom_call" | custom-call | flops 2415919104 | bytes 6000000 | tf_op jit(solution)/shard_map/output/pallas_call | solution.py:316
  81.1 0.9 collective-permute-start.16
  82.0 2.4 %collective-permute-start.17 = (bf16[64,3072]{1,0:T(8,128)(2,1)S(1)}, bf16[64,3072]{1,0:T(8,128)(2,1)S(1)}, u32[]{:S(2)}, u32[]{:S(2)}) collective-permute-start(bf16[64,3072]{1,0:T(8,128)(2,1)S(1)} %get-tuple-element.79), channel_id=1, source_target_pairs={{0,12},{1,13},{2,14},{3,15},{4,0},{5,1},{6,2},{7,3},{8,4},{9,5},{1... | collective-permute-start | bytes 1179656 | tf_op jit(solution)/shard_map/ppermute | solution.py:53
  84.4 1.2 %collective-permute-start.18 = (bf16[64,3072]{1,0:T(8,128)(2,1)S(1)}, bf16[64,3072]{1,0:T(8,128)(2,1)S(1)}, u32[]{:S(2)}, u32[]{:S(2)}) collective-permute-start(bf16[64,3072]{1,0:T(8,128)(2,1)S(1)} %get-tuple-element.80), channel_id=1, source_target_pairs={{0,8},{1,9},{2,10},{3,11},{4,12},{5,13},{6,14},{7,15},{8,0},{9,1},... | collective-permute-start | bytes 1179656 | tf_op jit(solution)/shard_map/ppermute | solution.py:53
  85.6 2.3 %collective-permute-done.12.c_ref = bf16[64,3072]{1,0:T(8,128)(2,1)S(1)} collective-permute-done((bf16[64,3072]{1,0:T(8,128)(2,1)S(1)}, bf16[64,3072]{1,0:T(8,128)(2,1)S(1)}, u32[]{:S(2)}, u32[]{:S(2)}) %collective-permute-start.12) | collective-permute-done | bytes 393248 | tf_op jit(solution)/shard_map/ppermute | solution.py:53
  87.9 0.2 add.129
  88.1 0.1 collective-permute-start.13
  88.2 3.2 %collective-permute-start.14 = (bf16[16,3072]{1,0:T(8,128)(2,1)S(1)}, bf16[16,3072]{1,0:T(8,128)(2,1)S(1)}, u32[]{:S(2)}, u32[]{:S(2)}) collective-permute-start(bf16[16,3072]{1,0:T(8,128)(2,1)S(1)} %get-tuple-element.75), channel_id=1, source_target_pairs={{0,3},{1,0},{2,1},{3,2},{4,7},{5,4},{6,5},{7,6},{8,11},{9,8},{10,9... | collective-permute-start | bytes 294920 | tf_op jit(solution)/shard_map/ppermute | solution.py:53
  91.4 1.7 %collective-permute-done.16.a_ref = bf16[64,3072]{1,0:T(8,128)(2,1)S(1)} collective-permute-done((bf16[64,3072]{1,0:T(8,128)(2,1)S(1)}, bf16[64,3072]{1,0:T(8,128)(2,1)S(1)}, u32[]{:S(2)}, u32[]{:S(2)}) %collective-permute-start.16) | collective-permute-done | bytes 393248 | tf_op jit(solution)/shard_map/ppermute | solution.py:53
  93.1 0.5 collective-permute-done.17.b_ref
  93.6 4.8 %collective-permute-done.18.c_ref = bf16[64,3072]{1,0:T(8,128)(2,1)S(1)} collective-permute-done((bf16[64,3072]{1,0:T(8,128)(2,1)S(1)}, bf16[64,3072]{1,0:T(8,128)(2,1)S(1)}, u32[]{:S(2)}, u32[]{:S(2)}) %collective-permute-start.18) | collective-permute-done | bytes 393248 | tf_op jit(solution)/shard_map/ppermute | solution.py:53
  98.4 0.2 add.131
  98.6 0.1 collective-permute-start.19
  98.7 3.2 %collective-permute-start.20 = (bf16[16,3072]{1,0:T(8,128)(2,1)S(1)}, bf16[16,3072]{1,0:T(8,128)(2,1)S(1)}, u32[]{:S(2)}, u32[]{:S(2)}) collective-permute-start(bf16[16,3072]{1,0:T(8,128)(2,1)S(1)} %get-tuple-element.83), channel_id=1, source_target_pairs={{0,3},{1,0},{2,1},{3,2},{4,7},{5,4},{6,5},{7,6},{8,11},{9,8},{10,9... | collective-permute-start | bytes 294920 | tf_op jit(solution)/shard_map/ppermute | solution.py:53
  102.0 2.5 %collective-permute-done.19.a_ref = bf16[16,3072]{1,0:T(8,128)(2,1)S(1)} collective-permute-done((bf16[16,3072]{1,0:T(8,128)(2,1)S(1)}, bf16[16,3072]{1,0:T(8,128)(2,1)S(1)}, u32[]{:S(2)}, u32[]{:S(2)}) %collective-permute-start.19) | collective-permute-done | bytes 98336 | tf_op jit(solution)/shard_map/ppermute | solution.py:53
  104.5 0.6 collective-permute-done.20.b_ref
  105.1 2.9 %collective-permute-done.21.c_ref = bf16[16,3072]{1,0:T(8,128)(2,1)S(1)} collective-permute-done((bf16[16,3072]{1,0:T(8,128)(2,1)S(1)}, bf16[16,3072]{1,0:T(8,128)(2,1)S(1)}, u32[]{:S(2)}, u32[]{:S(2)}) %collective-permute-start.21) | collective-permute-done | bytes 98336 | tf_op jit(solution)/shard_map/ppermute | solution.py:53
  108.1 0.7 pad_maximum_fusion
  (34 shorter events, 0.3 us)
Async XLA Ops:
  0.0 6.6 %collective-permute-start = (bf16[256,384]{1,0:T(8,128)(2,1)}, bf16[256,384]{1,0:T(8,128)(2,1)S(1)}, u32[]{:S(2)}, u32[]{:S(2)}) collective-permute-start(bf16[256,384]{1,0:T(8,128)(2,1)} %param.7), channel_id=1, source_target_pairs={{0,3},{1,0},{2,1},{3,2},{4,7},{5,4},{6,5},{7,6},{8,11},{9,8},{10,9... | collective-permute-start | bytes 589832 | tf_op jit(solution)/shard_map/ppermute | solution.py:53
  3.1 9.2 %collective-permute-start.1 = (bf16[256,384]{1,0:T(8,128)(2,1)}, bf16[256,384]{1,0:T(8,128)(2,1)S(1)}, u32[]{:S(2)}, u32[]{:S(2)}) collective-permute-start(bf16[256,384]{1,0:T(8,128)(2,1)} %param.7), channel_id=1, source_target_pairs={{0,1},{1,2},{2,3},{3,0},{4,5},{5,6},{6,7},{7,4},{8,9},{9,10},{10,1... | collective-permute-start | bytes 589832 | tf_op jit(solution)/shard_map/ppermute | solution.py:53
  3.1 9.2 %collective-permute-start.2 = (bf16[256,384]{1,0:T(8,128)(2,1)}, bf16[256,384]{1,0:T(8,128)(2,1)S(1)}, u32[]{:S(2)}, u32[]{:S(2)}) collective-permute-start(bf16[256,384]{1,0:T(8,128)(2,1)} %param.7), channel_id=1, source_target_pairs={{0,2},{1,3},{2,0},{3,1},{4,6},{5,7},{6,4},{7,5},{8,10},{9,11},{10,... | collective-permute-start | bytes 589832 | tf_op jit(solution)/shard_map/ppermute | solution.py:53
  12.4 22.0 %collective-permute-start.5 = (bf16[256,1536]{1,0:T(8,128)(2,1)S(1)}, bf16[256,1536]{1,0:T(8,128)(2,1)}, u32[]{:S(2)}, u32[]{:S(2)}) collective-permute-start(bf16[256,1536]{1,0:T(8,128)(2,1)S(1)} %constant_dynamic-update-slice_fusion.x_ref), channel_id=1, source_target_pairs={{0,12},{1,13},{2,14},{3,15},{4,0},{5,1},{6,2},{7,3},{8,4},{9,5},{1... | collective-permute-start | bytes 2359304 | tf_op jit(solution)/shard_map/ppermute | solution.py:53
  16.5 22.0 %collective-permute-start.4 = (bf16[256,1536]{1,0:T(8,128)(2,1)S(1)}, bf16[256,1536]{1,0:T(8,128)(2,1)}, u32[]{:S(2)}, u32[]{:S(2)}) collective-permute-start(bf16[256,1536]{1,0:T(8,128)(2,1)S(1)} %constant_dynamic-update-slice_fusion.x_ref), channel_id=1, source_target_pairs={{0,4},{1,5},{2,6},{3,7},{4,8},{5,9},{6,10},{7,11},{8,12},{9,13},{1... | collective-permute-start | bytes 2359304 | tf_op jit(solution)/shard_map/ppermute | solution.py:53
  16.5 24.6 %collective-permute-start.3 = (bf16[256,1536]{1,0:T(8,128)(2,1)S(1)}, bf16[256,1536]{1,0:T(8,128)(2,1)}, u32[]{:S(2)}, u32[]{:S(2)}) collective-permute-start(bf16[256,1536]{1,0:T(8,128)(2,1)S(1)} %constant_dynamic-update-slice_fusion.x_ref), channel_id=1, source_target_pairs={{0,8},{1,9},{2,10},{3,11},{4,12},{5,13},{6,14},{7,15},{8,0},{9,1},... | collective-permute-start | bytes 2359304 | tf_op jit(solution)/shard_map/ppermute | solution.py:53
  19.2 0.7 copy-start.14
  21.2 2.8 %copy-start = (bf16[6144,512]{1,0:T(8,128)(2,1)S(1)}, bf16[6144,512]{1,0:T(8,128)(2,1)}, u32[]{:S(2)}) copy-start(bf16[6144,512]{1,0:T(8,128)(2,1)} %wq_ref.3) | copy-start | bytes 18874372
  24.0 2.8 %copy-start.3 = (bf16[6144,512]{1,0:T(8,128)(2,1)S(1)}, bf16[6144,512]{1,0:T(8,128)(2,1)}, u32[]{:S(2)}) copy-start(bf16[6144,512]{1,0:T(8,128)(2,1)} %wk_ref.3) | copy-start | bytes 18874372
  26.7 2.8 %copy-start.6 = (bf16[6144,512]{1,0:T(8,128)(2,1)S(1)}, bf16[6144,512]{1,0:T(8,128)(2,1)}, u32[]{:S(2)}) copy-start(bf16[6144,512]{1,0:T(8,128)(2,1)} %wv_ref.3) | copy-start | bytes 18874372
  29.5 4.9 %copy-start.1 = (bf16[6144,512]{1,0:T(8,128)(2,1)S(1)}, bf16[6144,512]{1,0:T(8,128)(2,1)}, u32[]{:S(2)}) copy-start(bf16[6144,512]{1,0:T(8,128)(2,1)} %wq_ref.3) | copy-start | bytes 18874372
  29.5 4.9 %copy-start.4 = (bf16[6144,512]{1,0:T(8,128)(2,1)S(1)}, bf16[6144,512]{1,0:T(8,128)(2,1)}, u32[]{:S(2)}) copy-start(bf16[6144,512]{1,0:T(8,128)(2,1)} %wk_ref.3) | copy-start | bytes 18874372
  29.5 6.4 %copy-start.7 = (bf16[6144,512]{1,0:T(8,128)(2,1)S(1)}, bf16[6144,512]{1,0:T(8,128)(2,1)}, u32[]{:S(2)}) copy-start(bf16[6144,512]{1,0:T(8,128)(2,1)} %wv_ref.3) | copy-start | bytes 18874372
  41.1 2.6 %copy-start.9 = (bf16[256,512]{1,0:T(8,128)(2,1)S(1)}, bf16[256,512]{1,0:T(8,128)(2,1)}, u32[]{:S(2)}) copy-start(bf16[256,512]{1,0:T(8,128)(2,1)} %g_ref.5) | copy-start | bytes 786436
  44.8 0.7 copy-start.10
  45.5 0.7 copy-start.12
  46.2 1.8 %collective-permute-start.6 = (bf16[1088,128]{1,0:T(8,128)(2,1)}, bf16[1088,128]{1,0:T(8,128)(2,1)S(1)}, u32[]{:S(2)}, u32[]{:S(2)}) collective-permute-start(bf16[1088,128]{1,0:T(8,128)(2,1)} %get-tuple-element.59), channel_id=1, source_target_pairs={{0,16},{1,17},{2,18},{3,19},{4,20},{5,21},{6,22},{7,23},{8,24},{9,... | collective-permute-start | bytes 835592 | tf_op jit(solution)/shard_map/ppermute | solution.py:53
  48.0 1.0 copy-start.11
  48.9 0.9 copy-start.13
  50.6 7.2 %collective-permute-start.7 = (bf16[576,128]{1,0:T(8,128)(2,1)S(1)}, bf16[576,128]{1,0:T(8,128)(2,1)S(1)}, u32[]{:S(2)}, u32[]{:S(2)}) collective-permute-start(bf16[576,128]{1,0:T(8,128)(2,1)S(1)} %get-tuple-element.62), channel_id=1, source_target_pairs={{0,32},{1,33},{2,34},{3,35},{4,36},{5,37},{6,38},{7,39},{8,40},{9,... | collective-permute-start | bytes 442376 | tf_op jit(solution)/shard_map/ppermute | solution.py:53
  52.1 9.8 %collective-permute-start.8 = (bf16[576,128]{1,0:T(8,128)(2,1)S(1)}, bf16[576,128]{1,0:T(8,128)(2,1)S(1)}, u32[]{:S(2)}, u32[]{:S(2)}) collective-permute-start(bf16[576,128]{1,0:T(8,128)(2,1)S(1)} %get-tuple-element.63), channel_id=1, source_target_pairs={{0,64},{1,65},{2,66},{3,67},{4,68},{5,69},{6,70},{7,71},{8,72},{9,... | collective-permute-start | bytes 442376 | tf_op jit(solution)/shard_map/ppermute | solution.py:53
  54.9 7.0 %collective-permute-start.9 = (bf16[576,128]{1,0:T(8,128)(2,1)S(1)}, bf16[576,128]{1,0:T(8,128)(2,1)S(1)}, u32[]{:S(2)}, u32[]{:S(2)}) collective-permute-start(bf16[576,128]{1,0:T(8,128)(2,1)S(1)} %get-tuple-element.64), channel_id=1, source_target_pairs={{0,96},{1,97},{2,98},{3,99},{4,100},{5,101},{6,102},{7,103},{8,104... | collective-permute-start | bytes 442376 | tf_op jit(solution)/shard_map/ppermute | solution.py:53
  63.0 2.8 %copy-start.2 = (bf16[6144,512]{1,0:T(8,128)(2,1)S(1)}, bf16[6144,512]{1,0:T(8,128)(2,1)}, u32[]{:S(2)}) copy-start(bf16[6144,512]{1,0:T(8,128)(2,1)} %wq_ref.3) | copy-start | bytes 18874372
  65.8 2.8 %copy-start.5 = (bf16[6144,512]{1,0:T(8,128)(2,1)S(1)}, bf16[6144,512]{1,0:T(8,128)(2,1)}, u32[]{:S(2)}) copy-start(bf16[6144,512]{1,0:T(8,128)(2,1)} %wk_ref.3) | copy-start | bytes 18874372
  68.6 2.8 %copy-start.8 = (bf16[6144,512]{1,0:T(8,128)(2,1)S(1)}, bf16[6144,512]{1,0:T(8,128)(2,1)}, u32[]{:S(2)}) copy-start(bf16[6144,512]{1,0:T(8,128)(2,1)} %wv_ref.3) | copy-start | bytes 18874372
  74.0 10.4 %collective-permute-start.10 = (bf16[64,3072]{1,0:T(8,128)(2,1)S(1)}, bf16[64,3072]{1,0:T(8,128)(2,1)S(1)}, u32[]{:S(2)}, u32[]{:S(2)}) collective-permute-start(bf16[64,3072]{1,0:T(8,128)(2,1)S(1)} %get-tuple-element.70), channel_id=1, source_target_pairs={{0,4},{1,5},{2,6},{3,7},{4,8},{5,9},{6,10},{7,11},{8,12},{9,13},{1... | collective-permute-start | bytes 1179656 | tf_op jit(solution)/shard_map/ppermute | solution.py:53
  76.3 9.3 %collective-permute-start.11 = (bf16[64,3072]{1,0:T(8,128)(2,1)S(1)}, bf16[64,3072]{1,0:T(8,128)(2,1)S(1)}, u32[]{:S(2)}, u32[]{:S(2)}) collective-permute-start(bf16[64,3072]{1,0:T(8,128)(2,1)S(1)} %get-tuple-element.71), channel_id=1, source_target_pairs={{0,12},{1,13},{2,14},{3,15},{4,0},{5,1},{6,2},{7,3},{8,4},{9,5},{1... | collective-permute-start | bytes 1179656 | tf_op jit(solution)/shard_map/ppermute | solution.py:53
  77.3 10.6 %collective-permute-start.12 = (bf16[64,3072]{1,0:T(8,128)(2,1)S(1)}, bf16[64,3072]{1,0:T(8,128)(2,1)S(1)}, u32[]{:S(2)}, u32[]{:S(2)}) collective-permute-start(bf16[64,3072]{1,0:T(8,128)(2,1)S(1)} %get-tuple-element.72), channel_id=1, source_target_pairs={{0,8},{1,9},{2,10},{3,11},{4,12},{5,13},{6,14},{7,15},{8,0},{9,1},... | collective-permute-start | bytes 1179656 | tf_op jit(solution)/shard_map/ppermute | solution.py:53
  81.1 12.0 %collective-permute-start.16 = (bf16[64,3072]{1,0:T(8,128)(2,1)S(1)}, bf16[64,3072]{1,0:T(8,128)(2,1)S(1)}, u32[]{:S(2)}, u32[]{:S(2)}) collective-permute-start(bf16[64,3072]{1,0:T(8,128)(2,1)S(1)} %get-tuple-element.78), channel_id=1, source_target_pairs={{0,4},{1,5},{2,6},{3,7},{4,8},{5,9},{6,10},{7,11},{8,12},{9,13},{1... | collective-permute-start | bytes 1179656 | tf_op jit(solution)/shard_map/ppermute | solution.py:53
  82.0 11.6 %collective-permute-start.17 = (bf16[64,3072]{1,0:T(8,128)(2,1)S(1)}, bf16[64,3072]{1,0:T(8,128)(2,1)S(1)}, u32[]{:S(2)}, u32[]{:S(2)}) collective-permute-start(bf16[64,3072]{1,0:T(8,128)(2,1)S(1)} %get-tuple-element.79), channel_id=1, source_target_pairs={{0,12},{1,13},{2,14},{3,15},{4,0},{5,1},{6,2},{7,3},{8,4},{9,5},{1... | collective-permute-start | bytes 1179656 | tf_op jit(solution)/shard_map/ppermute | solution.py:53
  84.4 14.0 %collective-permute-start.18 = (bf16[64,3072]{1,0:T(8,128)(2,1)S(1)}, bf16[64,3072]{1,0:T(8,128)(2,1)S(1)}, u32[]{:S(2)}, u32[]{:S(2)}) collective-permute-start(bf16[64,3072]{1,0:T(8,128)(2,1)S(1)} %get-tuple-element.80), channel_id=1, source_target_pairs={{0,8},{1,9},{2,10},{3,11},{4,12},{5,13},{6,14},{7,15},{8,0},{9,1},... | collective-permute-start | bytes 1179656 | tf_op jit(solution)/shard_map/ppermute | solution.py:53
  88.1 13.8 %collective-permute-start.13 = (bf16[16,3072]{1,0:T(8,128)(2,1)S(1)}, bf16[16,3072]{1,0:T(8,128)(2,1)S(1)}, u32[]{:S(2)}, u32[]{:S(2)}) collective-permute-start(bf16[16,3072]{1,0:T(8,128)(2,1)S(1)} %get-tuple-element.74), channel_id=1, source_target_pairs={{0,1},{1,2},{2,3},{3,0},{4,5},{5,6},{6,7},{7,4},{8,9},{9,10},{10,1... | collective-permute-start | bytes 294920 | tf_op jit(solution)/shard_map/ppermute | solution.py:53
  88.2 13.7 %collective-permute-start.14 = (bf16[16,3072]{1,0:T(8,128)(2,1)S(1)}, bf16[16,3072]{1,0:T(8,128)(2,1)S(1)}, u32[]{:S(2)}, u32[]{:S(2)}) collective-permute-start(bf16[16,3072]{1,0:T(8,128)(2,1)S(1)} %get-tuple-element.75), channel_id=1, source_target_pairs={{0,3},{1,0},{2,1},{3,2},{4,7},{5,4},{6,5},{7,6},{8,11},{9,8},{10,9... | collective-permute-start | bytes 294920 | tf_op jit(solution)/shard_map/ppermute | solution.py:53
  93.1 8.8 %collective-permute-start.15 = (bf16[16,3072]{1,0:T(8,128)(2,1)S(1)}, bf16[16,3072]{1,0:T(8,128)(2,1)S(1)}, u32[]{:S(2)}, u32[]{:S(2)}) collective-permute-start(bf16[16,3072]{1,0:T(8,128)(2,1)S(1)} %get-tuple-element.76), channel_id=1, source_target_pairs={{0,2},{1,3},{2,0},{3,1},{4,6},{5,7},{6,4},{7,5},{8,10},{9,11},{10,... | collective-permute-start | bytes 294920 | tf_op jit(solution)/shard_map/ppermute | solution.py:53
  98.6 5.9 %collective-permute-start.19 = (bf16[16,3072]{1,0:T(8,128)(2,1)S(1)}, bf16[16,3072]{1,0:T(8,128)(2,1)S(1)}, u32[]{:S(2)}, u32[]{:S(2)}) collective-permute-start(bf16[16,3072]{1,0:T(8,128)(2,1)S(1)} %get-tuple-element.82), channel_id=1, source_target_pairs={{0,1},{1,2},{2,3},{3,0},{4,5},{5,6},{6,7},{7,4},{8,9},{9,10},{10,1... | collective-permute-start | bytes 294920 | tf_op jit(solution)/shard_map/ppermute | solution.py:53
  98.7 6.4 %collective-permute-start.20 = (bf16[16,3072]{1,0:T(8,128)(2,1)S(1)}, bf16[16,3072]{1,0:T(8,128)(2,1)S(1)}, u32[]{:S(2)}, u32[]{:S(2)}) collective-permute-start(bf16[16,3072]{1,0:T(8,128)(2,1)S(1)} %get-tuple-element.83), channel_id=1, source_target_pairs={{0,3},{1,0},{2,1},{3,2},{4,7},{5,4},{6,5},{7,6},{8,11},{9,8},{10,9... | collective-permute-start | bytes 294920 | tf_op jit(solution)/shard_map/ppermute | solution.py:53
  101.9 6.1 %collective-permute-start.21 = (bf16[16,3072]{1,0:T(8,128)(2,1)S(1)}, bf16[16,3072]{1,0:T(8,128)(2,1)S(1)}, u32[]{:S(2)}, u32[]{:S(2)}) collective-permute-start(bf16[16,3072]{1,0:T(8,128)(2,1)S(1)} %get-tuple-element.84), channel_id=1, source_target_pairs={{0,2},{1,3},{2,0},{3,1},{4,6},{5,7},{6,4},{7,5},{8,10},{9,11},{10,... | collective-permute-start | bytes 294920 | tf_op jit(solution)/shard_map/ppermute | solution.py:53

commit v2 on v1

--- a/solution.py
+++ b/solution.py
@@ -15,7 +15,8 @@
 DH = 128
 MIB = 2**20
 VMEM = pl.BlockSpec(memory_space=pltpu.VMEM)
-SMEM = pl.BlockSpec(memory_space=pltpu.SMEM)
+HBM = pl.BlockSpec(memory_space=pltpu.HBM)
+HALVES = 2
 
 
 def device(x, core, z, y):
@@ -51,6 +52,19 @@
 
 def move(array, pairs):
     return lax.ppermute(array, AXES, pairs)
+
+
+def place():
+    ctx, head = lax.axis_index("ctx"), lax.axis_index("head")
+    return ctx >> 1, ctx & 1, head >> 2, head & 3
+
+
+def member(slot, inner):
+    _, core, z, y = place()
+    first = core == 0
+    z = (z + jnp.where(first, REL[slot], REL[inner])) & 3
+    y = (y + jnp.where(first, REL[inner], REL[slot])) & 3
+    return z * 4 + y
 
 
 def params(mib):
@@ -98,10 +112,10 @@
 
 def decay_factors(log_decay):
     heads, rows = log_decay.shape
-    wide = jax.ShapeDtypeStruct((rows, heads * DH), F32)
+    wide = pltpu.VMEM((rows, heads * DH), F32)
     return pl.pallas_call(
         decay_kernel,
-        out_shape=(jax.ShapeDtypeStruct((heads, rows, rows), F32), wide, wide),
+        out_shape=(pltpu.VMEM((heads, rows, rows), F32), wide, wide),
         in_specs=[VMEM],
         out_specs=(VMEM, VMEM, VMEM),
         compiler_params=params(8),
@@ -110,34 +124,90 @@
     )(log_decay)
 
 
-def project_kernel(has_sum, slot, ids_ref, x_ref, *refs):
-    sums = refs[:3] if has_sum else None
-    weights = refs[3:6] if has_sum else refs[:3]
-    outs = refs[-3:]
-    width = x_ref.shape[1] // SIDE
-    x = x_ref[...]
-    starts = [pl.multiple_of(ids_ref[slot * SIDE + j] * width, 128) for j in range(SIDE)]
+def load_kernel(*refs):
+    count = len(refs) // 2
+    sources, targets, done = refs[:count], refs[count:-1], refs[-1]
+    pieces = done.shape[0] // count
+    copies = []
+    for n, (source, target) in enumerate(zip(sources, targets)):
+        rows = source.shape[0] // pieces
+        for i in range(pieces):
+            at = pl.ds(i * rows, rows)
+            copies.append(
+                pltpu.make_async_copy(source.at[at], target.at[at], done.at[n * pieces + i])
+            )
+    for copy in copies:
+        copy.start()
+    for copy in copies:
+        copy.wait()
+
+
+def load(arrays, mib):
+    moved = sum(2 * a.size * a.dtype.itemsize for a in arrays)
+    return pl.pallas_call(
+        load_kernel,
+        out_shape=tuple(pltpu.VMEM(a.shape, a.dtype) for a in arrays),
+        in_specs=[HBM] * len(arrays),
+        out_specs=(VMEM,) * len(arrays),
+        scratch_shapes=[pltpu.SemaphoreType.DMA((4 * len(arrays),))],
+        compiler_params=params(mib),
+        cost_estimate=cost(0, moved),
+        name="load",
+    )(*arrays)
+
+
+def join_kernel(*refs):
+    pieces, outs = refs[:SIDE], refs[-HALVES:]
+    width = pieces[0].shape[1]
+    for n, ref in enumerate(pieces):
+        for m, out_ref in enumerate(outs):
+            rows = out_ref.shape[0]
+            out_ref[:, n * width : (n + 1) * width] = ref[m * rows : (m + 1) * rows, :]
+
+
+def join(pieces, after):
+    rows, width = pieces[0].shape
+    return pl.pallas_call(
+        join_kernel,
+        out_shape=(pltpu.VMEM((rows // HALVES, SIDE * width), BF16),) * HALVES,
+        in_specs=[VMEM] * (SIDE + len(after)),
+        out_specs=(VMEM,) * HALVES,
+        compiler_params=params(4),
+        cost_estimate=cost(0, 2_000_000),
+        name="join",
+    )(*pieces, *after)
+
+
+def project_kernel(slots, has_sum, *refs):
+    count = HALVES * len(slots)
+    xs, refs = refs[:count], refs[count:]
+    sums, refs = (refs[:3], refs[3:]) if has_sum else (None, refs)
+    weights, outs = refs[:3], refs[-3:]
     for n, (w_ref, out_ref) in enumerate(zip(weights, outs)):
-        w = jnp.concatenate([w_ref[pl.ds(s, width), :] for s in starts], axis=0)
-        total = nn(x, w)
-        if has_sum:
-            total = total + sums[n][...]
+        total = sums[n][...] if has_sum else None
+        for m, slot in enumerate(slots):
+            x = jnp.concatenate([r[...] for r in xs[m * HALVES : (m + 1) * HALVES]], axis=0)
+            width = x.shape[1] // SIDE
+            starts = [pl.multiple_of(member(slot, j) * width, 128) for j in range(SIDE)]
+            w = jnp.concatenate([w_ref[pl.ds(s, width), :] for s in starts], axis=0)
+            term = nn(x, w)
+            total = term if total is None else total + term
         out_ref[...] = total.astype(out_ref.dtype)
 
 
-def project(ids, x, sums, weights, slot, kind):
-    rows, columns = x.shape[0], weights[0].shape[1]
+def project(xs, slots, sums, weights, kind, after=()):
+    rows, columns = HALVES * xs[0].shape[0], weights[0].shape[1]
+    inner = xs[0].shape[1] * len(slots)
     has_sum = sums is not None
-    out = jax.ShapeDtypeStruct((rows, columns), kind)
-    return pl.pallas_call(
-        functools.partial(project_kernel, has_sum, slot),
-        out_shape=(out,) * 3,
-        in_specs=[SMEM] + [VMEM] * (4 + 3 * has_sum),
+    return pl.pallas_call(
+        functools.partial(project_kernel, slots, has_sum),
+        out_shape=(pltpu.VMEM((rows, columns), kind),) * 3,
+        in_specs=[VMEM] * (len(xs) + 3 + 3 * has_sum + len(after)),
         out_specs=(VMEM,) * 3,
         compiler_params=params(12),
-        cost_estimate=cost(2 * 3 * rows * x.shape[1] * columns, 6_000_000),
+        cost_estimate=cost(2 * 3 * rows * inner * columns, 4_000 * inner),
         name="project",
-    )(ids, x, *(sums or ()), *weights)
+    )(*xs, *(sums or ()), *weights, *after)
 
 
 def states_kernel(q_ref, k_ref, v_ref, g_ref, lead_ref, tail_ref, l_ref, m_ref, pay_ref):
@@ -160,8 +230,8 @@
 
 def states(q, k, v, g, lead, tail):
     columns = q.shape[1]
-    state = jax.ShapeDtypeStruct((columns, DH), F32)
-    pay = jax.ShapeDtypeStruct((2 * columns + columns // 8, DH), BF16)
+    state = pltpu.VMEM((columns, DH), F32)
+    pay = pltpu.VMEM((2 * columns + columns // 8, DH), BF16)
     return pl.pallas_call(
         states_kernel,
         out_shape=(state, state, pay),
@@ -186,7 +256,7 @@
 
 
 def intra(q, k, v, g, weights):
-    out = jax.ShapeDtypeStruct(q.shape, F32)
+    out = pltpu.VMEM(q.shape, F32)
     return pl.pallas_call(
         intra_kernel,
         out_shape=(out,) * 3,
@@ -198,11 +268,11 @@
     )(q, k, v, g, weights)
 
 
-def chip_kernel(place_ref, l_ref, m_ref, lead_ref, peer_ref, *pays):
+def chip_kernel(l_ref, m_ref, lead_ref, peer_ref, *pays):
     columns = l_ref.shape[0]
     rows = lead_ref.shape[0]
     heads = columns // DH
-    core, x = place_ref[0], place_ref[1]
+    x, core, _, _ = place()
     first = core == 0
     for h in range(heads):
         s = slice(h * DH, (h + 1) * DH)
@@ -219,26 +289,26 @@
             pay_ref[pl.ds(columns + h * 16, 16), :] = decay
 
 
-def chip_states(place, own_l, own_m, lead, peer):
+def chip_states(own_l, own_m, lead, peer):
     columns = own_l.shape[0]
-    pay = jax.ShapeDtypeStruct((columns + columns // 8, DH), BF16)
+    pay = pltpu.VMEM((columns + columns // 8, DH), BF16)
     return pl.pallas_call(
         chip_kernel,
         out_shape=(pay,) * 3,
-        in_specs=[SMEM] + [VMEM] * 4,
+        in_specs=[VMEM] * 4,
         out_specs=(VMEM,) * 3,
         compiler_params=params(8),
         cost_estimate=cost(1_000_000, 2_000_000),
         name="chip_states",
-    )(place, own_l, own_m, lead, peer)
+    )(own_l, own_m, lead, peer)
 
 
 def inter_kernel(
-    place_ref, ids_ref, q_ref, k_ref, v_ref, g_ref, lead_ref, tail_ref, peer_ref, one_ref, two_ref,
-    three_ref, dq_ref, dk_ref, dv_ref, out_ref, whole_ref,
+    q_ref, k_ref, v_ref, g_ref, lead_ref, tail_ref, peer_ref, one_ref, two_ref, three_ref,
+    dq_ref, dk_ref, dv_ref, out_ref, whole_ref,
 ):
     rows, columns = q_ref.shape
-    core, x = place_ref[0], place_ref[1]
+    x, core, _, _ = place()
     first = core == 0
     far = (one_ref, two_ref, three_ref)
 
@@ -273,30 +343,31 @@
         dv = dv_ref[:, c] + tail * nn(k, grad)
         for n, result in enumerate((dq, dk, dv)):
             whole_ref[:, pl.ds(n * columns + h * DH, DH)] = result.astype(BF16)
-    for n in range(16):
-        start = pl.multiple_of(ids_ref[n] * 16, 16)
+    for n in range(SIDE * SIDE):
+        start = pl.multiple_of(member(n // SIDE, n % SIDE) * 16, 16)
         out_ref[pl.ds(n * 16, 16), :] = whole_ref[pl.ds(start, 16), :]
 
 
-def inter(place, ids, q, k, v, g, lead, tail, peer, far, within):
+def inter(q, k, v, g, lead, tail, peer, far, within):
     rows, columns = q.shape
     return pl.pallas_call(
         inter_kernel,
-        out_shape=jax.ShapeDtypeStruct((rows, 3 * columns), BF16),
-        in_specs=[SMEM] * 2 + [VMEM] * 13,
+        out_shape=pltpu.VMEM((rows, 3 * columns), BF16),
+        in_specs=[VMEM] * 13,
         out_specs=VMEM,
         scratch_shapes=[pltpu.VMEM((rows, 3 * columns), BF16)],
         compiler_params=params(8),
         cost_estimate=cost(150_000_000, 6_000_000),
         name="inter",
-    )(place, ids, q, k, v, g, lead, tail, peer, *far, *within)
-
-
-def output_kernel(start, tile, d_ref, wq_ref, wk_ref, wv_ref, own_ref, *sends):
+    )(q, k, v, g, lead, tail, peer, *far, *within)
+
+
+def output_kernel(start, tile, d_ref, wq_ref, wk_ref, wv_ref, *refs):
+    outs = refs[-SIDE:]
     rows = d_ref.shape[0]
     piece = rows // SIDE
     inner = wq_ref.shape[1]
-    for n in range(own_ref.shape[1] // tile):
+    for n in range(outs[0].shape[1] // tile):
         total = jnp.zeros((rows, tile), F32)
         for part, w_ref in enumerate((wq_ref, wk_ref, wv_ref)):
             total += nt(
@@ -304,99 +375,129 @@
                 w_ref[pl.ds(start + n * tile, tile), :],
             )
         c = slice(n * tile, (n + 1) * tile)
-        own_ref[:, c] = total[:piece]
-        for slot, send_ref in enumerate(sends, 1):
-            send_ref[:, c] = total[slot * piece : (slot + 1) * piece].astype(BF16)
-
-
-def output(d, weights, start, width):
+        for slot, out_ref in enumerate(outs):
+            out_ref[:, c] = total[slot * piece : (slot + 1) * piece].astype(out_ref.dtype)
+
+
+def output(d, weights, start, width, kinds, after=()):
     rows = d.shape[0]
-    piece = rows // SIDE
-    send = jax.ShapeDtypeStruct((piece, width), BF16)
     return pl.pallas_call(
         functools.partial(output_kernel, start, 512),
-        out_shape=(jax.ShapeDtypeStruct((piece, width), F32),) + (send,) * 3,
-        in_specs=[VMEM] * 4,
-        out_specs=(VMEM,) * 4,
+        out_shape=tuple(pltpu.VMEM((rows // SIDE, width), kind) for kind in kinds),
+        in_specs=[VMEM] * (4 + len(after)),
+        out_specs=(VMEM,) * SIDE,
         compiler_params=params(12),
         cost_estimate=cost(2 * rows * width * d.shape[1], 6_000_000),
         name="output",
-    )(d, *weights)
-
-
-def add_kernel(own_ref, a_ref, b_ref, c_ref, keep_ref, *sends):
-    piece = keep_ref.shape[0]
-    total = (
-        own_ref[...]
-        + a_ref[...].astype(F32)
-        + b_ref[...].astype(F32)
-        + c_ref[...].astype(F32)
-    )
-    keep_ref[...] = total[:piece].astype(keep_ref.dtype)
-    for slot, send_ref in enumerate(sends, 1):
-        send_ref[...] = total[slot * piece : (slot + 1) * piece].astype(BF16)
-
-
-def add(own, parts, last):
-    rows, width = own.shape
-    piece = rows if last else rows // SIDE
-    keep = jax.ShapeDtypeStruct((piece, width), BF16 if last else F32)
-    send = jax.ShapeDtypeStruct((piece, width), BF16)
-    count = 0 if last else 3
-    return pl.pallas_call(
-        add_kernel,
-        out_shape=(keep,) + (send,) * count,
-        in_specs=[VMEM] * 4,
-        out_specs=(VMEM,) * (1 + count),
-        compiler_params=params(12),
-        cost_estimate=cost(2_000_000, 4_000_000),
+    )(d, *weights, *after)
+
+
+def relay_kernel(own_ref, other_ref, *refs):
+    out_ref = refs[-1]
+    out_ref[...] = (own_ref[...] + other_ref[...].astype(F32)).astype(BF16)
+
+
+def relay(own, other, after=()):
+    return pl.pallas_call(
+        relay_kernel,
+        out_shape=pltpu.VMEM(own.shape, BF16),
+        in_specs=[VMEM] * (2 + len(after)),
+        out_specs=VMEM,
+        compiler_params=params(4),
+        cost_estimate=cost(0, 100_000),
+        name="relay",
+    )(own, other, *after)
+
+
+def total_of(own_ref, parts):
+    total = own_ref[...]
+    for ref in parts:
+        total = total + ref[...].astype(F32)
+    return total
+
+
+def add_kernel(terms, *refs):
+    own_ref, *parts = refs[:terms]
+    earlier, outs = refs[terms:-SIDE], refs[-SIDE:]
+    piece, width = outs[0].shape
+    total = total_of(own_ref, parts)
+    c = slice(width - own_ref.shape[1], width)
+    for slot, out_ref in enumerate(outs):
+        if earlier:
+            out_ref[:, : c.start] = earlier[slot][...]
+        out_ref[:, c] = total[slot * piece : (slot + 1) * piece].astype(out_ref.dtype)
+
+
+def add(half, earlier=()):
+    rows, width = half[0].shape
+    piece = rows // SIDE
+    width += earlier[0].shape[1] if earlier else 0
+    return pl.pallas_call(
+        functools.partial(add_kernel, len(half)),
+        out_shape=(pltpu.VMEM((piece, width), F32),) + (pltpu.VMEM((piece, width), BF16),) * 3,
+        in_specs=[VMEM] * (len(half) + len(earlier)),
+        out_specs=(VMEM,) * SIDE,
+        compiler_params=params(8),
+        cost_estimate=cost(0, 500_000),
         name="add",
+    )(*half, *earlier)
+
+
+def finish_kernel(own_ref, a_ref, b_ref, c_ref, out_ref):
+    out_ref[...] = total_of(own_ref, (a_ref, b_ref, c_ref)).astype(BF16)
+
+
+def finish(own, parts):
+    return pl.pallas_call(
+        finish_kernel,
+        out_shape=jax.ShapeDtypeStruct(own.shape, BF16),
+        in_specs=[VMEM] * SIDE,
+        out_specs=VMEM,
+        compiler_params=params(8),
+        cost_estimate=cost(500_000, 1_000_000),
+        name="finish",
     )(own, *parts)
 
 
+def near_move(array, offset):
+    return move(array, plane_perm(True, offset))
+
+
+def wide_move(array, offset):
+    return move(array, plane_perm(False, offset))
+
+
 def shards(features, w_query, w_key, w_value, log_decay, d_out):
-    weights = (w_query, w_key, w_value)
-    ctx, head = lax.axis_index("ctx"), lax.axis_index("head")
-    x, core = ctx // 2, ctx % 2
-    z, y = head // 4, head % 4
-    rel = jnp.array(REL, jnp.int32)
-    slot, inner = rel[:, None], rel[None, :]
-    ids = jnp.where(
-        core == 0,
-        (z + slot) % 4 * 4 + (y + inner) % 4,
-        (z + inner) % 4 * 4 + (y + slot) % 4,
-    ).reshape(16)
-    place = jnp.stack([core, x])
-
-    near = [move(features, plane_perm(True, -r)) for r in REL[1:]]
-    leading, tail, factors = None, None, None
+    near = [near_move(features, -r) for r in REL[1:]]
+    own, *weights = load((features, w_query, w_key), 48)
+    top, low = join((own, *near), (weights[0],))
+    weights, g = (*weights, w_value), d_out
+    next_top, last_low = wide_move(top, -1), wide_move(low, 1)
+    next_low, last_top = wide_move(low, -1), wide_move(top, 1)
+    far_top, far_low = wide_move(next_top, -1), wide_move(last_low, 1)
     factors, lead, tail = decay_factors(log_decay)
-    mine = jnp.concatenate([features, *near], axis=1)
-    blocks = [move(mine, plane_perm(False, -r)) for r in REL[1:]]
-    sums = project(ids, mine, None, weights, 0, F32)
-    sums = project(ids, blocks[0], sums, weights, 1, F32)
-    sums = project(ids, blocks[1], sums, weights, 2, F32)
-    q, k, v = project(ids, blocks[2], sums, weights, 3, BF16)
-
-    own_l, own_m, pay = states(q, k, v, d_out, lead, tail)
+    sums = project((top, low), (0,), None, weights, F32, (lead,))
+    sums = project((next_top, next_low), (1,), sums, weights, F32)
+    sums = project((last_top, last_low), (2,), sums, weights, F32)
+    q, k, v = project((far_top, far_low), (3,), sums, weights, BF16)
+
+    own_l, own_m, pay = states(q, k, v, g, lead, tail)
     peer = move(pay, core_perm())
-    chip = chip_states(place, own_l, own_m, lead, peer)
+    chip = chip_states(own_l, own_m, lead, peer)
     far = [move(p, chip_perm(d)) for d, p in enumerate(chip, 1)]
-    within = intra(q, k, v, d_out, factors)
-    d = inter(place, ids, q, k, v, d_out, lead, tail, peer, far, within)
-
-    width = w_query.shape[0] // 2
-    kept = []
-    for start in (0, width):
-        own, *sends = output(d, weights, start, width)
-        parts = [move(s, plane_perm(False, r)) for s, r in zip(sends, REL[1:])]
-        kept.append((own, parts))
-    results = []
-    for own, parts in kept:
-        keep, *sends = add(own, parts, False)
-        parts = [move(s, plane_perm(True, r)) for s, r in zip(sends, REL[1:])]
-        results.append((keep, parts))
-    return jnp.concatenate([add(keep, parts, True)[0] for keep, parts in results], axis=1)
+    within = intra(q, k, v, g, factors)
+    d = inter(q, k, v, g, lead, tail, peer, far, within)
+
+    width = w_query.shape[0] // HALVES
+    a_own, a_next, a_last, a_far = output(d, weights, 0, width, (F32, F32, BF16, BF16))
+    b_own, b_next, b_last, b_far = output(d, weights, width, width, (F32, BF16, F32, BF16), (a_own,))
+    a_last, a_far = wide_move(a_last, -1), wide_move(a_far, 1)
+    b_next, b_far = wide_move(b_next, 1), wide_move(b_far, -1)
+    a_next = relay(a_next, a_far)
+    b_last = relay(b_last, b_far, (a_next,))
+    a_next, b_last = wide_move(a_next, 1), wide_move(b_last, -1)
+    keep, *sends = add((b_own, b_next, b_last), add((a_own, a_last, a_next)))
+    return finish(keep, [near_move(s, r) for s, r in zip(sends, REL[1:])])
 
 
 def solution(mesh):

time: 109 us -> 84.5 us (0.78)
  local copies, waits for them, and re-layouts: 23.4 us -> 0.02 us
  starting transfers between devices: 32.5 us -> 34.7 us
  other arithmetic: 1.51 us -> 0 us
  waiting for transfers between devices: 30.1 us -> 28.7 us
    unnamed x33 -> x6, local copies, waits for them, and re-layouts: 23.2 us -> 0.02 us
    ppermute x22, starting transfers between devices: 32.5 us -> 34.7 us  [move(): return lax.ppermute(array, AXES, pairs)]
    ppermute x22, waiting for transfers between devices: 30.1 us -> 28.7 us  [move(): return lax.ppermute(array, AXES, pairs)]
    pallas_call x13 -> x16, Pallas kernels: 18.4 us -> 18.9 us  [the longest x4 5.54 us: project(): pl.pallas_call(functools.partial(project_kernel, slots, has_sum), out_sha...]
  transfers between devices with their start and end apart: 22 -> 22, of which waited for: 12 -> 14; matrix products, arithmetic and copies ran while one was open for 2% -> 0% of each run, Pallas kernels for 12% -> 17%
where the time goes in v2:
time: 84.5 us; the launch traced here: 84.4 us
  starting transfers between devices  34.7 us (41%)
  waiting for transfers between devices  28.7 us (34%)
  Pallas kernels  20.8 us (25%)
    ppermute x22, starting transfers between devices, move(): return lax.ppermute(array, AXES, pairs)  34.7 us
    ppermute x22, waiting for transfers between devices, move(): return lax.ppermute(array, AXES, pairs)  28.7 us
    pallas_call x4, Pallas kernels, project(): pl.pallas_call(functools.partial(project_kernel, slots, has_sum), out_sha...  5.54 us
    pallas_call x2, Pallas kernels, output(): pl.pallas_call(functools.partial(output_kernel, start, 512), out_shape=tu...  5.26 us
    pallas_call x1, Pallas kernels, load(): pl.pallas_call(load_kernel, out_shape=tuple((pltpu.VMEM(a.shape, a.dtype)...  4.84 us
  transfers between devices with their start and end apart: 22, of which 14 were waited for; matrix products, arithmetic and copies ran while one was open for 0% of the time, Pallas kernels for 17%

profile of v2, /device:TPU:0, one launch (start us, length us, event | category | flops | bytes accessed | tf_op | source)
XLA Modules:
  0.0 84.4 jit_solution(17325399208554159940)
XLA Ops:
  0.0 3.1 %collective-permute-start = (bf16[256,384]{1,0:T(8,128)(2,1)}, bf16[256,384]{1,0:T(8,128)(2,1)S(1)}, u32[]{:S(2)}, u32[]{:S(2)}) collective-permute-start(bf16[256,384]{1,0:T(8,128)(2,1)} %refs_0_.1), channel_id=1, source_target_pairs={{0,3},{1,0},{2,1},{3,2},{4,7},{5,4},{6,5},{7,6},{8,11},{9,8},{10,9... | collective-permute-start | bytes 589832 | tf_op jit(solution)/shard_map/ppermute | solution.py:54
  3.1 0.0 collective-permute-start.1
  3.1 2.2 %collective-permute-start.2 = (bf16[256,384]{1,0:T(8,128)(2,1)}, bf16[256,384]{1,0:T(8,128)(2,1)S(1)}, u32[]{:S(2)}, u32[]{:S(2)}) collective-permute-start(bf16[256,384]{1,0:T(8,128)(2,1)} %refs_0_.1), channel_id=1, source_target_pairs={{0,2},{1,3},{2,0},{3,1},{4,6},{5,7},{6,4},{7,5},{8,10},{9,11},{10,... | collective-permute-start | bytes 589832 | tf_op jit(solution)/shard_map/ppermute | solution.py:54
  5.3 4.8 %load.1 = (bf16[256,384]{1,0:T(8,128)(2,1)S(1)}, bf16[6144,512]{1,0:T(8,128)(2,1)S(1)}, bf16[6144,512]{1,0:T(8,128)(2,1)S(1)}) custom-call(bf16[256,384]{1,0:T(8,128)(2,1)} %refs_0_.1, bf16[6144,512]{1,0:T(8,128)(2,1)} %refs_1_.1, bf16[6144,512]{1,0:T(8,128)(2,1)} %refs_2_.1), custom_call_target="tpu_custom_call" | custom-call | bytes 25559040 | tf_op jit(solution)/shard_map/load/pallas_call | solution.py:147
  10.2 0.0 copy-start.2
  10.2 0.0 copy-start
  10.2 0.0 collective-permute-done.refs_1_
  10.2 2.1 %collective-permute-done.1.refs_2_ = bf16[256,384]{1,0:T(8,128)(2,1)S(1)} collective-permute-done((bf16[256,384]{1,0:T(8,128)(2,1)}, bf16[256,384]{1,0:T(8,128)(2,1)S(1)}, u32[]{:S(2)}, u32[]{:S(2)}) %collective-permute-start.1) | collective-permute-done | bytes 196640 | tf_op jit(solution)/shard_map/ppermute | solution.py:54
  12.3 0.0 collective-permute-done.2.refs_3_
  12.3 0.1 join.1
  12.4 4.1 %collective-permute-start.3 = (bf16[128,1536]{1,0:T(8,128)(2,1)S(1)}, bf16[128,1536]{1,0:T(8,128)(2,1)S(1)}, u32[]{:S(2)}, u32[]{:S(2)}) collective-permute-start(bf16[128,1536]{1,0:T(8,128)(2,1)S(1)} %get-tuple-element.52.refs_0_), channel_id=1, source_target_pairs={{0,12},{1,13},{2,14},{3,15},{4,0},{5,1},{6,2},{7,3},{8,4},{9,5},{1... | collective-permute-start | bytes 1179656 | tf_op jit(solution)/shard_map/ppermute | solution.py:54
  16.5 0.0 collective-permute-start.5
  16.5 3.2 %collective-permute-start.8 = (bf16[128,1536]{1,0:T(8,128)(2,1)S(1)}, bf16[128,1536]{1,0:T(8,128)(2,1)S(1)}, u32[]{:S(2)}, u32[]{:S(2)}) collective-permute-start(bf16[128,1536]{1,0:T(8,128)(2,1)S(1)} %get-tuple-element.53.refs_1_), channel_id=1, source_target_pairs={{0,12},{1,13},{2,14},{3,15},{4,0},{5,1},{6,2},{7,3},{8,4},{9,5},{1... | collective-permute-start | bytes 1179656 | tf_op jit(solution)/shard_map/ppermute | solution.py:54
  19.7 0.0 collective-permute-start.7
  19.7 2.1 %collective-permute-done.3.refs_0_ = bf16[128,1536]{1,0:T(8,128)(2,1)S(1)} collective-permute-done((bf16[128,1536]{1,0:T(8,128)(2,1)S(1)}, bf16[128,1536]{1,0:T(8,128)(2,1)S(1)}, u32[]{:S(2)}, u32[]{:S(2)}) %collective-permute-start.3) | collective-permute-done | bytes 393248 | tf_op jit(solution)/shard_map/ppermute | solution.py:54
  21.8 3.7 %collective-permute-start.4 = (bf16[128,1536]{1,0:T(8,128)(2,1)S(1)}, bf16[128,1536]{1,0:T(8,128)(2,1)S(1)}, u32[]{:S(2)}, u32[]{:S(2)}) collective-permute-start(bf16[128,1536]{1,0:T(8,128)(2,1)S(1)} %collective-permute-done.3.refs_0_), channel_id=1, source_target_pairs={{0,12},{1,13},{2,14},{3,15},{4,0},{5,1},{6,2},{7,3},{8,4},{9,5},{1... | collective-permute-start | bytes 1179656 | tf_op jit(solution)/shard_map/ppermute | solution.py:54
  25.5 0.0 collective-permute-done.5.refs_1_
  25.5 0.0 collective-permute-start.6
  25.5 1.3 %decay.1 = (f32[4,256,256]{2,1,0:T(8,128)S(1)}, f32[256,512]{1,0:T(8,128)S(1)}, f32[256,512]{1,0:T(8,128)S(1)}) custom-call(f32[4,256]{1,0:T(4,128)S(1)} %copy-done.2), custom_call_target="tpu_custom_call" | custom-call | flops 2000000 | bytes 2000000 | tf_op jit(solution)/shard_map/decay/pallas_call | solution.py:116
  26.8 1.4 %project.4 = (f32[256,512]{1,0:T(8,128)S(1)}, f32[256,512]{1,0:T(8,128)S(1)}, f32[256,512]{1,0:T(8,128)S(1)}) custom-call(bf16[128,1536]{1,0:T(8,128)(2,1)S(1)} %get-tuple-element.52.refs_0_, bf16[128,1536]{1,0:T(8,128)(2,1)S(1)} %get-tuple-element.53.refs_1_, bf16[6144,512]{1,0:T(8,128)(2,1)S(1)} %get-tuple-element.51.refs_4_.refs_2_.refs_5_.wq_ref, ...), custom_call_target="tpu_custom_call" | custom-call | flops 1207959552 | bytes 6144000 | tf_op jit(solution)/shard_map/project/pallas_call | solution.py:202
  28.2 0.0 collective-permute-done.8.refs_1_
  28.2 1.4 %project.5 = (f32[256,512]{1,0:T(8,128)S(1)}, f32[256,512]{1,0:T(8,128)S(1)}, f32[256,512]{1,0:T(8,128)S(1)}) custom-call(bf16[128,1536]{1,0:T(8,128)(2,1)S(1)} %collective-permute-done.3.refs_0_, bf16[128,1536]{1,0:T(8,128)(2,1)S(1)} %collective-permute-done.8.refs_1_, f32[256,512]{1,0:T(8,128)S(1)} %get-tuple-element.56.refs_2_, ...), custom_call_target="tpu_custom_call" | custom-call | flops 1207959552 | bytes 6144000 | tf_op jit(solution)/shard_map/project/pallas_call | solution.py:202
  29.6 0.1 collective-permute-done.7.refs_0_
  29.7 1.4 %project.6 = (f32[256,512]{1,0:T(8,128)S(1)}, f32[256,512]{1,0:T(8,128)S(1)}, f32[256,512]{1,0:T(8,128)S(1)}) custom-call(bf16[128,1536]{1,0:T(8,128)(2,1)S(1)} %collective-permute-done.7.refs_0_, bf16[128,1536]{1,0:T(8,128)(2,1)S(1)} %collective-permute-done.5.refs_1_, f32[256,512]{1,0:T(8,128)S(1)} %get-tuple-element.59.refs_2_, ...), custom_call_target="tpu_custom_call" | custom-call | flops 1207959552 | bytes 6144000 | tf_op jit(solution)/shard_map/project/pallas_call | solution.py:202
  31.1 0.0 collective-permute-done.4.refs_0_
  31.1 3.4 %collective-permute-done.6.refs_1_ = bf16[128,1536]{1,0:T(8,128)(2,1)S(1)} collective-permute-done((bf16[128,1536]{1,0:T(8,128)(2,1)S(1)}, bf16[128,1536]{1,0:T(8,128)(2,1)S(1)}, u32[]{:S(2)}, u32[]{:S(2)}) %collective-permute-start.6) | collective-permute-done | bytes 393248 | tf_op jit(solution)/shard_map/ppermute | solution.py:54
  34.5 1.4 %project.7 = (bf16[256,512]{1,0:T(8,128)(2,1)S(1)}, bf16[256,512]{1,0:T(8,128)(2,1)S(1)}, bf16[256,512]{1,0:T(8,128)(2,1)S(1)}) custom-call(bf16[128,1536]{1,0:T(8,128)(2,1)S(1)} %collective-permute-done.4.refs_0_, bf16[128,1536]{1,0:T(8,128)(2,1)S(1)} %collective-permute-done.6.refs_1_, f32[256,512]{1,0:T(8,128)S(1)} %get-tuple-element.62.refs_2_, ...), custom_call_target="tpu_custom_call" | custom-call | flops 1207959552 | bytes 6144000 | tf_op jit(solution)/shard_map/project/pallas_call | solution.py:202
  35.9 0.4 states.1
  36.2 0.1 collective-permute-start.9
  36.3 1.5 %collective-permute-done.9.peer_ref = bf16[1088,128]{1,0:T(8,128)(2,1)S(1)} collective-permute-done((bf16[1088,128]{1,0:T(8,128)(2,1)S(1)}, bf16[1088,128]{1,0:T(8,128)(2,1)S(1)}, u32[]{:S(2)}, u32[]{:S(2)}) %collective-permute-start.9) | collective-permute-done | bytes 278560 | tf_op jit(solution)/shard_map/ppermute | solution.py:54
  37.9 0.1 chip_states.1
  38.0 1.6 %collective-permute-start.10 = (bf16[576,128]{1,0:T(8,128)(2,1)S(1)}, bf16[576,128]{1,0:T(8,128)(2,1)S(1)}, u32[]{:S(2)}, u32[]{:S(2)}) collective-permute-start(bf16[576,128]{1,0:T(8,128)(2,1)S(1)} %get-tuple-element.72), channel_id=1, source_target_pairs={{0,32},{1,33},{2,34},{3,35},{4,36},{5,37},{6,38},{7,39},{8,40},{9,... | collective-permute-start | bytes 442376 | tf_op jit(solution)/shard_map/ppermute | solution.py:54
  39.6 2.7 %collective-permute-start.11 = (bf16[576,128]{1,0:T(8,128)(2,1)S(1)}, bf16[576,128]{1,0:T(8,128)(2,1)S(1)}, u32[]{:S(2)}, u32[]{:S(2)}) collective-permute-start(bf16[576,128]{1,0:T(8,128)(2,1)S(1)} %get-tuple-element.73), channel_id=1, source_target_pairs={{0,64},{1,65},{2,66},{3,67},{4,68},{5,69},{6,70},{7,71},{8,72},{9,... | collective-permute-start | bytes 442376 | tf_op jit(solution)/shard_map/ppermute | solution.py:54
  42.3 1.4 %collective-permute-start.12 = (bf16[576,128]{1,0:T(8,128)(2,1)S(1)}, bf16[576,128]{1,0:T(8,128)(2,1)S(1)}, u32[]{:S(2)}, u32[]{:S(2)}) collective-permute-start(bf16[576,128]{1,0:T(8,128)(2,1)S(1)} %get-tuple-element.74), channel_id=1, source_target_pairs={{0,96},{1,97},{2,98},{3,99},{4,100},{5,101},{6,102},{7,103},{8,104... | collective-permute-start | bytes 442376 | tf_op jit(solution)/shard_map/ppermute | solution.py:54
  43.8 1.5 %intra.1 = (f32[256,512]{1,0:T(8,128)S(1)}, f32[256,512]{1,0:T(8,128)S(1)}, f32[256,512]{1,0:T(8,128)S(1)}) custom-call(bf16[256,512]{1,0:T(8,128)(2,1)S(1)} %get-tuple-element.65.q_ref, bf16[256,512]{1,0:T(8,128)(2,1)S(1)} %get-tuple-element.66.k_ref, bf16[256,512]{1,0:T(8,128)(2,1)S(1)} %get-tuple-element.67.v_ref, bf16[256,512]{1,0:T(8,128)(2,1)S(1)} %copy-done.1, ...), custom_call_target="tpu_custom_call" | custom-call | flops 340000000 | bytes 4000000 | tf_op jit(solution)/shard_map/intra/pallas_call | solution.py:260
  45.3 0.0 collective-permute-done.10.one_ref
  45.3 4.1 %collective-permute-done.11.two_ref = bf16[576,128]{1,0:T(8,128)(2,1)S(1)} collective-permute-done((bf16[576,128]{1,0:T(8,128)(2,1)S(1)}, bf16[576,128]{1,0:T(8,128)(2,1)S(1)}, u32[]{:S(2)}, u32[]{:S(2)}) %collective-permute-start.11) | collective-permute-done | bytes 147488 | tf_op jit(solution)/shard_map/ppermute | solution.py:54
  49.4 0.0 collective-permute-done.12.three_ref
  49.4 0.6 inter.1.d_ref
  49.9 2.6 %output.2 = (f32[64,3072]{1,0:T(8,128)S(1)}, f32[64,3072]{1,0:T(8,128)S(1)}, bf16[64,3072]{1,0:T(8,128)(2,1)S(1)}, bf16[64,3072]{1,0:T(8,128)(2,1)S(1)}) custom-call(bf16[256,1536]{1,0:T(8,128)(2,1)S(1)} %inter.1.d_ref, bf16[6144,512]{1,0:T(8,128)(2,1)S(1)} %get-tuple-element.51.refs_4_.refs_2_.refs_5_.wq_ref, ...), custom_call_target="tpu_custom_call" | custom-call | flops 2415919104 | bytes 6000000 | tf_op jit(solution)/shard_map/output/pallas_call | solution.py:384
  52.6 0.1 collective-permute-start.15
  52.7 2.6 %output.3 = (f32[64,3072]{1,0:T(8,128)S(1)}, bf16[64,3072]{1,0:T(8,128)(2,1)S(1)}, f32[64,3072]{1,0:T(8,128)S(1)}, bf16[64,3072]{1,0:T(8,128)(2,1)S(1)}) custom-call(bf16[256,1536]{1,0:T(8,128)(2,1)S(1)} %inter.1.d_ref, bf16[6144,512]{1,0:T(8,128)(2,1)S(1)} %get-tuple-element.51.refs_4_.refs_2_.refs_5_.wq_ref, ...), custom_call_target="tpu_custom_call" | custom-call | flops 2415919104 | bytes 6000000 | tf_op jit(solution)/shard_map/output/pallas_call | solution.py:384
  55.3 3.3 %collective-permute-start.14 = (bf16[64,3072]{1,0:T(8,128)(2,1)S(1)}, bf16[64,3072]{1,0:T(8,128)(2,1)S(1)}, u32[]{:S(2)}, u32[]{:S(2)}) collective-permute-start(bf16[64,3072]{1,0:T(8,128)(2,1)S(1)} %get-tuple-element.83), channel_id=1, source_target_pairs={{0,12},{1,13},{2,14},{3,15},{4,0},{5,1},{6,2},{7,3},{8,4},{9,5},{1... | collective-permute-start | bytes 1179656 | tf_op jit(solution)/shard_map/ppermute | solution.py:54
  58.6 0.1 collective-permute-start.17
  58.7 1.9 %collective-permute-start.13 = (bf16[64,3072]{1,0:T(8,128)(2,1)S(1)}, bf16[64,3072]{1,0:T(8,128)(2,1)S(1)}, u32[]{:S(2)}, u32[]{:S(2)}) collective-permute-start(bf16[64,3072]{1,0:T(8,128)(2,1)S(1)} %get-tuple-element.81), channel_id=1, source_target_pairs={{0,4},{1,5},{2,6},{3,7},{4,8},{5,9},{6,10},{7,11},{8,12},{9,13},{1... | collective-permute-start | bytes 1179656 | tf_op jit(solution)/shard_map/ppermute | solution.py:54
  60.6 1.0 %collective-permute-done.15.other_ref = bf16[64,3072]{1,0:T(8,128)(2,1)S(1)} collective-permute-done((bf16[64,3072]{1,0:T(8,128)(2,1)S(1)}, bf16[64,3072]{1,0:T(8,128)(2,1)S(1)}, u32[]{:S(2)}, u32[]{:S(2)}) %collective-permute-start.15) | collective-permute-done | bytes 393248 | tf_op jit(solution)/shard_map/ppermute | solution.py:54
  61.6 0.1 relay.2.refs_0_
  61.7 0.1 collective-permute-start.18
  61.8 2.1 %collective-permute-done.14.other_ref = bf16[64,3072]{1,0:T(8,128)(2,1)S(1)} collective-permute-done((bf16[64,3072]{1,0:T(8,128)(2,1)S(1)}, bf16[64,3072]{1,0:T(8,128)(2,1)S(1)}, u32[]{:S(2)}, u32[]{:S(2)}) %collective-permute-start.14) | collective-permute-done | bytes 393248 | tf_op jit(solution)/shard_map/ppermute | solution.py:54
  63.9 0.1 relay.3
  64.0 3.8 %collective-permute-start.16 = (bf16[64,3072]{1,0:T(8,128)(2,1)S(1)}, bf16[64,3072]{1,0:T(8,128)(2,1)S(1)}, u32[]{:S(2)}, u32[]{:S(2)}) collective-permute-start(bf16[64,3072]{1,0:T(8,128)(2,1)S(1)} %relay.3), channel_id=1, source_target_pairs={{0,12},{1,13},{2,14},{3,15},{4,0},{5,1},{6,2},{7,3},{8,4},{9,5},{1... | collective-permute-start | bytes 1179656 | tf_op jit(solution)/shard_map/ppermute | solution.py:54
  67.7 0.4 collective-permute-done.17.refs_1_
  68.1 3.8 %collective-permute-done.18.refs_2_ = bf16[64,3072]{1,0:T(8,128)(2,1)S(1)} collective-permute-done((bf16[64,3072]{1,0:T(8,128)(2,1)S(1)}, bf16[64,3072]{1,0:T(8,128)(2,1)S(1)}, u32[]{:S(2)}, u32[]{:S(2)}) %collective-permute-start.18) | collective-permute-done | bytes 393248 | tf_op jit(solution)/shard_map/ppermute | solution.py:54
  71.9 0.1 add.2
  72.0 0.0 collective-permute-done.13.refs_1_
  72.0 1.0 %collective-permute-done.16.refs_2_ = bf16[64,3072]{1,0:T(8,128)(2,1)S(1)} collective-permute-done((bf16[64,3072]{1,0:T(8,128)(2,1)S(1)}, bf16[64,3072]{1,0:T(8,128)(2,1)S(1)}, u32[]{:S(2)}, u32[]{:S(2)}) %collective-permute-start.16) | collective-permute-done | bytes 393248 | tf_op jit(solution)/shard_map/ppermute | solution.py:54
  73.0 0.1 add.3
  73.1 0.1 collective-permute-start.19
  73.2 3.2 %collective-permute-start.20 = (bf16[16,6144]{1,0:T(8,128)(2,1)S(1)}, bf16[16,6144]{1,0:T(8,128)(2,1)S(1)}, u32[]{:S(2)}, u32[]{:S(2)}) collective-permute-start(bf16[16,6144]{1,0:T(8,128)(2,1)S(1)} %get-tuple-element.93), channel_id=1, source_target_pairs={{0,3},{1,0},{2,1},{3,2},{4,7},{5,4},{6,5},{7,6},{8,11},{9,8},{10,9... | collective-permute-start | bytes 589832 | tf_op jit(solution)/shard_map/ppermute | solution.py:54
  76.5 0.0 collective-permute-start.21
  76.5 3.6 %collective-permute-done.19.a_ref = bf16[16,6144]{1,0:T(8,128)(2,1)S(1)} collective-permute-done((bf16[16,6144]{1,0:T(8,128)(2,1)S(1)}, bf16[16,6144]{1,0:T(8,128)(2,1)S(1)}, u32[]{:S(2)}, u32[]{:S(2)}) %collective-permute-start.19) | collective-permute-done | bytes 196640 | tf_op jit(solution)/shard_map/ppermute | solution.py:54
  80.1 1.7 %collective-permute-done.20.b_ref = bf16[16,6144]{1,0:T(8,128)(2,1)S(1)} collective-permute-done((bf16[16,6144]{1,0:T(8,128)(2,1)S(1)}, bf16[16,6144]{1,0:T(8,128)(2,1)S(1)}, u32[]{:S(2)}, u32[]{:S(2)}) %collective-permute-start.20) | collective-permute-done | bytes 196640 | tf_op jit(solution)/shard_map/ppermute | solution.py:54
  81.7 1.9 %collective-permute-done.21.c_ref = bf16[16,6144]{1,0:T(8,128)(2,1)S(1)} collective-permute-done((bf16[16,6144]{1,0:T(8,128)(2,1)S(1)}, bf16[16,6144]{1,0:T(8,128)(2,1)S(1)}, u32[]{:S(2)}, u32[]{:S(2)}) %collective-permute-start.21) | collective-permute-done | bytes 196640 | tf_op jit(solution)/shard_map/ppermute | solution.py:54
  83.6 0.8 finish.1
  (4 shorter events, 0.0 us)
Async XLA Ops:
  0.0 10.2 %collective-permute-start = (bf16[256,384]{1,0:T(8,128)(2,1)}, bf16[256,384]{1,0:T(8,128)(2,1)S(1)}, u32[]{:S(2)}, u32[]{:S(2)}) collective-permute-start(bf16[256,384]{1,0:T(8,128)(2,1)} %refs_0_.1), channel_id=1, source_target_pairs={{0,3},{1,0},{2,1},{3,2},{4,7},{5,4},{6,5},{7,6},{8,11},{9,8},{10,9... | collective-permute-start | bytes 589832 | tf_op jit(solution)/shard_map/ppermute | solution.py:54
  3.1 9.2 %collective-permute-start.1 = (bf16[256,384]{1,0:T(8,128)(2,1)}, bf16[256,384]{1,0:T(8,128)(2,1)S(1)}, u32[]{:S(2)}, u32[]{:S(2)}) collective-permute-start(bf16[256,384]{1,0:T(8,128)(2,1)} %refs_0_.1), channel_id=1, source_target_pairs={{0,1},{1,2},{2,3},{3,0},{4,5},{5,6},{6,7},{7,4},{8,9},{9,10},{10,1... | collective-permute-start | bytes 589832 | tf_op jit(solution)/shard_map/ppermute | solution.py:54
  3.1 9.2 %collective-permute-start.2 = (bf16[256,384]{1,0:T(8,128)(2,1)}, bf16[256,384]{1,0:T(8,128)(2,1)S(1)}, u32[]{:S(2)}, u32[]{:S(2)}) collective-permute-start(bf16[256,384]{1,0:T(8,128)(2,1)} %refs_0_.1), channel_id=1, source_target_pairs={{0,2},{1,3},{2,0},{3,1},{4,6},{5,7},{6,4},{7,5},{8,10},{9,11},{10,... | collective-permute-start | bytes 589832 | tf_op jit(solution)/shard_map/ppermute | solution.py:54
  10.2 15.3 %copy-start.2 = (f32[4,256]{1,0:T(4,128)S(1)}, f32[4,256]{1,0:T(4,128)}, u32[]{:S(2)}) copy-start(f32[4,256]{1,0:T(4,128)} %decay_ref.1) | copy-start | bytes 12292
  10.2 16.6 %copy-start = (bf16[6144,512]{1,0:T(8,128)(2,1)S(1)}, bf16[6144,512]{1,0:T(8,128)(2,1)}, u32[]{:S(2)}) copy-start(bf16[6144,512]{1,0:T(8,128)(2,1)} %wv_ref.3) | copy-start | bytes 18874372
  12.4 9.4 %collective-permute-start.3 = (bf16[128,1536]{1,0:T(8,128)(2,1)S(1)}, bf16[128,1536]{1,0:T(8,128)(2,1)S(1)}, u32[]{:S(2)}, u32[]{:S(2)}) collective-permute-start(bf16[128,1536]{1,0:T(8,128)(2,1)S(1)} %get-tuple-element.52.refs_0_), channel_id=1, source_target_pairs={{0,12},{1,13},{2,14},{3,15},{4,0},{5,1},{6,2},{7,3},{8,4},{9,5},{1... | collective-permute-start | bytes 1179656 | tf_op jit(solution)/shard_map/ppermute | solution.py:54
  16.5 9.0 %collective-permute-start.5 = (bf16[128,1536]{1,0:T(8,128)(2,1)S(1)}, bf16[128,1536]{1,0:T(8,128)(2,1)S(1)}, u32[]{:S(2)}, u32[]{:S(2)}) collective-permute-start(bf16[128,1536]{1,0:T(8,128)(2,1)S(1)} %get-tuple-element.53.refs_1_), channel_id=1, source_target_pairs={{0,4},{1,5},{2,6},{3,7},{4,8},{5,9},{6,10},{7,11},{8,12},{9,13},{1... | collective-permute-start | bytes 1179656 | tf_op jit(solution)/shard_map/ppermute | solution.py:54
  16.5 11.7 %collective-permute-start.8 = (bf16[128,1536]{1,0:T(8,128)(2,1)S(1)}, bf16[128,1536]{1,0:T(8,128)(2,1)S(1)}, u32[]{:S(2)}, u32[]{:S(2)}) collective-permute-start(bf16[128,1536]{1,0:T(8,128)(2,1)S(1)} %get-tuple-element.53.refs_1_), channel_id=1, source_target_pairs={{0,12},{1,13},{2,14},{3,15},{4,0},{5,1},{6,2},{7,3},{8,4},{9,5},{1... | collective-permute-start | bytes 1179656 | tf_op jit(solution)/shard_map/ppermute | solution.py:54
  19.7 10.0 %collective-permute-start.7 = (bf16[128,1536]{1,0:T(8,128)(2,1)S(1)}, bf16[128,1536]{1,0:T(8,128)(2,1)S(1)}, u32[]{:S(2)}, u32[]{:S(2)}) collective-permute-start(bf16[128,1536]{1,0:T(8,128)(2,1)S(1)} %get-tuple-element.52.refs_0_), channel_id=1, source_target_pairs={{0,4},{1,5},{2,6},{3,7},{4,8},{5,9},{6,10},{7,11},{8,12},{9,13},{1... | collective-permute-start | bytes 1179656 | tf_op jit(solution)/shard_map/ppermute | solution.py:54
  21.8 9.3 %collective-permute-start.4 = (bf16[128,1536]{1,0:T(8,128)(2,1)S(1)}, bf16[128,1536]{1,0:T(8,128)(2,1)S(1)}, u32[]{:S(2)}, u32[]{:S(2)}) collective-permute-start(bf16[128,1536]{1,0:T(8,128)(2,1)S(1)} %collective-permute-done.3.refs_0_), channel_id=1, source_target_pairs={{0,12},{1,13},{2,14},{3,15},{4,0},{5,1},{6,2},{7,3},{8,4},{9,5},{1... | collective-permute-start | bytes 1179656 | tf_op jit(solution)/shard_map/ppermute | solution.py:54
  25.5 9.0 %collective-permute-start.6 = (bf16[128,1536]{1,0:T(8,128)(2,1)S(1)}, bf16[128,1536]{1,0:T(8,128)(2,1)S(1)}, u32[]{:S(2)}, u32[]{:S(2)}) collective-permute-start(bf16[128,1536]{1,0:T(8,128)(2,1)S(1)} %collective-permute-done.5.refs_1_), channel_id=1, source_target_pairs={{0,4},{1,5},{2,6},{3,7},{4,8},{5,9},{6,10},{7,11},{8,12},{9,13},{1... | collective-permute-start | bytes 1179656 | tf_op jit(solution)/shard_map/ppermute | solution.py:54
  34.5 1.4 %copy-start.1 = (bf16[256,512]{1,0:T(8,128)(2,1)S(1)}, bf16[256,512]{1,0:T(8,128)(2,1)}, u32[]{:S(2)}) copy-start(bf16[256,512]{1,0:T(8,128)(2,1)} %g_ref.5) | copy-start | bytes 786436
  36.2 1.6 %collective-permute-start.9 = (bf16[1088,128]{1,0:T(8,128)(2,1)S(1)}, bf16[1088,128]{1,0:T(8,128)(2,1)S(1)}, u32[]{:S(2)}, u32[]{:S(2)}) collective-permute-start(bf16[1088,128]{1,0:T(8,128)(2,1)S(1)} %get-tuple-element.69), channel_id=1, source_target_pairs={{0,16},{1,17},{2,18},{3,19},{4,20},{5,21},{6,22},{7,23},{8,24},{9,... | collective-permute-start | bytes 835592 | tf_op jit(solution)/shard_map/ppermute | solution.py:54
  38.0 7.2 %collective-permute-start.10 = (bf16[576,128]{1,0:T(8,128)(2,1)S(1)}, bf16[576,128]{1,0:T(8,128)(2,1)S(1)}, u32[]{:S(2)}, u32[]{:S(2)}) collective-permute-start(bf16[576,128]{1,0:T(8,128)(2,1)S(1)} %get-tuple-element.72), channel_id=1, source_target_pairs={{0,32},{1,33},{2,34},{3,35},{4,36},{5,37},{6,38},{7,39},{8,40},{9,... | collective-permute-start | bytes 442376 | tf_op jit(solution)/shard_map/ppermute | solution.py:54
  39.6 9.8 %collective-permute-start.11 = (bf16[576,128]{1,0:T(8,128)(2,1)S(1)}, bf16[576,128]{1,0:T(8,128)(2,1)S(1)}, u32[]{:S(2)}, u32[]{:S(2)}) collective-permute-start(bf16[576,128]{1,0:T(8,128)(2,1)S(1)} %get-tuple-element.73), channel_id=1, source_target_pairs={{0,64},{1,65},{2,66},{3,67},{4,68},{5,69},{6,70},{7,71},{8,72},{9,... | collective-permute-start | bytes 442376 | tf_op jit(solution)/shard_map/ppermute | solution.py:54
  42.3 7.0 %collective-permute-start.12 = (bf16[576,128]{1,0:T(8,128)(2,1)S(1)}, bf16[576,128]{1,0:T(8,128)(2,1)S(1)}, u32[]{:S(2)}, u32[]{:S(2)}) collective-permute-start(bf16[576,128]{1,0:T(8,128)(2,1)S(1)} %get-tuple-element.74), channel_id=1, source_target_pairs={{0,96},{1,97},{2,98},{3,99},{4,100},{5,101},{6,102},{7,103},{8,104... | collective-permute-start | bytes 442376 | tf_op jit(solution)/shard_map/ppermute | solution.py:54
  52.6 9.1 %collective-permute-start.15 = (bf16[64,3072]{1,0:T(8,128)(2,1)S(1)}, bf16[64,3072]{1,0:T(8,128)(2,1)S(1)}, u32[]{:S(2)}, u32[]{:S(2)}) collective-permute-start(bf16[64,3072]{1,0:T(8,128)(2,1)S(1)} %get-tuple-element.85), channel_id=1, source_target_pairs={{0,4},{1,5},{2,6},{3,7},{4,8},{5,9},{6,10},{7,11},{8,12},{9,13},{1... | collective-permute-start | bytes 1179656 | tf_op jit(solution)/shard_map/ppermute | solution.py:54
  55.3 8.6 %collective-permute-start.14 = (bf16[64,3072]{1,0:T(8,128)(2,1)S(1)}, bf16[64,3072]{1,0:T(8,128)(2,1)S(1)}, u32[]{:S(2)}, u32[]{:S(2)}) collective-permute-start(bf16[64,3072]{1,0:T(8,128)(2,1)S(1)} %get-tuple-element.83), channel_id=1, source_target_pairs={{0,12},{1,13},{2,14},{3,15},{4,0},{5,1},{6,2},{7,3},{8,4},{9,5},{1... | collective-permute-start | bytes 1179656 | tf_op jit(solution)/shard_map/ppermute | solution.py:54
  58.6 9.5 %collective-permute-start.17 = (bf16[64,3072]{1,0:T(8,128)(2,1)S(1)}, bf16[64,3072]{1,0:T(8,128)(2,1)S(1)}, u32[]{:S(2)}, u32[]{:S(2)}) collective-permute-start(bf16[64,3072]{1,0:T(8,128)(2,1)S(1)} %get-tuple-element.86), channel_id=1, source_target_pairs={{0,12},{1,13},{2,14},{3,15},{4,0},{5,1},{6,2},{7,3},{8,4},{9,5},{1... | collective-permute-start | bytes 1179656 | tf_op jit(solution)/shard_map/ppermute | solution.py:54
  58.7 13.3 %collective-permute-start.13 = (bf16[64,3072]{1,0:T(8,128)(2,1)S(1)}, bf16[64,3072]{1,0:T(8,128)(2,1)S(1)}, u32[]{:S(2)}, u32[]{:S(2)}) collective-permute-start(bf16[64,3072]{1,0:T(8,128)(2,1)S(1)} %get-tuple-element.81), channel_id=1, source_target_pairs={{0,4},{1,5},{2,6},{3,7},{4,8},{5,9},{6,10},{7,11},{8,12},{9,13},{1... | collective-permute-start | bytes 1179656 | tf_op jit(solution)/shard_map/ppermute | solution.py:54
  61.7 10.2 %collective-permute-start.18 = (bf16[64,3072]{1,0:T(8,128)(2,1)S(1)}, bf16[64,3072]{1,0:T(8,128)(2,1)S(1)}, u32[]{:S(2)}, u32[]{:S(2)}) collective-permute-start(bf16[64,3072]{1,0:T(8,128)(2,1)S(1)} %relay.2.refs_0_), channel_id=1, source_target_pairs={{0,4},{1,5},{2,6},{3,7},{4,8},{5,9},{6,10},{7,11},{8,12},{9,13},{1... | collective-permute-start | bytes 1179656 | tf_op jit(solution)/shard_map/ppermute | solution.py:54
  64.0 9.1 %collective-permute-start.16 = (bf16[64,3072]{1,0:T(8,128)(2,1)S(1)}, bf16[64,3072]{1,0:T(8,128)(2,1)S(1)}, u32[]{:S(2)}, u32[]{:S(2)}) collective-permute-start(bf16[64,3072]{1,0:T(8,128)(2,1)S(1)} %relay.3), channel_id=1, source_target_pairs={{0,12},{1,13},{2,14},{3,15},{4,0},{5,1},{6,2},{7,3},{8,4},{9,5},{1... | collective-permute-start | bytes 1179656 | tf_op jit(solution)/shard_map/ppermute | solution.py:54
  73.1 6.9 %collective-permute-start.19 = (bf16[16,6144]{1,0:T(8,128)(2,1)S(1)}, bf16[16,6144]{1,0:T(8,128)(2,1)S(1)}, u32[]{:S(2)}, u32[]{:S(2)}) collective-permute-start(bf16[16,6144]{1,0:T(8,128)(2,1)S(1)} %get-tuple-element.92), channel_id=1, source_target_pairs={{0,1},{1,2},{2,3},{3,0},{4,5},{5,6},{6,7},{7,4},{8,9},{9,10},{10,1... | collective-permute-start | bytes 589832 | tf_op jit(solution)/shard_map/ppermute | solution.py:54
  73.2 8.5 %collective-permute-start.20 = (bf16[16,6144]{1,0:T(8,128)(2,1)S(1)}, bf16[16,6144]{1,0:T(8,128)(2,1)S(1)}, u32[]{:S(2)}, u32[]{:S(2)}) collective-permute-start(bf16[16,6144]{1,0:T(8,128)(2,1)S(1)} %get-tuple-element.93), channel_id=1, source_target_pairs={{0,3},{1,0},{2,1},{3,2},{4,7},{5,4},{6,5},{7,6},{8,11},{9,8},{10,9... | collective-permute-start | bytes 589832 | tf_op jit(solution)/shard_map/ppermute | solution.py:54
  76.5 7.2 %collective-permute-start.21 = (bf16[16,6144]{1,0:T(8,128)(2,1)S(1)}, bf16[16,6144]{1,0:T(8,128)(2,1)S(1)}, u32[]{:S(2)}, u32[]{:S(2)}) collective-permute-start(bf16[16,6144]{1,0:T(8,128)(2,1)S(1)} %get-tuple-element.94), channel_id=1, source_target_pairs={{0,2},{1,3},{2,0},{3,1},{4,6},{5,7},{6,4},{7,5},{8,10},{9,11},{10,... | collective-permute-start | bytes 589832 | tf_op jit(solution)/shard_map/ppermute | solution.py:54

commit v3 on v2

--- a/solution.py
+++ b/solution.py
@@ -210,31 +210,47 @@
     )(*xs, *(sums or ()), *weights, *after)
 
 
+def stack(lines):
+    row = lax.broadcasted_iota(jnp.int32, (16, DH), 0)
+    block = jnp.zeros((16, DH), F32)
+    for n, line in enumerate(lines):
+        block = jnp.where(row == n, line, block)
+    return block.astype(BF16)
+
+
+def line_of(ref, start, n):
+    return ref[pl.ds(start, 16), :].astype(F32)[n : n + 1, :]
+
+
 def states_kernel(q_ref, k_ref, v_ref, g_ref, lead_ref, tail_ref, l_ref, m_ref, pay_ref):
     rows, columns = q_ref.shape
     heads = columns // DH
+    local, grad = [], []
     for h in range(heads):
         c = slice(h * DH, (h + 1) * DH)
-        s = slice(h * DH, (h + 1) * DH)
         k = (k_ref[:, c].astype(F32) * tail_ref[:, c]).astype(BF16)
         q = (q_ref[:, c].astype(F32) * lead_ref[:, c]).astype(BF16)
-        local = tn(k, v_ref[:, c])
-        grad = tn(q, g_ref[:, c])
-        l_ref[s, :] = local
-        m_ref[s, :] = grad
-        pay_ref[s, :] = local.astype(BF16)
-        pay_ref[pl.ds(columns + h * DH, DH), :] = grad.astype(BF16)
-        own = jnp.broadcast_to(lead_ref[rows - 1 : rows, c], (16, DH))
-        pay_ref[pl.ds(2 * columns + h * 16, 16), :] = own.astype(BF16)
+        local.append(tn(k, v_ref[:, c]))
+        grad.append(tn(q, g_ref[:, c]))
+    first = place()[1] == 0
+    half = heads // 2
+    for i in range(half):
+        s = slice(i * DH, (i + 1) * DH)
+        for ref, state, at in ((l_ref, local, i), (m_ref, grad, half + i)):
+            low, high = state[i], state[half + i]
+            ref[s, :] = jnp.where(first, low, high)
+            pay_ref[at * DH : (at + 1) * DH, :] = jnp.where(first, high, low).astype(BF16)
+    pay_ref[pl.ds(columns, 16), :] = stack(
+        [lead_ref[rows - 1 : rows, h * DH : (h + 1) * DH] for h in range(heads)]
+    )
 
 
 def states(q, k, v, g, lead, tail):
     columns = q.shape[1]
-    state = pltpu.VMEM((columns, DH), F32)
-    pay = pltpu.VMEM((2 * columns + columns // 8, DH), BF16)
+    state = pltpu.VMEM((columns // 2, DH), F32)
     return pl.pallas_call(
         states_kernel,
-        out_shape=(state, state, pay),
+        out_shape=(state, state, pltpu.VMEM((columns + 16, DH), BF16)),
         in_specs=[VMEM] * 6,
         out_specs=(VMEM,) * 3,
         compiler_params=params(8),
@@ -268,62 +284,68 @@
     )(q, k, v, g, weights)
 
 
+def pair_of(l_ref, m_ref, lead_ref, peer_ref):
+    columns, rows = peer_ref.shape[0] - 16, lead_ref.shape[0]
+    half = columns // DH // 2
+    first = place()[1] == 0
+    for i in range(half):
+        s = slice(i * DH, (i + 1) * DH)
+        own, other = (
+            jnp.where(first, line(i), line(half + i))
+            for line in (
+                lambda h: lead_ref[rows - 1 : rows, h * DH : (h + 1) * DH],
+                lambda h: line_of(peer_ref, columns, h),
+            )
+        )
+        peer_l = peer_ref[s, :].astype(F32)
+        peer_m = peer_ref[(half + i) * DH : (half + i + 1) * DH, :].astype(F32)
+        yield i, (l_ref[s, :], peer_l), (m_ref[s, :], peer_m), (own, other)
+
+
 def chip_kernel(l_ref, m_ref, lead_ref, peer_ref, *pays):
-    columns = l_ref.shape[0]
-    rows = lead_ref.shape[0]
-    heads = columns // DH
     x, core, _, _ = place()
     first = core == 0
-    for h in range(heads):
-        s = slice(h * DH, (h + 1) * DH)
-        own_decay = lead_ref[rows - 1 : rows, s]
-        peer_decay = peer_ref[pl.ds(2 * columns + h * 16, 16), :].astype(F32)[0:1, :]
-        peer_l = peer_ref[s, :].astype(F32)
-        peer_m = peer_ref[pl.ds(columns + h * DH, DH), :].astype(F32)
-        own_l, own_m = l_ref[s, :], m_ref[s, :]
-        chip_l = jnp.where(first, peer_decay * own_l + peer_l, own_decay * peer_l + own_l)
-        chip_m = jnp.where(first, own_m + own_decay * peer_m, peer_m + peer_decay * own_m)
-        decay = jnp.broadcast_to(own_decay * peer_decay, (16, DH)).astype(BF16)
+    decays = []
+    rows = pays[0].shape[0] - 16
+    for i, (own_l, peer_l), (own_m, peer_m), (own, other) in pair_of(l_ref, m_ref, lead_ref, peer_ref):
+        chip_l = jnp.where(first, other * own_l + peer_l, own * peer_l + own_l)
+        chip_m = jnp.where(first, own_m + own * peer_m, peer_m + other * own_m)
+        decays.append(own * other)
         for d, pay_ref in enumerate(pays, 1):
-            pay_ref[s, :] = jnp.where(x + d < 4, chip_l, chip_m).astype(BF16)
-            pay_ref[pl.ds(columns + h * 16, 16), :] = decay
+            both = jnp.where(x + d < 4, chip_l, chip_m)
+            pay_ref[i * DH : (i + 1) * DH, :] = both.astype(BF16)
+    for pay_ref in pays:
+        pay_ref[pl.ds(rows, 16), :] = stack(decays)
 
 
 def chip_states(own_l, own_m, lead, peer):
-    columns = own_l.shape[0]
-    pay = pltpu.VMEM((columns + columns // 8, DH), BF16)
+    pay = pltpu.VMEM((own_l.shape[0] + 16, DH), BF16)
     return pl.pallas_call(
         chip_kernel,
         out_shape=(pay,) * 3,
         in_specs=[VMEM] * 4,
         out_specs=(VMEM,) * 3,
         compiler_params=params(8),
-        cost_estimate=cost(1_000_000, 2_000_000),
+        cost_estimate=cost(500_000, 1_000_000),
         name="chip_states",
     )(own_l, own_m, lead, peer)
 
 
-def inter_kernel(
-    q_ref, k_ref, v_ref, g_ref, lead_ref, tail_ref, peer_ref, one_ref, two_ref, three_ref,
-    dq_ref, dk_ref, dv_ref, out_ref, whole_ref,
-):
-    rows, columns = q_ref.shape
+def outer_kernel(l_ref, m_ref, lead_ref, peer_ref, one_ref, two_ref, three_ref, *refs):
+    mine_ref, theirs_ref = refs[-2:]
     x, core, _, _ = place()
     first = core == 0
     far = (one_ref, two_ref, three_ref)
+    rows = one_ref.shape[0] - 16
 
     def chance(condition):
         return jnp.where(condition, 1.0, 0.0).astype(F32)
 
-    for h in range(columns // DH):
-        c = slice(h * DH, (h + 1) * DH)
-        peer_decay = peer_ref[pl.ds(2 * columns + h * 16, 16), :].astype(F32)[0:1, :]
-        peer_l = peer_ref[c, :].astype(F32)
-        peer_m = peer_ref[pl.ds(columns + h * DH, DH), :].astype(F32)
-        one, two, three = (r[c, :].astype(F32) for r in far)
-        d_one, d_two, d_three = (
-            r[pl.ds(columns + h * 16, 16), :].astype(F32)[0:1, :] for r in far
-        )
+    for i, (own_l, peer_l), (own_m, peer_m), (own, other) in pair_of(l_ref, m_ref, lead_ref, peer_ref):
+        s = slice(i * DH, (i + 1) * DH)
+        one, two, three = (r[s, :].astype(F32) for r in far)
+        d_one, _, d_three = (line_of(r, rows, i) for r in far)
+        d_two = line_of(two_ref, rows, i)
         before = (
             chance(x >= 1) * one
             + (chance(x >= 2) * d_one) * two
@@ -334,8 +356,43 @@
             + (chance(x <= 1) * d_three) * two
             + (chance(x <= 0) * d_three * d_two) * one
         )
-        state = jnp.where(first, before, peer_decay * before + peer_l).astype(BF16)
-        grad = jnp.where(first, peer_decay * after + peer_m, after).astype(BF16)
+        low_decay, high_decay = jnp.where(first, own, other), jnp.where(first, other, own)
+        low_l, high_m = jnp.where(first, own_l, peer_l), jnp.where(first, peer_m, own_m)
+        low = (before, high_decay * after + high_m)
+        high = (low_decay * before + low_l, after)
+        for n in range(2):
+            at = slice(n * rows + i * DH, n * rows + (i + 1) * DH)
+            mine_ref[at, :] = jnp.where(first, low[n], high[n]).astype(BF16)
+            theirs_ref[at, :] = jnp.where(first, high[n], low[n]).astype(BF16)
+
+
+def outer_states(own_l, own_m, lead, peer, far, after):
+    out = pltpu.VMEM((2 * own_l.shape[0], DH), BF16)
+    return pl.pallas_call(
+        outer_kernel,
+        out_shape=(out, out),
+        in_specs=[VMEM] * (7 + len(after)),
+        out_specs=(VMEM,) * 2,
+        compiler_params=params(8),
+        cost_estimate=cost(500_000, 1_000_000),
+        name="outer_states",
+    )(own_l, own_m, lead, peer, *far, *after)
+
+
+def inter_kernel(
+    q_ref, k_ref, v_ref, g_ref, lead_ref, tail_ref, mine_ref, theirs_ref, dq_ref, dk_ref, dv_ref,
+    out_ref, whole_ref,
+):
+    columns = q_ref.shape[1]
+    first = place()[1] == 0
+    half = columns // DH // 2
+    for h in range(columns // DH):
+        c = slice(h * DH, (h + 1) * DH)
+        own = first if h < half else jnp.logical_not(first)
+        state, grad = (
+            jnp.where(own, mine_ref[at : at + DH, :], theirs_ref[at : at + DH, :])
+            for at in (h % half * DH, (half + h % half) * DH)
+        )
         k, v, g = k_ref[:, c], v_ref[:, c], g_ref[:, c]
         lead, tail = lead_ref[:, c], tail_ref[:, c]
         dq = dq_ref[:, c] + lead * nt(g, state)
@@ -348,18 +405,18 @@
         out_ref[pl.ds(n * 16, 16), :] = whole_ref[pl.ds(start, 16), :]
 
 
-def inter(q, k, v, g, lead, tail, peer, far, within):
+def inter(q, k, v, g, lead, tail, mine, theirs, within):
     rows, columns = q.shape
     return pl.pallas_call(
         inter_kernel,
         out_shape=pltpu.VMEM((rows, 3 * columns), BF16),
-        in_specs=[VMEM] * 13,
+        in_specs=[VMEM] * 11,
         out_specs=VMEM,
         scratch_shapes=[pltpu.VMEM((rows, 3 * columns), BF16)],
         compiler_params=params(8),
         cost_estimate=cost(150_000_000, 6_000_000),
         name="inter",
-    )(q, k, v, g, lead, tail, peer, *far, *within)
+    )(q, k, v, g, lead, tail, mine, theirs, *within)
 
 
 def output_kernel(start, tile, d_ref, wq_ref, wk_ref, wv_ref, *refs):
@@ -486,7 +543,9 @@
     chip = chip_states(own_l, own_m, lead, peer)
     far = [move(p, chip_perm(d)) for d, p in enumerate(chip, 1)]
     within = intra(q, k, v, g, factors)
-    d = inter(q, k, v, g, lead, tail, peer, far, within)
+    mine, theirs = outer_states(own_l, own_m, lead, peer, far, within[:1])
+    theirs = move(theirs, core_perm())
+    d = inter(q, k, v, g, lead, tail, mine, theirs, within)
 
     width = w_query.shape[0] // HALVES
     a_own, a_next, a_last, a_far = output(d, weights, 0, width, (F32, F32, BF16, BF16))

time: 84.5 us -> 83.2 us (0.985)
  waiting for transfers between devices: 28.7 us -> 27.1 us
    ppermute x22 -> x23, waiting for transfers between devices: 28.7 us -> 27.1 us  [move(): return lax.ppermute(array, AXES, pairs)]
    ppermute x22 -> x23, starting transfers between devices: 34.7 us -> 34.9 us  [move(): return lax.ppermute(array, AXES, pairs)]
  transfers between devices with their start and end apart: 22 -> 23, of which waited for: 14 -> 16; matrix products, arithmetic and copies ran while one was open for 0% -> 0% of each run, Pallas kernels for 17% -> 18%
where the time goes in v3:
time: 83.2 us; the launch traced here: 83.1 us
  starting transfers between devices  34.9 us (42%)
  waiting for transfers between devices  27.1 us (33%)
  Pallas kernels  20.8 us (25%)
    ppermute x23, starting transfers between devices, move(): return lax.ppermute(array, AXES, pairs)  34.9 us
    ppermute x23, waiting for transfers between devices, move(): return lax.ppermute(array, AXES, pairs)  27.1 us
    pallas_call x4, Pallas kernels, project(): pl.pallas_call(functools.partial(project_kernel, slots, has_sum), out_sha...  5.54 us
    pallas_call x2, Pallas kernels, output(): pl.pallas_call(functools.partial(output_kernel, start, 512), out_shape=tu...  5.26 us
    pallas_call x1, Pallas kernels, load(): pl.pallas_call(load_kernel, out_shape=tuple((pltpu.VMEM(a.shape, a.dtype)...  4.84 us
  transfers between devices with their start and end apart: 23, of which 16 were waited for; matrix products, arithmetic and copies ran while one was open for 0% of the time, Pallas kernels for 18%

profile of v3, /device:TPU:0, one launch (start us, length us, event | category | flops | bytes accessed | tf_op | source)
XLA Modules:
  0.0 83.1 jit_solution(1782867831784660097)
XLA Ops:
  0.0 3.1 %collective-permute-start = (bf16[256,384]{1,0:T(8,128)(2,1)}, bf16[256,384]{1,0:T(8,128)(2,1)S(1)}, u32[]{:S(2)}, u32[]{:S(2)}) collective-permute-start(bf16[256,384]{1,0:T(8,128)(2,1)} %refs_0_.1), channel_id=1, source_target_pairs={{0,3},{1,0},{2,1},{3,2},{4,7},{5,4},{6,5},{7,6},{8,11},{9,8},{10,9... | collective-permute-start | bytes 589832 | tf_op jit(solution)/shard_map/ppermute | solution.py:54
  3.1 0.0 collective-permute-start.1
  3.1 2.2 %collective-permute-start.2 = (bf16[256,384]{1,0:T(8,128)(2,1)}, bf16[256,384]{1,0:T(8,128)(2,1)S(1)}, u32[]{:S(2)}, u32[]{:S(2)}) collective-permute-start(bf16[256,384]{1,0:T(8,128)(2,1)} %refs_0_.1), channel_id=1, source_target_pairs={{0,2},{1,3},{2,0},{3,1},{4,6},{5,7},{6,4},{7,5},{8,10},{9,11},{10,... | collective-permute-start | bytes 589832 | tf_op jit(solution)/shard_map/ppermute | solution.py:54
  5.3 4.8 %load.1 = (bf16[256,384]{1,0:T(8,128)(2,1)S(1)}, bf16[6144,512]{1,0:T(8,128)(2,1)S(1)}, bf16[6144,512]{1,0:T(8,128)(2,1)S(1)}) custom-call(bf16[256,384]{1,0:T(8,128)(2,1)} %refs_0_.1, bf16[6144,512]{1,0:T(8,128)(2,1)} %refs_1_.1, bf16[6144,512]{1,0:T(8,128)(2,1)} %refs_2_.1), custom_call_target="tpu_custom_call" | custom-call | bytes 25559040 | tf_op jit(solution)/shard_map/load/pallas_call | solution.py:147
  10.2 0.0 copy-start.2
  10.2 0.0 copy-start
  10.2 0.0 collective-permute-done.refs_1_
  10.2 2.1 %collective-permute-done.1.refs_2_ = bf16[256,384]{1,0:T(8,128)(2,1)S(1)} collective-permute-done((bf16[256,384]{1,0:T(8,128)(2,1)}, bf16[256,384]{1,0:T(8,128)(2,1)S(1)}, u32[]{:S(2)}, u32[]{:S(2)}) %collective-permute-start.1) | collective-permute-done | bytes 196640 | tf_op jit(solution)/shard_map/ppermute | solution.py:54
  12.3 0.0 collective-permute-done.2.refs_3_
  12.3 0.1 join.1
  12.4 4.1 %collective-permute-start.3 = (bf16[128,1536]{1,0:T(8,128)(2,1)S(1)}, bf16[128,1536]{1,0:T(8,128)(2,1)S(1)}, u32[]{:S(2)}, u32[]{:S(2)}) collective-permute-start(bf16[128,1536]{1,0:T(8,128)(2,1)S(1)} %get-tuple-element.54.refs_0_), channel_id=1, source_target_pairs={{0,12},{1,13},{2,14},{3,15},{4,0},{5,1},{6,2},{7,3},{8,4},{9,5},{1... | collective-permute-start | bytes 1179656 | tf_op jit(solution)/shard_map/ppermute | solution.py:54
  16.5 0.0 collective-permute-start.5
  16.5 3.2 %collective-permute-start.8 = (bf16[128,1536]{1,0:T(8,128)(2,1)S(1)}, bf16[128,1536]{1,0:T(8,128)(2,1)S(1)}, u32[]{:S(2)}, u32[]{:S(2)}) collective-permute-start(bf16[128,1536]{1,0:T(8,128)(2,1)S(1)} %get-tuple-element.55.refs_1_), channel_id=1, source_target_pairs={{0,12},{1,13},{2,14},{3,15},{4,0},{5,1},{6,2},{7,3},{8,4},{9,5},{1... | collective-permute-start | bytes 1179656 | tf_op jit(solution)/shard_map/ppermute | solution.py:54
  19.7 0.0 collective-permute-start.7
  19.7 2.1 %collective-permute-done.3.refs_0_ = bf16[128,1536]{1,0:T(8,128)(2,1)S(1)} collective-permute-done((bf16[128,1536]{1,0:T(8,128)(2,1)S(1)}, bf16[128,1536]{1,0:T(8,128)(2,1)S(1)}, u32[]{:S(2)}, u32[]{:S(2)}) %collective-permute-start.3) | collective-permute-done | bytes 393248 | tf_op jit(solution)/shard_map/ppermute | solution.py:54
  21.8 3.7 %collective-permute-start.4 = (bf16[128,1536]{1,0:T(8,128)(2,1)S(1)}, bf16[128,1536]{1,0:T(8,128)(2,1)S(1)}, u32[]{:S(2)}, u32[]{:S(2)}) collective-permute-start(bf16[128,1536]{1,0:T(8,128)(2,1)S(1)} %collective-permute-done.3.refs_0_), channel_id=1, source_target_pairs={{0,12},{1,13},{2,14},{3,15},{4,0},{5,1},{6,2},{7,3},{8,4},{9,5},{1... | collective-permute-start | bytes 1179656 | tf_op jit(solution)/shard_map/ppermute | solution.py:54
  25.5 0.0 collective-permute-done.5.refs_1_
  25.5 0.0 collective-permute-start.6
  25.5 1.3 %decay.1 = (f32[4,256,256]{2,1,0:T(8,128)S(1)}, f32[256,512]{1,0:T(8,128)S(1)}, f32[256,512]{1,0:T(8,128)S(1)}) custom-call(f32[4,256]{1,0:T(4,128)S(1)} %copy-done.2), custom_call_target="tpu_custom_call" | custom-call | flops 2000000 | bytes 2000000 | tf_op jit(solution)/shard_map/decay/pallas_call | solution.py:116
  26.8 1.4 %project.4 = (f32[256,512]{1,0:T(8,128)S(1)}, f32[256,512]{1,0:T(8,128)S(1)}, f32[256,512]{1,0:T(8,128)S(1)}) custom-call(bf16[128,1536]{1,0:T(8,128)(2,1)S(1)} %get-tuple-element.54.refs_0_, bf16[128,1536]{1,0:T(8,128)(2,1)S(1)} %get-tuple-element.55.refs_1_, bf16[6144,512]{1,0:T(8,128)(2,1)S(1)} %get-tuple-element.53.refs_4_.refs_2_.refs_5_.wq_ref, ...), custom_call_target="tpu_custom_call" | custom-call | flops 1207959552 | bytes 6144000 | tf_op jit(solution)/shard_map/project/pallas_call | solution.py:202
  28.2 0.0 collective-permute-done.8.refs_1_
  28.2 1.4 %project.5 = (f32[256,512]{1,0:T(8,128)S(1)}, f32[256,512]{1,0:T(8,128)S(1)}, f32[256,512]{1,0:T(8,128)S(1)}) custom-call(bf16[128,1536]{1,0:T(8,128)(2,1)S(1)} %collective-permute-done.3.refs_0_, bf16[128,1536]{1,0:T(8,128)(2,1)S(1)} %collective-permute-done.8.refs_1_, f32[256,512]{1,0:T(8,128)S(1)} %get-tuple-element.58.refs_2_, ...), custom_call_target="tpu_custom_call" | custom-call | flops 1207959552 | bytes 6144000 | tf_op jit(solution)/shard_map/project/pallas_call | solution.py:202
  29.6 0.1 collective-permute-done.7.refs_0_
  29.7 1.4 %project.6 = (f32[256,512]{1,0:T(8,128)S(1)}, f32[256,512]{1,0:T(8,128)S(1)}, f32[256,512]{1,0:T(8,128)S(1)}) custom-call(bf16[128,1536]{1,0:T(8,128)(2,1)S(1)} %collective-permute-done.7.refs_0_, bf16[128,1536]{1,0:T(8,128)(2,1)S(1)} %collective-permute-done.5.refs_1_, f32[256,512]{1,0:T(8,128)S(1)} %get-tuple-element.61.refs_2_, ...), custom_call_target="tpu_custom_call" | custom-call | flops 1207959552 | bytes 6144000 | tf_op jit(solution)/shard_map/project/pallas_call | solution.py:202
  31.1 0.0 collective-permute-done.4.refs_0_
  31.1 3.4 %collective-permute-done.6.refs_1_ = bf16[128,1536]{1,0:T(8,128)(2,1)S(1)} collective-permute-done((bf16[128,1536]{1,0:T(8,128)(2,1)S(1)}, bf16[128,1536]{1,0:T(8,128)(2,1)S(1)}, u32[]{:S(2)}, u32[]{:S(2)}) %collective-permute-start.6) | collective-permute-done | bytes 393248 | tf_op jit(solution)/shard_map/ppermute | solution.py:54
  34.5 1.4 %project.7 = (bf16[256,512]{1,0:T(8,128)(2,1)S(1)}, bf16[256,512]{1,0:T(8,128)(2,1)S(1)}, bf16[256,512]{1,0:T(8,128)(2,1)S(1)}) custom-call(bf16[128,1536]{1,0:T(8,128)(2,1)S(1)} %collective-permute-done.4.refs_0_, bf16[128,1536]{1,0:T(8,128)(2,1)S(1)} %collective-permute-done.6.refs_1_, f32[256,512]{1,0:T(8,128)S(1)} %get-tuple-element.64.refs_2_, ...), custom_call_target="tpu_custom_call" | custom-call | flops 1207959552 | bytes 6144000 | tf_op jit(solution)/shard_map/project/pallas_call | solution.py:202
  35.9 0.4 states.1
  36.3 0.1 collective-permute-start.9
  36.3 1.3 %collective-permute-done.9.peer_ref = bf16[528,128]{1,0:T(8,128)(2,1)S(1)} collective-permute-done((bf16[528,128]{1,0:T(8,128)(2,1)S(1)}, bf16[528,128]{1,0:T(8,128)(2,1)S(1)}, u32[]{:S(2)}, u32[]{:S(2)}) %collective-permute-start.9) | collective-permute-done | bytes 135200 | tf_op jit(solution)/shard_map/ppermute | solution.py:54
  37.7 0.1 chip_states.1
  37.8 1.6 %collective-permute-start.10 = (bf16[272,128]{1,0:T(8,128)(2,1)S(1)}, bf16[272,128]{1,0:T(8,128)(2,1)S(1)}, u32[]{:S(2)}, u32[]{:S(2)}) collective-permute-start(bf16[272,128]{1,0:T(8,128)(2,1)S(1)} %get-tuple-element.74), channel_id=1, source_target_pairs={{0,32},{1,33},{2,34},{3,35},{4,36},{5,37},{6,38},{7,39},{8,40},{9,... | collective-permute-start | bytes 208904 | tf_op jit(solution)/shard_map/ppermute | solution.py:54
  39.3 2.7 %collective-permute-start.11 = (bf16[272,128]{1,0:T(8,128)(2,1)S(1)}, bf16[272,128]{1,0:T(8,128)(2,1)S(1)}, u32[]{:S(2)}, u32[]{:S(2)}) collective-permute-start(bf16[272,128]{1,0:T(8,128)(2,1)S(1)} %get-tuple-element.75), channel_id=1, source_target_pairs={{0,64},{1,65},{2,66},{3,67},{4,68},{5,69},{6,70},{7,71},{8,72},{9,... | collective-permute-start | bytes 208904 | tf_op jit(solution)/shard_map/ppermute | solution.py:54
  42.1 1.4 %collective-permute-start.12 = (bf16[272,128]{1,0:T(8,128)(2,1)S(1)}, bf16[272,128]{1,0:T(8,128)(2,1)S(1)}, u32[]{:S(2)}, u32[]{:S(2)}) collective-permute-start(bf16[272,128]{1,0:T(8,128)(2,1)S(1)} %get-tuple-element.76), channel_id=1, source_target_pairs={{0,96},{1,97},{2,98},{3,99},{4,100},{5,101},{6,102},{7,103},{8,104... | collective-permute-start | bytes 208904 | tf_op jit(solution)/shard_map/ppermute | solution.py:54
  43.5 1.5 %intra.1 = (f32[256,512]{1,0:T(8,128)S(1)}, f32[256,512]{1,0:T(8,128)S(1)}, f32[256,512]{1,0:T(8,128)S(1)}) custom-call(bf16[256,512]{1,0:T(8,128)(2,1)S(1)} %get-tuple-element.67.q_ref, bf16[256,512]{1,0:T(8,128)(2,1)S(1)} %get-tuple-element.68.k_ref, bf16[256,512]{1,0:T(8,128)(2,1)S(1)} %get-tuple-element.69.v_ref, bf16[256,512]{1,0:T(8,128)(2,1)S(1)} %copy-done.1, ...), custom_call_target="tpu_custom_call" | custom-call | flops 340000000 | bytes 4000000 | tf_op jit(solution)/shard_map/intra/pallas_call | solution.py:276
  45.0 0.7 collective-permute-done.11.two_ref
  45.8 0.6 collective-permute-done.12.three_ref
  46.4 0.1 outer_states.1
  46.5 0.3 collective-permute-start.13
  46.8 1.3 %collective-permute-done.13.theirs_ref = bf16[512,128]{1,0:T(8,128)(2,1)S(1)} collective-permute-done((bf16[512,128]{1,0:T(8,128)(2,1)S(1)}, bf16[512,128]{1,0:T(8,128)(2,1)S(1)}, u32[]{:S(2)}, u32[]{:S(2)}) %collective-permute-start.13) | collective-permute-done | bytes 131104 | tf_op jit(solution)/shard_map/ppermute | solution.py:54
  48.1 0.5 inter.1.d_ref
  48.7 2.6 %output.2 = (f32[64,3072]{1,0:T(8,128)S(1)}, f32[64,3072]{1,0:T(8,128)S(1)}, bf16[64,3072]{1,0:T(8,128)(2,1)S(1)}, bf16[64,3072]{1,0:T(8,128)(2,1)S(1)}) custom-call(bf16[256,1536]{1,0:T(8,128)(2,1)S(1)} %inter.1.d_ref, bf16[6144,512]{1,0:T(8,128)(2,1)S(1)} %get-tuple-element.53.refs_4_.refs_2_.refs_5_.wq_ref, ...), custom_call_target="tpu_custom_call" | custom-call | flops 2415919104 | bytes 6000000 | tf_op jit(solution)/shard_map/output/pallas_call | solution.py:441
  51.3 0.1 collective-permute-start.16
  51.4 2.6 %output.3 = (f32[64,3072]{1,0:T(8,128)S(1)}, bf16[64,3072]{1,0:T(8,128)(2,1)S(1)}, f32[64,3072]{1,0:T(8,128)S(1)}, bf16[64,3072]{1,0:T(8,128)(2,1)S(1)}) custom-call(bf16[256,1536]{1,0:T(8,128)(2,1)S(1)} %inter.1.d_ref, bf16[6144,512]{1,0:T(8,128)(2,1)S(1)} %get-tuple-element.53.refs_4_.refs_2_.refs_5_.wq_ref, ...), custom_call_target="tpu_custom_call" | custom-call | flops 2415919104 | bytes 6000000 | tf_op jit(solution)/shard_map/output/pallas_call | solution.py:441
  54.0 3.3 %collective-permute-start.15 = (bf16[64,3072]{1,0:T(8,128)(2,1)S(1)}, bf16[64,3072]{1,0:T(8,128)(2,1)S(1)}, u32[]{:S(2)}, u32[]{:S(2)}) collective-permute-start(bf16[64,3072]{1,0:T(8,128)(2,1)S(1)} %get-tuple-element.87), channel_id=1, source_target_pairs={{0,12},{1,13},{2,14},{3,15},{4,0},{5,1},{6,2},{7,3},{8,4},{9,5},{1... | collective-permute-start | bytes 1179656 | tf_op jit(solution)/shard_map/ppermute | solution.py:54
  57.3 0.1 collective-permute-start.18
  57.4 1.9 %collective-permute-start.14 = (bf16[64,3072]{1,0:T(8,128)(2,1)S(1)}, bf16[64,3072]{1,0:T(8,128)(2,1)S(1)}, u32[]{:S(2)}, u32[]{:S(2)}) collective-permute-start(bf16[64,3072]{1,0:T(8,128)(2,1)S(1)} %get-tuple-element.85), channel_id=1, source_target_pairs={{0,4},{1,5},{2,6},{3,7},{4,8},{5,9},{6,10},{7,11},{8,12},{9,13},{1... | collective-permute-start | bytes 1179656 | tf_op jit(solution)/shard_map/ppermute | solution.py:54
  59.4 1.0 %collective-permute-done.16.other_ref = bf16[64,3072]{1,0:T(8,128)(2,1)S(1)} collective-permute-done((bf16[64,3072]{1,0:T(8,128)(2,1)S(1)}, bf16[64,3072]{1,0:T(8,128)(2,1)S(1)}, u32[]{:S(2)}, u32[]{:S(2)}) %collective-permute-start.16) | collective-permute-done | bytes 393248 | tf_op jit(solution)/shard_map/ppermute | solution.py:54
  60.4 0.1 relay.2.refs_0_
  60.4 0.1 collective-permute-start.19
  60.5 2.1 %collective-permute-done.15.other_ref = bf16[64,3072]{1,0:T(8,128)(2,1)S(1)} collective-permute-done((bf16[64,3072]{1,0:T(8,128)(2,1)S(1)}, bf16[64,3072]{1,0:T(8,128)(2,1)S(1)}, u32[]{:S(2)}, u32[]{:S(2)}) %collective-permute-start.15) | collective-permute-done | bytes 393248 | tf_op jit(solution)/shard_map/ppermute | solution.py:54
  62.6 0.1 relay.3
  62.7 3.8 %collective-permute-start.17 = (bf16[64,3072]{1,0:T(8,128)(2,1)S(1)}, bf16[64,3072]{1,0:T(8,128)(2,1)S(1)}, u32[]{:S(2)}, u32[]{:S(2)}) collective-permute-start(bf16[64,3072]{1,0:T(8,128)(2,1)S(1)} %relay.3), channel_id=1, source_target_pairs={{0,12},{1,13},{2,14},{3,15},{4,0},{5,1},{6,2},{7,3},{8,4},{9,5},{1... | collective-permute-start | bytes 1179656 | tf_op jit(solution)/shard_map/ppermute | solution.py:54
  66.5 0.4 collective-permute-done.18.refs_1_
  66.8 3.8 %collective-permute-done.19.refs_2_ = bf16[64,3072]{1,0:T(8,128)(2,1)S(1)} collective-permute-done((bf16[64,3072]{1,0:T(8,128)(2,1)S(1)}, bf16[64,3072]{1,0:T(8,128)(2,1)S(1)}, u32[]{:S(2)}, u32[]{:S(2)}) %collective-permute-start.19) | collective-permute-done | bytes 393248 | tf_op jit(solution)/shard_map/ppermute | solution.py:54
  70.6 0.1 add.2
  70.7 1.0 %collective-permute-done.17.refs_2_ = bf16[64,3072]{1,0:T(8,128)(2,1)S(1)} collective-permute-done((bf16[64,3072]{1,0:T(8,128)(2,1)S(1)}, bf16[64,3072]{1,0:T(8,128)(2,1)S(1)}, u32[]{:S(2)}, u32[]{:S(2)}) %collective-permute-start.17) | collective-permute-done | bytes 393248 | tf_op jit(solution)/shard_map/ppermute | solution.py:54
  71.8 0.1 add.3
  71.9 0.1 collective-permute-start.20
  72.0 3.2 %collective-permute-start.21 = (bf16[16,6144]{1,0:T(8,128)(2,1)S(1)}, bf16[16,6144]{1,0:T(8,128)(2,1)S(1)}, u32[]{:S(2)}, u32[]{:S(2)}) collective-permute-start(bf16[16,6144]{1,0:T(8,128)(2,1)S(1)} %get-tuple-element.97), channel_id=1, source_target_pairs={{0,3},{1,0},{2,1},{3,2},{4,7},{5,4},{6,5},{7,6},{8,11},{9,8},{10,9... | collective-permute-start | bytes 589832 | tf_op jit(solution)/shard_map/ppermute | solution.py:54
  75.2 3.6 %collective-permute-done.20.a_ref = bf16[16,6144]{1,0:T(8,128)(2,1)S(1)} collective-permute-done((bf16[16,6144]{1,0:T(8,128)(2,1)S(1)}, bf16[16,6144]{1,0:T(8,128)(2,1)S(1)}, u32[]{:S(2)}, u32[]{:S(2)}) %collective-permute-start.20) | collective-permute-done | bytes 196640 | tf_op jit(solution)/shard_map/ppermute | solution.py:54
  78.8 1.7 %collective-permute-done.21.b_ref = bf16[16,6144]{1,0:T(8,128)(2,1)S(1)} collective-permute-done((bf16[16,6144]{1,0:T(8,128)(2,1)S(1)}, bf16[16,6144]{1,0:T(8,128)(2,1)S(1)}, u32[]{:S(2)}, u32[]{:S(2)}) %collective-permute-start.21) | collective-permute-done | bytes 196640 | tf_op jit(solution)/shard_map/ppermute | solution.py:54
  80.5 1.9 %collective-permute-done.22.c_ref = bf16[16,6144]{1,0:T(8,128)(2,1)S(1)} collective-permute-done((bf16[16,6144]{1,0:T(8,128)(2,1)S(1)}, bf16[16,6144]{1,0:T(8,128)(2,1)S(1)}, u32[]{:S(2)}, u32[]{:S(2)}) %collective-permute-start.22) | collective-permute-done | bytes 196640 | tf_op jit(solution)/shard_map/ppermute | solution.py:54
  82.4 0.8 finish.1
  (7 shorter events, 0.0 us)
Async XLA Ops:
  0.0 10.2 %collective-permute-start = (bf16[256,384]{1,0:T(8,128)(2,1)}, bf16[256,384]{1,0:T(8,128)(2,1)S(1)}, u32[]{:S(2)}, u32[]{:S(2)}) collective-permute-start(bf16[256,384]{1,0:T(8,128)(2,1)} %refs_0_.1), channel_id=1, source_target_pairs={{0,3},{1,0},{2,1},{3,2},{4,7},{5,4},{6,5},{7,6},{8,11},{9,8},{10,9... | collective-permute-start | bytes 589832 | tf_op jit(solution)/shard_map/ppermute | solution.py:54
  3.1 9.2 %collective-permute-start.1 = (bf16[256,384]{1,0:T(8,128)(2,1)}, bf16[256,384]{1,0:T(8,128)(2,1)S(1)}, u32[]{:S(2)}, u32[]{:S(2)}) collective-permute-start(bf16[256,384]{1,0:T(8,128)(2,1)} %refs_0_.1), channel_id=1, source_target_pairs={{0,1},{1,2},{2,3},{3,0},{4,5},{5,6},{6,7},{7,4},{8,9},{9,10},{10,1... | collective-permute-start | bytes 589832 | tf_op jit(solution)/shard_map/ppermute | solution.py:54
  3.1 9.2 %collective-permute-start.2 = (bf16[256,384]{1,0:T(8,128)(2,1)}, bf16[256,384]{1,0:T(8,128)(2,1)S(1)}, u32[]{:S(2)}, u32[]{:S(2)}) collective-permute-start(bf16[256,384]{1,0:T(8,128)(2,1)} %refs_0_.1), channel_id=1, source_target_pairs={{0,2},{1,3},{2,0},{3,1},{4,6},{5,7},{6,4},{7,5},{8,10},{9,11},{10,... | collective-permute-start | bytes 589832 | tf_op jit(solution)/shard_map/ppermute | solution.py:54
  10.2 15.3 %copy-start.2 = (f32[4,256]{1,0:T(4,128)S(1)}, f32[4,256]{1,0:T(4,128)}, u32[]{:S(2)}) copy-start(f32[4,256]{1,0:T(4,128)} %decay_ref.1) | copy-start | bytes 12292
  10.2 16.6 %copy-start = (bf16[6144,512]{1,0:T(8,128)(2,1)S(1)}, bf16[6144,512]{1,0:T(8,128)(2,1)}, u32[]{:S(2)}) copy-start(bf16[6144,512]{1,0:T(8,128)(2,1)} %wv_ref.3) | copy-start | bytes 18874372
  12.4 9.4 %collective-permute-start.3 = (bf16[128,1536]{1,0:T(8,128)(2,1)S(1)}, bf16[128,1536]{1,0:T(8,128)(2,1)S(1)}, u32[]{:S(2)}, u32[]{:S(2)}) collective-permute-start(bf16[128,1536]{1,0:T(8,128)(2,1)S(1)} %get-tuple-element.54.refs_0_), channel_id=1, source_target_pairs={{0,12},{1,13},{2,14},{3,15},{4,0},{5,1},{6,2},{7,3},{8,4},{9,5},{1... | collective-permute-start | bytes 1179656 | tf_op jit(solution)/shard_map/ppermute | solution.py:54
  16.5 9.0 %collective-permute-start.5 = (bf16[128,1536]{1,0:T(8,128)(2,1)S(1)}, bf16[128,1536]{1,0:T(8,128)(2,1)S(1)}, u32[]{:S(2)}, u32[]{:S(2)}) collective-permute-start(bf16[128,1536]{1,0:T(8,128)(2,1)S(1)} %get-tuple-element.55.refs_1_), channel_id=1, source_target_pairs={{0,4},{1,5},{2,6},{3,7},{4,8},{5,9},{6,10},{7,11},{8,12},{9,13},{1... | collective-permute-start | bytes 1179656 | tf_op jit(solution)/shard_map/ppermute | solution.py:54
  16.5 11.7 %collective-permute-start.8 = (bf16[128,1536]{1,0:T(8,128)(2,1)S(1)}, bf16[128,1536]{1,0:T(8,128)(2,1)S(1)}, u32[]{:S(2)}, u32[]{:S(2)}) collective-permute-start(bf16[128,1536]{1,0:T(8,128)(2,1)S(1)} %get-tuple-element.55.refs_1_), channel_id=1, source_target_pairs={{0,12},{1,13},{2,14},{3,15},{4,0},{5,1},{6,2},{7,3},{8,4},{9,5},{1... | collective-permute-start | bytes 1179656 | tf_op jit(solution)/shard_map/ppermute | solution.py:54
  19.7 10.0 %collective-permute-start.7 = (bf16[128,1536]{1,0:T(8,128)(2,1)S(1)}, bf16[128,1536]{1,0:T(8,128)(2,1)S(1)}, u32[]{:S(2)}, u32[]{:S(2)}) collective-permute-start(bf16[128,1536]{1,0:T(8,128)(2,1)S(1)} %get-tuple-element.54.refs_0_), channel_id=1, source_target_pairs={{0,4},{1,5},{2,6},{3,7},{4,8},{5,9},{6,10},{7,11},{8,12},{9,13},{1... | collective-permute-start | bytes 1179656 | tf_op jit(solution)/shard_map/ppermute | solution.py:54
  21.8 9.3 %collective-permute-start.4 = (bf16[128,1536]{1,0:T(8,128)(2,1)S(1)}, bf16[128,1536]{1,0:T(8,128)(2,1)S(1)}, u32[]{:S(2)}, u32[]{:S(2)}) collective-permute-start(bf16[128,1536]{1,0:T(8,128)(2,1)S(1)} %collective-permute-done.3.refs_0_), channel_id=1, source_target_pairs={{0,12},{1,13},{2,14},{3,15},{4,0},{5,1},{6,2},{7,3},{8,4},{9,5},{1... | collective-permute-start | bytes 1179656 | tf_op jit(solution)/shard_map/ppermute | solution.py:54
  25.5 9.0 %collective-permute-start.6 = (bf16[128,1536]{1,0:T(8,128)(2,1)S(1)}, bf16[128,1536]{1,0:T(8,128)(2,1)S(1)}, u32[]{:S(2)}, u32[]{:S(2)}) collective-permute-start(bf16[128,1536]{1,0:T(8,128)(2,1)S(1)} %collective-permute-done.5.refs_1_), channel_id=1, source_target_pairs={{0,4},{1,5},{2,6},{3,7},{4,8},{5,9},{6,10},{7,11},{8,12},{9,13},{1... | collective-permute-start | bytes 1179656 | tf_op jit(solution)/shard_map/ppermute | solution.py:54
  34.5 1.4 %copy-start.1 = (bf16[256,512]{1,0:T(8,128)(2,1)S(1)}, bf16[256,512]{1,0:T(8,128)(2,1)}, u32[]{:S(2)}) copy-start(bf16[256,512]{1,0:T(8,128)(2,1)} %g_ref.5) | copy-start | bytes 786436
  36.3 1.4 %collective-permute-start.9 = (bf16[528,128]{1,0:T(8,128)(2,1)S(1)}, bf16[528,128]{1,0:T(8,128)(2,1)S(1)}, u32[]{:S(2)}, u32[]{:S(2)}) collective-permute-start(bf16[528,128]{1,0:T(8,128)(2,1)S(1)} %get-tuple-element.73), channel_id=1, source_target_pairs={{0,16},{1,17},{2,18},{3,19},{4,20},{5,21},{6,22},{7,23},{8,24},{9,... | collective-permute-start | bytes 405512 | tf_op jit(solution)/shard_map/ppermute | solution.py:54
  37.8 7.2 %collective-permute-start.10 = (bf16[272,128]{1,0:T(8,128)(2,1)S(1)}, bf16[272,128]{1,0:T(8,128)(2,1)S(1)}, u32[]{:S(2)}, u32[]{:S(2)}) collective-permute-start(bf16[272,128]{1,0:T(8,128)(2,1)S(1)} %get-tuple-element.74), channel_id=1, source_target_pairs={{0,32},{1,33},{2,34},{3,35},{4,36},{5,37},{6,38},{7,39},{8,40},{9,... | collective-permute-start | bytes 208904 | tf_op jit(solution)/shard_map/ppermute | solution.py:54
  39.3 6.4 %collective-permute-start.11 = (bf16[272,128]{1,0:T(8,128)(2,1)S(1)}, bf16[272,128]{1,0:T(8,128)(2,1)S(1)}, u32[]{:S(2)}, u32[]{:S(2)}) collective-permute-start(bf16[272,128]{1,0:T(8,128)(2,1)S(1)} %get-tuple-element.75), channel_id=1, source_target_pairs={{0,64},{1,65},{2,66},{3,67},{4,68},{5,69},{6,70},{7,71},{8,72},{9,... | collective-permute-start | bytes 208904 | tf_op jit(solution)/shard_map/ppermute | solution.py:54
  42.1 4.3 %collective-permute-start.12 = (bf16[272,128]{1,0:T(8,128)(2,1)S(1)}, bf16[272,128]{1,0:T(8,128)(2,1)S(1)}, u32[]{:S(2)}, u32[]{:S(2)}) collective-permute-start(bf16[272,128]{1,0:T(8,128)(2,1)S(1)} %get-tuple-element.76), channel_id=1, source_target_pairs={{0,96},{1,97},{2,98},{3,99},{4,100},{5,101},{6,102},{7,103},{8,104... | collective-permute-start | bytes 208904 | tf_op jit(solution)/shard_map/ppermute | solution.py:54
  46.5 1.6 %collective-permute-start.13 = (bf16[512,128]{1,0:T(8,128)(2,1)S(1)}, bf16[512,128]{1,0:T(8,128)(2,1)S(1)}, u32[]{:S(2)}, u32[]{:S(2)}) collective-permute-start(bf16[512,128]{1,0:T(8,128)(2,1)S(1)} %get-tuple-element.80), channel_id=1, source_target_pairs={{0,16},{1,17},{2,18},{3,19},{4,20},{5,21},{6,22},{7,23},{8,24},{9,... | collective-permute-start | bytes 393224 | tf_op jit(solution)/shard_map/ppermute | solution.py:54
  51.3 9.1 %collective-permute-start.16 = (bf16[64,3072]{1,0:T(8,128)(2,1)S(1)}, bf16[64,3072]{1,0:T(8,128)(2,1)S(1)}, u32[]{:S(2)}, u32[]{:S(2)}) collective-permute-start(bf16[64,3072]{1,0:T(8,128)(2,1)S(1)} %get-tuple-element.89), channel_id=1, source_target_pairs={{0,4},{1,5},{2,6},{3,7},{4,8},{5,9},{6,10},{7,11},{8,12},{9,13},{1... | collective-permute-start | bytes 1179656 | tf_op jit(solution)/shard_map/ppermute | solution.py:54
  54.0 8.6 %collective-permute-start.15 = (bf16[64,3072]{1,0:T(8,128)(2,1)S(1)}, bf16[64,3072]{1,0:T(8,128)(2,1)S(1)}, u32[]{:S(2)}, u32[]{:S(2)}) collective-permute-start(bf16[64,3072]{1,0:T(8,128)(2,1)S(1)} %get-tuple-element.87), channel_id=1, source_target_pairs={{0,12},{1,13},{2,14},{3,15},{4,0},{5,1},{6,2},{7,3},{8,4},{9,5},{1... | collective-permute-start | bytes 1179656 | tf_op jit(solution)/shard_map/ppermute | solution.py:54
  57.3 9.5 %collective-permute-start.18 = (bf16[64,3072]{1,0:T(8,128)(2,1)S(1)}, bf16[64,3072]{1,0:T(8,128)(2,1)S(1)}, u32[]{:S(2)}, u32[]{:S(2)}) collective-permute-start(bf16[64,3072]{1,0:T(8,128)(2,1)S(1)} %get-tuple-element.90), channel_id=1, source_target_pairs={{0,12},{1,13},{2,14},{3,15},{4,0},{5,1},{6,2},{7,3},{8,4},{9,5},{1... | collective-permute-start | bytes 1179656 | tf_op jit(solution)/shard_map/ppermute | solution.py:54
  57.4 13.3 %collective-permute-start.14 = (bf16[64,3072]{1,0:T(8,128)(2,1)S(1)}, bf16[64,3072]{1,0:T(8,128)(2,1)S(1)}, u32[]{:S(2)}, u32[]{:S(2)}) collective-permute-start(bf16[64,3072]{1,0:T(8,128)(2,1)S(1)} %get-tuple-element.85), channel_id=1, source_target_pairs={{0,4},{1,5},{2,6},{3,7},{4,8},{5,9},{6,10},{7,11},{8,12},{9,13},{1... | collective-permute-start | bytes 1179656 | tf_op jit(solution)/shard_map/ppermute | solution.py:54
  60.4 10.2 %collective-permute-start.19 = (bf16[64,3072]{1,0:T(8,128)(2,1)S(1)}, bf16[64,3072]{1,0:T(8,128)(2,1)S(1)}, u32[]{:S(2)}, u32[]{:S(2)}) collective-permute-start(bf16[64,3072]{1,0:T(8,128)(2,1)S(1)} %relay.2.refs_0_), channel_id=1, source_target_pairs={{0,4},{1,5},{2,6},{3,7},{4,8},{5,9},{6,10},{7,11},{8,12},{9,13},{1... | collective-permute-start | bytes 1179656 | tf_op jit(solution)/shard_map/ppermute | solution.py:54
  62.7 9.1 %collective-permute-start.17 = (bf16[64,3072]{1,0:T(8,128)(2,1)S(1)}, bf16[64,3072]{1,0:T(8,128)(2,1)S(1)}, u32[]{:S(2)}, u32[]{:S(2)}) collective-permute-start(bf16[64,3072]{1,0:T(8,128)(2,1)S(1)} %relay.3), channel_id=1, source_target_pairs={{0,12},{1,13},{2,14},{3,15},{4,0},{5,1},{6,2},{7,3},{8,4},{9,5},{1... | collective-permute-start | bytes 1179656 | tf_op jit(solution)/shard_map/ppermute | solution.py:54
  71.9 6.9 %collective-permute-start.20 = (bf16[16,6144]{1,0:T(8,128)(2,1)S(1)}, bf16[16,6144]{1,0:T(8,128)(2,1)S(1)}, u32[]{:S(2)}, u32[]{:S(2)}) collective-permute-start(bf16[16,6144]{1,0:T(8,128)(2,1)S(1)} %get-tuple-element.96), channel_id=1, source_target_pairs={{0,1},{1,2},{2,3},{3,0},{4,5},{5,6},{6,7},{7,4},{8,9},{9,10},{10,1... | collective-permute-start | bytes 589832 | tf_op jit(solution)/shard_map/ppermute | solution.py:54
  72.0 8.5 %collective-permute-start.21 = (bf16[16,6144]{1,0:T(8,128)(2,1)S(1)}, bf16[16,6144]{1,0:T(8,128)(2,1)S(1)}, u32[]{:S(2)}, u32[]{:S(2)}) collective-permute-start(bf16[16,6144]{1,0:T(8,128)(2,1)S(1)} %get-tuple-element.97), channel_id=1, source_target_pairs={{0,3},{1,0},{2,1},{3,2},{4,7},{5,4},{6,5},{7,6},{8,11},{9,8},{10,9... | collective-permute-start | bytes 589832 | tf_op jit(solution)/shard_map/ppermute | solution.py:54
  75.2 7.2 %collective-permute-start.22 = (bf16[16,6144]{1,0:T(8,128)(2,1)S(1)}, bf16[16,6144]{1,0:T(8,128)(2,1)S(1)}, u32[]{:S(2)}, u32[]{:S(2)}) collective-permute-start(bf16[16,6144]{1,0:T(8,128)(2,1)S(1)} %get-tuple-element.98), channel_id=1, source_target_pairs={{0,2},{1,3},{2,0},{3,1},{4,6},{5,7},{6,4},{7,5},{8,10},{9,11},{10,... | collective-permute-start | bytes 589832 | tf_op jit(solution)/shard_map/ppermute | solution.py:54

commit v4 on v3

--- a/solution.py
+++ b/solution.py
@@ -379,44 +379,77 @@
     )(own_l, own_m, lead, peer, *far, *after)
 
 
-def inter_kernel(
-    q_ref, k_ref, v_ref, g_ref, lead_ref, tail_ref, mine_ref, theirs_ref, dq_ref, dk_ref, dv_ref,
-    out_ref, whole_ref,
-):
-    columns = q_ref.shape[1]
-    first = place()[1] == 0
-    half = columns // DH // 2
-    for h in range(columns // DH):
-        c = slice(h * DH, (h + 1) * DH)
-        own = first if h < half else jnp.logical_not(first)
-        state, grad = (
-            jnp.where(own, mine_ref[at : at + DH, :], theirs_ref[at : at + DH, :])
-            for at in (h % half * DH, (half + h % half) * DH)
-        )
-        k, v, g = k_ref[:, c], v_ref[:, c], g_ref[:, c]
-        lead, tail = lead_ref[:, c], tail_ref[:, c]
-        dq = dq_ref[:, c] + lead * nt(g, state)
-        dk = dk_ref[:, c] + tail * nt(v, grad)
-        dv = dv_ref[:, c] + tail * nn(k, grad)
-        for n, result in enumerate((dq, dk, dv)):
-            whole_ref[:, pl.ds(n * columns + h * DH, DH)] = result.astype(BF16)
+def columns_of(core, columns, i):
+    return pl.ds(pl.multiple_of(core * (columns // 2) + i * DH, DH), DH)
+
+
+def inter_terms(refs, states_ref, c, i):
+    k_ref, v_ref, g_ref, lead_ref, tail_ref, dq_ref, dk_ref, dv_ref = refs
+    half = states_ref.shape[0] // 2
+    state = states_ref[i * DH : (i + 1) * DH, :]
+    grad = states_ref[half + i * DH : half + (i + 1) * DH, :]
+    lead, tail = lead_ref[:, c], tail_ref[:, c]
+    return (
+        (dq_ref[:, c] + lead * nt(g_ref[:, c], state)).astype(BF16),
+        (dk_ref[:, c] + tail * nt(v_ref[:, c], grad)).astype(BF16),
+        (dv_ref[:, c] + tail * nn(k_ref[:, c], grad)).astype(BF16),
+    )
+
+
+def inter_own_kernel(*refs):
+    refs, states_ref, out_ref = refs[:8], refs[8], refs[9]
+    columns = refs[0].shape[1]
+    core = place()[1]
+    for i in range(columns // DH // 2):
+        results = inter_terms(refs, states_ref, columns_of(core, columns, i), i)
+        for n, result in enumerate(results):
+            at = n * (columns // 2) + i * DH
+            out_ref[:, at : at + DH] = result
+
+
+def inter_kernel(*refs):
+    refs, states_ref, own_ref, out_ref, whole_ref = refs[:8], refs[8], refs[9], refs[10], refs[11]
+    columns = refs[0].shape[1]
+    core = place()[1]
+    for i in range(columns // DH // 2):
+        results = inter_terms(refs, states_ref, columns_of(1 - core, columns, i), i)
+        for n, result in enumerate(results):
+            at = pl.multiple_of(n * columns + (1 - core) * (columns // 2) + i * DH, DH)
+            whole_ref[:, pl.ds(at, DH)] = result
+    for n in range(3):
+        at = pl.multiple_of(n * columns + core * (columns // 2), DH)
+        own = slice(n * (columns // 2), (n + 1) * (columns // 2))
+        whole_ref[:, pl.ds(at, columns // 2)] = own_ref[:, own]
     for n in range(SIDE * SIDE):
         start = pl.multiple_of(member(n // SIDE, n % SIDE) * 16, 16)
         out_ref[pl.ds(n * 16, 16), :] = whole_ref[pl.ds(start, 16), :]
 
 
-def inter(q, k, v, g, lead, tail, mine, theirs, within):
-    rows, columns = q.shape
+def inter_own(k, v, g, lead, tail, within, states):
+    rows, columns = k.shape
+    return pl.pallas_call(
+        inter_own_kernel,
+        out_shape=pltpu.VMEM((rows, 3 * columns // 2), BF16),
+        in_specs=[VMEM] * 9,
+        out_specs=VMEM,
+        compiler_params=params(8),
+        cost_estimate=cost(75_000_000, 3_000_000),
+        name="inter_own",
+    )(k, v, g, lead, tail, *within, states)
+
+
+def inter(k, v, g, lead, tail, within, states, own):
+    rows, columns = k.shape
     return pl.pallas_call(
         inter_kernel,
         out_shape=pltpu.VMEM((rows, 3 * columns), BF16),
-        in_specs=[VMEM] * 11,
+        in_specs=[VMEM] * 10,
         out_specs=VMEM,
         scratch_shapes=[pltpu.VMEM((rows, 3 * columns), BF16)],
         compiler_params=params(8),
-        cost_estimate=cost(150_000_000, 6_000_000),
+        cost_estimate=cost(75_000_000, 4_000_000),
         name="inter",
-    )(q, k, v, g, lead, tail, mine, theirs, *within)
+    )(k, v, g, lead, tail, *within, states, own)
 
 
 def output_kernel(start, tile, d_ref, wq_ref, wk_ref, wv_ref, *refs):
@@ -545,7 +578,8 @@
     within = intra(q, k, v, g, factors)
     mine, theirs = outer_states(own_l, own_m, lead, peer, far, within[:1])
     theirs = move(theirs, core_perm())
-    d = inter(q, k, v, g, lead, tail, mine, theirs, within)
+    ready = inter_own(k, v, g, lead, tail, within, mine)
+    d = inter(k, v, g, lead, tail, within, theirs, ready)
 
     width = w_query.shape[0] // HALVES
     a_own, a_next, a_last, a_far = output(d, weights, 0, width, (F32, F32, BF16, BF16))

time: 83.2 us -> 83.1 us (level)
  no operation moved by 1% of the time
where the time goes in v4:
time: 83.1 us; the launch traced here: 83 us
  starting transfers between devices  34.9 us (42%)
  waiting for transfers between devices  26.8 us (32%)
  Pallas kernels  21 us (25%)
    ppermute x23, starting transfers between devices, move(): return lax.ppermute(array, AXES, pairs)  34.9 us
    ppermute x23, waiting for transfers between devices, move(): return lax.ppermute(array, AXES, pairs)  26.8 us
    pallas_call x4, Pallas kernels, project(): pl.pallas_call(functools.partial(project_kernel, slots, has_sum), out_sha...  5.54 us
    pallas_call x2, Pallas kernels, output(): pl.pallas_call(functools.partial(output_kernel, start, 512), out_shape=tu...  5.26 us
    pallas_call x1, Pallas kernels, load(): pl.pallas_call(load_kernel, out_shape=tuple((pltpu.VMEM(a.shape, a.dtype)...  4.84 us
  transfers between devices with their start and end apart: 23, of which 16 were waited for; matrix products, arithmetic and copies ran while one was open for 0% of the time, Pallas kernels for 18%

profile of v4, /device:TPU:0, one launch (start us, length us, event | category | flops | bytes accessed | tf_op | source)
XLA Modules:
  0.0 83.0 jit_solution(4245234939439309020)
XLA Ops:
  0.0 3.1 %collective-permute-start = (bf16[256,384]{1,0:T(8,128)(2,1)}, bf16[256,384]{1,0:T(8,128)(2,1)S(1)}, u32[]{:S(2)}, u32[]{:S(2)}) collective-permute-start(bf16[256,384]{1,0:T(8,128)(2,1)} %refs_0_.1), channel_id=1, source_target_pairs={{0,3},{1,0},{2,1},{3,2},{4,7},{5,4},{6,5},{7,6},{8,11},{9,8},{10,9... | collective-permute-start | bytes 589832 | tf_op jit(solution)/shard_map/ppermute | solution.py:54
  3.1 0.0 collective-permute-start.1
  3.1 2.2 %collective-permute-start.2 = (bf16[256,384]{1,0:T(8,128)(2,1)}, bf16[256,384]{1,0:T(8,128)(2,1)S(1)}, u32[]{:S(2)}, u32[]{:S(2)}) collective-permute-start(bf16[256,384]{1,0:T(8,128)(2,1)} %refs_0_.1), channel_id=1, source_target_pairs={{0,2},{1,3},{2,0},{3,1},{4,6},{5,7},{6,4},{7,5},{8,10},{9,11},{10,... | collective-permute-start | bytes 589832 | tf_op jit(solution)/shard_map/ppermute | solution.py:54
  5.3 4.8 %load.1 = (bf16[256,384]{1,0:T(8,128)(2,1)S(1)}, bf16[6144,512]{1,0:T(8,128)(2,1)S(1)}, bf16[6144,512]{1,0:T(8,128)(2,1)S(1)}) custom-call(bf16[256,384]{1,0:T(8,128)(2,1)} %refs_0_.1, bf16[6144,512]{1,0:T(8,128)(2,1)} %refs_1_.1, bf16[6144,512]{1,0:T(8,128)(2,1)} %refs_2_.3), custom_call_target="tpu_custom_call" | custom-call | bytes 25559040 | tf_op jit(solution)/shard_map/load/pallas_call | solution.py:147
  10.2 0.0 copy-start.2
  10.2 0.0 copy-start
  10.2 0.0 collective-permute-done.refs_1_
  10.2 2.1 %collective-permute-done.1.refs_2_ = bf16[256,384]{1,0:T(8,128)(2,1)S(1)} collective-permute-done((bf16[256,384]{1,0:T(8,128)(2,1)}, bf16[256,384]{1,0:T(8,128)(2,1)S(1)}, u32[]{:S(2)}, u32[]{:S(2)}) %collective-permute-start.1) | collective-permute-done | bytes 196640 | tf_op jit(solution)/shard_map/ppermute | solution.py:54
  12.3 0.0 collective-permute-done.2.refs_3_
  12.3 0.1 join.1
  12.4 4.1 %collective-permute-start.3 = (bf16[128,1536]{1,0:T(8,128)(2,1)S(1)}, bf16[128,1536]{1,0:T(8,128)(2,1)S(1)}, u32[]{:S(2)}, u32[]{:S(2)}) collective-permute-start(bf16[128,1536]{1,0:T(8,128)(2,1)S(1)} %get-tuple-element.54.refs_0_), channel_id=1, source_target_pairs={{0,12},{1,13},{2,14},{3,15},{4,0},{5,1},{6,2},{7,3},{8,4},{9,5},{1... | collective-permute-start | bytes 1179656 | tf_op jit(solution)/shard_map/ppermute | solution.py:54
  16.5 3.2 %collective-permute-start.8 = (bf16[128,1536]{1,0:T(8,128)(2,1)S(1)}, bf16[128,1536]{1,0:T(8,128)(2,1)S(1)}, u32[]{:S(2)}, u32[]{:S(2)}) collective-permute-start(bf16[128,1536]{1,0:T(8,128)(2,1)S(1)} %get-tuple-element.55.refs_1_), channel_id=1, source_target_pairs={{0,12},{1,13},{2,14},{3,15},{4,0},{5,1},{6,2},{7,3},{8,4},{9,5},{1... | collective-permute-start | bytes 1179656 | tf_op jit(solution)/shard_map/ppermute | solution.py:54
  19.7 0.0 collective-permute-start.7
  19.7 2.1 %collective-permute-done.3.refs_0_ = bf16[128,1536]{1,0:T(8,128)(2,1)S(1)} collective-permute-done((bf16[128,1536]{1,0:T(8,128)(2,1)S(1)}, bf16[128,1536]{1,0:T(8,128)(2,1)S(1)}, u32[]{:S(2)}, u32[]{:S(2)}) %collective-permute-start.3) | collective-permute-done | bytes 393248 | tf_op jit(solution)/shard_map/ppermute | solution.py:54
  21.8 3.7 %collective-permute-start.4 = (bf16[128,1536]{1,0:T(8,128)(2,1)S(1)}, bf16[128,1536]{1,0:T(8,128)(2,1)S(1)}, u32[]{:S(2)}, u32[]{:S(2)}) collective-permute-start(bf16[128,1536]{1,0:T(8,128)(2,1)S(1)} %collective-permute-done.3.refs_0_), channel_id=1, source_target_pairs={{0,12},{1,13},{2,14},{3,15},{4,0},{5,1},{6,2},{7,3},{8,4},{9,5},{1... | collective-permute-start | bytes 1179656 | tf_op jit(solution)/shard_map/ppermute | solution.py:54
  25.5 0.0 collective-permute-start.6
  25.5 1.3 %decay.1 = (f32[4,256,256]{2,1,0:T(8,128)S(1)}, f32[256,512]{1,0:T(8,128)S(1)}, f32[256,512]{1,0:T(8,128)S(1)}) custom-call(f32[4,256]{1,0:T(4,128)S(1)} %copy-done.2), custom_call_target="tpu_custom_call" | custom-call | flops 2000000 | bytes 2000000 | tf_op jit(solution)/shard_map/decay/pallas_call | solution.py:116
  26.8 1.4 %project.4 = (f32[256,512]{1,0:T(8,128)S(1)}, f32[256,512]{1,0:T(8,128)S(1)}, f32[256,512]{1,0:T(8,128)S(1)}) custom-call(bf16[128,1536]{1,0:T(8,128)(2,1)S(1)} %get-tuple-element.54.refs_0_, bf16[128,1536]{1,0:T(8,128)(2,1)S(1)} %get-tuple-element.55.refs_1_, bf16[6144,512]{1,0:T(8,128)(2,1)S(1)} %get-tuple-element.53.refs_4_.refs_2_.refs_5_.wq_ref, ...), custom_call_target="tpu_custom_call" | custom-call | flops 1207959552 | bytes 6144000 | tf_op jit(solution)/shard_map/project/pallas_call | solution.py:202
  28.2 0.0 collective-permute-done.8.refs_1_
  28.2 1.4 %project.5 = (f32[256,512]{1,0:T(8,128)S(1)}, f32[256,512]{1,0:T(8,128)S(1)}, f32[256,512]{1,0:T(8,128)S(1)}) custom-call(bf16[128,1536]{1,0:T(8,128)(2,1)S(1)} %collective-permute-done.3.refs_0_, bf16[128,1536]{1,0:T(8,128)(2,1)S(1)} %collective-permute-done.8.refs_1_, f32[256,512]{1,0:T(8,128)S(1)} %get-tuple-element.58.refs_2_, ...), custom_call_target="tpu_custom_call" | custom-call | flops 1207959552 | bytes 6144000 | tf_op jit(solution)/shard_map/project/pallas_call | solution.py:202
  29.6 0.1 collective-permute-done.7.refs_0_
  29.7 1.4 %project.6 = (f32[256,512]{1,0:T(8,128)S(1)}, f32[256,512]{1,0:T(8,128)S(1)}, f32[256,512]{1,0:T(8,128)S(1)}) custom-call(bf16[128,1536]{1,0:T(8,128)(2,1)S(1)} %collective-permute-done.7.refs_0_, bf16[128,1536]{1,0:T(8,128)(2,1)S(1)} %collective-permute-done.5.refs_1_, f32[256,512]{1,0:T(8,128)S(1)} %get-tuple-element.61.refs_2_, ...), custom_call_target="tpu_custom_call" | custom-call | flops 1207959552 | bytes 6144000 | tf_op jit(solution)/shard_map/project/pallas_call | solution.py:202
  31.1 3.4 %collective-permute-done.6.refs_1_ = bf16[128,1536]{1,0:T(8,128)(2,1)S(1)} collective-permute-done((bf16[128,1536]{1,0:T(8,128)(2,1)S(1)}, bf16[128,1536]{1,0:T(8,128)(2,1)S(1)}, u32[]{:S(2)}, u32[]{:S(2)}) %collective-permute-start.6) | collective-permute-done | bytes 393248 | tf_op jit(solution)/shard_map/ppermute | solution.py:54
  34.5 1.4 %project.7 = (bf16[256,512]{1,0:T(8,128)(2,1)S(1)}, bf16[256,512]{1,0:T(8,128)(2,1)S(1)}, bf16[256,512]{1,0:T(8,128)(2,1)S(1)}) custom-call(bf16[128,1536]{1,0:T(8,128)(2,1)S(1)} %collective-permute-done.4.refs_0_, bf16[128,1536]{1,0:T(8,128)(2,1)S(1)} %collective-permute-done.6.refs_1_, f32[256,512]{1,0:T(8,128)S(1)} %get-tuple-element.64.refs_2_, ...), custom_call_target="tpu_custom_call" | custom-call | flops 1207959552 | bytes 6144000 | tf_op jit(solution)/shard_map/project/pallas_call | solution.py:202
  35.9 0.4 states.1
  36.3 0.1 collective-permute-start.9
  36.3 1.3 %collective-permute-done.9.peer_ref = bf16[528,128]{1,0:T(8,128)(2,1)S(1)} collective-permute-done((bf16[528,128]{1,0:T(8,128)(2,1)S(1)}, bf16[528,128]{1,0:T(8,128)(2,1)S(1)}, u32[]{:S(2)}, u32[]{:S(2)}) %collective-permute-start.9) | collective-permute-done | bytes 135200 | tf_op jit(solution)/shard_map/ppermute | solution.py:54
  37.7 0.1 chip_states.1
  37.8 1.6 %collective-permute-start.10 = (bf16[272,128]{1,0:T(8,128)(2,1)S(1)}, bf16[272,128]{1,0:T(8,128)(2,1)S(1)}, u32[]{:S(2)}, u32[]{:S(2)}) collective-permute-start(bf16[272,128]{1,0:T(8,128)(2,1)S(1)} %get-tuple-element.78), channel_id=1, source_target_pairs={{0,32},{1,33},{2,34},{3,35},{4,36},{5,37},{6,38},{7,39},{8,40},{9,... | collective-permute-start | bytes 208904 | tf_op jit(solution)/shard_map/ppermute | solution.py:54
  39.3 2.7 %collective-permute-start.11 = (bf16[272,128]{1,0:T(8,128)(2,1)S(1)}, bf16[272,128]{1,0:T(8,128)(2,1)S(1)}, u32[]{:S(2)}, u32[]{:S(2)}) collective-permute-start(bf16[272,128]{1,0:T(8,128)(2,1)S(1)} %get-tuple-element.79), channel_id=1, source_target_pairs={{0,64},{1,65},{2,66},{3,67},{4,68},{5,69},{6,70},{7,71},{8,72},{9,... | collective-permute-start | bytes 208904 | tf_op jit(solution)/shard_map/ppermute | solution.py:54
  42.1 1.4 %collective-permute-start.12 = (bf16[272,128]{1,0:T(8,128)(2,1)S(1)}, bf16[272,128]{1,0:T(8,128)(2,1)S(1)}, u32[]{:S(2)}, u32[]{:S(2)}) collective-permute-start(bf16[272,128]{1,0:T(8,128)(2,1)S(1)} %get-tuple-element.80), channel_id=1, source_target_pairs={{0,96},{1,97},{2,98},{3,99},{4,100},{5,101},{6,102},{7,103},{8,104... | collective-permute-start | bytes 208904 | tf_op jit(solution)/shard_map/ppermute | solution.py:54
  43.5 1.5 %intra.1 = (f32[256,512]{1,0:T(8,128)S(1)}, f32[256,512]{1,0:T(8,128)S(1)}, f32[256,512]{1,0:T(8,128)S(1)}) custom-call(bf16[256,512]{1,0:T(8,128)(2,1)S(1)} %get-tuple-element.70.q_ref, bf16[256,512]{1,0:T(8,128)(2,1)S(1)} %get-tuple-element.67.k_ref.refs_0_, bf16[256,512]{1,0:T(8,128)(2,1)S(1)} %get-tuple-element.68.v_ref.refs_1_, ...), custom_call_target="tpu_custom_call" | custom-call | flops 340000000 | bytes 4000000 | tf_op jit(solution)/shard_map/intra/pallas_call | solution.py:276
  45.0 0.7 collective-permute-done.11.two_ref
  45.8 0.6 collective-permute-done.12.three_ref
  46.4 0.1 outer_states.1
  46.5 0.3 collective-permute-start.13
  46.8 0.3 inter_own.1.refs_9_
  47.1 1.0 %collective-permute-done.13.refs_8_ = bf16[512,128]{1,0:T(8,128)(2,1)S(1)} collective-permute-done((bf16[512,128]{1,0:T(8,128)(2,1)S(1)}, bf16[512,128]{1,0:T(8,128)(2,1)S(1)}, u32[]{:S(2)}, u32[]{:S(2)}) %collective-permute-start.13) | collective-permute-done | bytes 131104 | tf_op jit(solution)/shard_map/ppermute | solution.py:54
  48.1 0.4 inter.1.d_ref
  48.6 2.6 %output.2 = (f32[64,3072]{1,0:T(8,128)S(1)}, f32[64,3072]{1,0:T(8,128)S(1)}, bf16[64,3072]{1,0:T(8,128)(2,1)S(1)}, bf16[64,3072]{1,0:T(8,128)(2,1)S(1)}) custom-call(bf16[256,1536]{1,0:T(8,128)(2,1)S(1)} %inter.1.d_ref, bf16[6144,512]{1,0:T(8,128)(2,1)S(1)} %get-tuple-element.53.refs_4_.refs_2_.refs_5_.wq_ref, ...), custom_call_target="tpu_custom_call" | custom-call | flops 2415919104 | bytes 6000000 | tf_op jit(solution)/shard_map/output/pallas_call | solution.py:474
  51.2 0.1 collective-permute-start.16
  51.3 2.6 %output.3 = (f32[64,3072]{1,0:T(8,128)S(1)}, bf16[64,3072]{1,0:T(8,128)(2,1)S(1)}, f32[64,3072]{1,0:T(8,128)S(1)}, bf16[64,3072]{1,0:T(8,128)(2,1)S(1)}) custom-call(bf16[256,1536]{1,0:T(8,128)(2,1)S(1)} %inter.1.d_ref, bf16[6144,512]{1,0:T(8,128)(2,1)S(1)} %get-tuple-element.53.refs_4_.refs_2_.refs_5_.wq_ref, ...), custom_call_target="tpu_custom_call" | custom-call | flops 2415919104 | bytes 6000000 | tf_op jit(solution)/shard_map/output/pallas_call | solution.py:474
  53.9 3.3 %collective-permute-start.15 = (bf16[64,3072]{1,0:T(8,128)(2,1)S(1)}, bf16[64,3072]{1,0:T(8,128)(2,1)S(1)}, u32[]{:S(2)}, u32[]{:S(2)}) collective-permute-start(bf16[64,3072]{1,0:T(8,128)(2,1)S(1)} %get-tuple-element.87), channel_id=1, source_target_pairs={{0,12},{1,13},{2,14},{3,15},{4,0},{5,1},{6,2},{7,3},{8,4},{9,5},{1... | collective-permute-start | bytes 1179656 | tf_op jit(solution)/shard_map/ppermute | solution.py:54
  57.2 0.1 collective-permute-start.18
  57.3 1.9 %collective-permute-start.14 = (bf16[64,3072]{1,0:T(8,128)(2,1)S(1)}, bf16[64,3072]{1,0:T(8,128)(2,1)S(1)}, u32[]{:S(2)}, u32[]{:S(2)}) collective-permute-start(bf16[64,3072]{1,0:T(8,128)(2,1)S(1)} %get-tuple-element.85), channel_id=1, source_target_pairs={{0,4},{1,5},{2,6},{3,7},{4,8},{5,9},{6,10},{7,11},{8,12},{9,13},{1... | collective-permute-start | bytes 1179656 | tf_op jit(solution)/shard_map/ppermute | solution.py:54
  59.2 1.0 %collective-permute-done.16.other_ref = bf16[64,3072]{1,0:T(8,128)(2,1)S(1)} collective-permute-done((bf16[64,3072]{1,0:T(8,128)(2,1)S(1)}, bf16[64,3072]{1,0:T(8,128)(2,1)S(1)}, u32[]{:S(2)}, u32[]{:S(2)}) %collective-permute-start.16) | collective-permute-done | bytes 393248 | tf_op jit(solution)/shard_map/ppermute | solution.py:54
  60.3 0.1 relay.2.refs_0_
  60.3 0.1 collective-permute-start.19
  60.4 2.1 %collective-permute-done.15.other_ref = bf16[64,3072]{1,0:T(8,128)(2,1)S(1)} collective-permute-done((bf16[64,3072]{1,0:T(8,128)(2,1)S(1)}, bf16[64,3072]{1,0:T(8,128)(2,1)S(1)}, u32[]{:S(2)}, u32[]{:S(2)}) %collective-permute-start.15) | collective-permute-done | bytes 393248 | tf_op jit(solution)/shard_map/ppermute | solution.py:54
  62.5 0.1 relay.3
  62.6 3.8 %collective-permute-start.17 = (bf16[64,3072]{1,0:T(8,128)(2,1)S(1)}, bf16[64,3072]{1,0:T(8,128)(2,1)S(1)}, u32[]{:S(2)}, u32[]{:S(2)}) collective-permute-start(bf16[64,3072]{1,0:T(8,128)(2,1)S(1)} %relay.3), channel_id=1, source_target_pairs={{0,12},{1,13},{2,14},{3,15},{4,0},{5,1},{6,2},{7,3},{8,4},{9,5},{1... | collective-permute-start | bytes 1179656 | tf_op jit(solution)/shard_map/ppermute | solution.py:54
  66.3 0.4 collective-permute-done.18.refs_1_
  66.7 3.8 %collective-permute-done.19.refs_2_ = bf16[64,3072]{1,0:T(8,128)(2,1)S(1)} collective-permute-done((bf16[64,3072]{1,0:T(8,128)(2,1)S(1)}, bf16[64,3072]{1,0:T(8,128)(2,1)S(1)}, u32[]{:S(2)}, u32[]{:S(2)}) %collective-permute-start.19) | collective-permute-done | bytes 393248 | tf_op jit(solution)/shard_map/ppermute | solution.py:54
  70.5 0.1 add.2
  70.6 0.0 collective-permute-done.14.refs_1_
  70.6 1.0 %collective-permute-done.17.refs_2_ = bf16[64,3072]{1,0:T(8,128)(2,1)S(1)} collective-permute-done((bf16[64,3072]{1,0:T(8,128)(2,1)S(1)}, bf16[64,3072]{1,0:T(8,128)(2,1)S(1)}, u32[]{:S(2)}, u32[]{:S(2)}) %collective-permute-start.17) | collective-permute-done | bytes 393248 | tf_op jit(solution)/shard_map/ppermute | solution.py:54
  71.6 0.1 add.3
  71.8 0.1 collective-permute-start.20
  71.8 3.2 %collective-permute-start.21 = (bf16[16,6144]{1,0:T(8,128)(2,1)S(1)}, bf16[16,6144]{1,0:T(8,128)(2,1)S(1)}, u32[]{:S(2)}, u32[]{:S(2)}) collective-permute-start(bf16[16,6144]{1,0:T(8,128)(2,1)S(1)} %get-tuple-element.97), channel_id=1, source_target_pairs={{0,3},{1,0},{2,1},{3,2},{4,7},{5,4},{6,5},{7,6},{8,11},{9,8},{10,9... | collective-permute-start | bytes 589832 | tf_op jit(solution)/shard_map/ppermute | solution.py:54
  75.1 0.0 collective-permute-start.22
  75.1 3.6 %collective-permute-done.20.a_ref = bf16[16,6144]{1,0:T(8,128)(2,1)S(1)} collective-permute-done((bf16[16,6144]{1,0:T(8,128)(2,1)S(1)}, bf16[16,6144]{1,0:T(8,128)(2,1)S(1)}, u32[]{:S(2)}, u32[]{:S(2)}) %collective-permute-start.20) | collective-permute-done | bytes 196640 | tf_op jit(solution)/shard_map/ppermute | solution.py:54
  78.7 1.7 %collective-permute-done.21.b_ref = bf16[16,6144]{1,0:T(8,128)(2,1)S(1)} collective-permute-done((bf16[16,6144]{1,0:T(8,128)(2,1)S(1)}, bf16[16,6144]{1,0:T(8,128)(2,1)S(1)}, u32[]{:S(2)}, u32[]{:S(2)}) %collective-permute-start.21) | collective-permute-done | bytes 196640 | tf_op jit(solution)/shard_map/ppermute | solution.py:54
  80.4 1.9 %collective-permute-done.22.c_ref = bf16[16,6144]{1,0:T(8,128)(2,1)S(1)} collective-permute-done((bf16[16,6144]{1,0:T(8,128)(2,1)S(1)}, bf16[16,6144]{1,0:T(8,128)(2,1)S(1)}, u32[]{:S(2)}, u32[]{:S(2)}) %collective-permute-start.22) | collective-permute-done | bytes 196640 | tf_op jit(solution)/shard_map/ppermute | solution.py:54
  82.2 0.8 finish.1
  (8 shorter events, 0.0 us)
Async XLA Ops:
  0.0 10.2 %collective-permute-start = (bf16[256,384]{1,0:T(8,128)(2,1)}, bf16[256,384]{1,0:T(8,128)(2,1)S(1)}, u32[]{:S(2)}, u32[]{:S(2)}) collective-permute-start(bf16[256,384]{1,0:T(8,128)(2,1)} %refs_0_.1), channel_id=1, source_target_pairs={{0,3},{1,0},{2,1},{3,2},{4,7},{5,4},{6,5},{7,6},{8,11},{9,8},{10,9... | collective-permute-start | bytes 589832 | tf_op jit(solution)/shard_map/ppermute | solution.py:54
  3.1 9.2 %collective-permute-start.1 = (bf16[256,384]{1,0:T(8,128)(2,1)}, bf16[256,384]{1,0:T(8,128)(2,1)S(1)}, u32[]{:S(2)}, u32[]{:S(2)}) collective-permute-start(bf16[256,384]{1,0:T(8,128)(2,1)} %refs_0_.1), channel_id=1, source_target_pairs={{0,1},{1,2},{2,3},{3,0},{4,5},{5,6},{6,7},{7,4},{8,9},{9,10},{10,1... | collective-permute-start | bytes 589832 | tf_op jit(solution)/shard_map/ppermute | solution.py:54
  3.1 9.2 %collective-permute-start.2 = (bf16[256,384]{1,0:T(8,128)(2,1)}, bf16[256,384]{1,0:T(8,128)(2,1)S(1)}, u32[]{:S(2)}, u32[]{:S(2)}) collective-permute-start(bf16[256,384]{1,0:T(8,128)(2,1)} %refs_0_.1), channel_id=1, source_target_pairs={{0,2},{1,3},{2,0},{3,1},{4,6},{5,7},{6,4},{7,5},{8,10},{9,11},{10,... | collective-permute-start | bytes 589832 | tf_op jit(solution)/shard_map/ppermute | solution.py:54
  10.2 15.3 %copy-start.2 = (f32[4,256]{1,0:T(4,128)S(1)}, f32[4,256]{1,0:T(4,128)}, u32[]{:S(2)}) copy-start(f32[4,256]{1,0:T(4,128)} %decay_ref.1) | copy-start | bytes 12292
  10.2 16.6 %copy-start = (bf16[6144,512]{1,0:T(8,128)(2,1)S(1)}, bf16[6144,512]{1,0:T(8,128)(2,1)}, u32[]{:S(2)}) copy-start(bf16[6144,512]{1,0:T(8,128)(2,1)} %wv_ref.3) | copy-start | bytes 18874372
  12.4 9.4 %collective-permute-start.3 = (bf16[128,1536]{1,0:T(8,128)(2,1)S(1)}, bf16[128,1536]{1,0:T(8,128)(2,1)S(1)}, u32[]{:S(2)}, u32[]{:S(2)}) collective-permute-start(bf16[128,1536]{1,0:T(8,128)(2,1)S(1)} %get-tuple-element.54.refs_0_), channel_id=1, source_target_pairs={{0,12},{1,13},{2,14},{3,15},{4,0},{5,1},{6,2},{7,3},{8,4},{9,5},{1... | collective-permute-start | bytes 1179656 | tf_op jit(solution)/shard_map/ppermute | solution.py:54
  16.5 9.0 %collective-permute-start.5 = (bf16[128,1536]{1,0:T(8,128)(2,1)S(1)}, bf16[128,1536]{1,0:T(8,128)(2,1)S(1)}, u32[]{:S(2)}, u32[]{:S(2)}) collective-permute-start(bf16[128,1536]{1,0:T(8,128)(2,1)S(1)} %get-tuple-element.55.refs_1_), channel_id=1, source_target_pairs={{0,4},{1,5},{2,6},{3,7},{4,8},{5,9},{6,10},{7,11},{8,12},{9,13},{1... | collective-permute-start | bytes 1179656 | tf_op jit(solution)/shard_map/ppermute | solution.py:54
  16.5 11.7 %collective-permute-start.8 = (bf16[128,1536]{1,0:T(8,128)(2,1)S(1)}, bf16[128,1536]{1,0:T(8,128)(2,1)S(1)}, u32[]{:S(2)}, u32[]{:S(2)}) collective-permute-start(bf16[128,1536]{1,0:T(8,128)(2,1)S(1)} %get-tuple-element.55.refs_1_), channel_id=1, source_target_pairs={{0,12},{1,13},{2,14},{3,15},{4,0},{5,1},{6,2},{7,3},{8,4},{9,5},{1... | collective-permute-start | bytes 1179656 | tf_op jit(solution)/shard_map/ppermute | solution.py:54
  19.7 10.0 %collective-permute-start.7 = (bf16[128,1536]{1,0:T(8,128)(2,1)S(1)}, bf16[128,1536]{1,0:T(8,128)(2,1)S(1)}, u32[]{:S(2)}, u32[]{:S(2)}) collective-permute-start(bf16[128,1536]{1,0:T(8,128)(2,1)S(1)} %get-tuple-element.54.refs_0_), channel_id=1, source_target_pairs={{0,4},{1,5},{2,6},{3,7},{4,8},{5,9},{6,10},{7,11},{8,12},{9,13},{1... | collective-permute-start | bytes 1179656 | tf_op jit(solution)/shard_map/ppermute | solution.py:54
  21.8 9.3 %collective-permute-start.4 = (bf16[128,1536]{1,0:T(8,128)(2,1)S(1)}, bf16[128,1536]{1,0:T(8,128)(2,1)S(1)}, u32[]{:S(2)}, u32[]{:S(2)}) collective-permute-start(bf16[128,1536]{1,0:T(8,128)(2,1)S(1)} %collective-permute-done.3.refs_0_), channel_id=1, source_target_pairs={{0,12},{1,13},{2,14},{3,15},{4,0},{5,1},{6,2},{7,3},{8,4},{9,5},{1... | collective-permute-start | bytes 1179656 | tf_op jit(solution)/shard_map/ppermute | solution.py:54
  25.5 9.0 %collective-permute-start.6 = (bf16[128,1536]{1,0:T(8,128)(2,1)S(1)}, bf16[128,1536]{1,0:T(8,128)(2,1)S(1)}, u32[]{:S(2)}, u32[]{:S(2)}) collective-permute-start(bf16[128,1536]{1,0:T(8,128)(2,1)S(1)} %collective-permute-done.5.refs_1_), channel_id=1, source_target_pairs={{0,4},{1,5},{2,6},{3,7},{4,8},{5,9},{6,10},{7,11},{8,12},{9,13},{1... | collective-permute-start | bytes 1179656 | tf_op jit(solution)/shard_map/ppermute | solution.py:54
  34.5 1.4 %copy-start.1 = (bf16[256,512]{1,0:T(8,128)(2,1)S(1)}, bf16[256,512]{1,0:T(8,128)(2,1)}, u32[]{:S(2)}) copy-start(bf16[256,512]{1,0:T(8,128)(2,1)} %refs_2_.5) | copy-start | bytes 786436
  36.3 1.4 %collective-permute-start.9 = (bf16[528,128]{1,0:T(8,128)(2,1)S(1)}, bf16[528,128]{1,0:T(8,128)(2,1)S(1)}, u32[]{:S(2)}, u32[]{:S(2)}) collective-permute-start(bf16[528,128]{1,0:T(8,128)(2,1)S(1)} %get-tuple-element.77), channel_id=1, source_target_pairs={{0,16},{1,17},{2,18},{3,19},{4,20},{5,21},{6,22},{7,23},{8,24},{9,... | collective-permute-start | bytes 405512 | tf_op jit(solution)/shard_map/ppermute | solution.py:54
  37.8 7.2 %collective-permute-start.10 = (bf16[272,128]{1,0:T(8,128)(2,1)S(1)}, bf16[272,128]{1,0:T(8,128)(2,1)S(1)}, u32[]{:S(2)}, u32[]{:S(2)}) collective-permute-start(bf16[272,128]{1,0:T(8,128)(2,1)S(1)} %get-tuple-element.78), channel_id=1, source_target_pairs={{0,32},{1,33},{2,34},{3,35},{4,36},{5,37},{6,38},{7,39},{8,40},{9,... | collective-permute-start | bytes 208904 | tf_op jit(solution)/shard_map/ppermute | solution.py:54
  39.3 6.4 %collective-permute-start.11 = (bf16[272,128]{1,0:T(8,128)(2,1)S(1)}, bf16[272,128]{1,0:T(8,128)(2,1)S(1)}, u32[]{:S(2)}, u32[]{:S(2)}) collective-permute-start(bf16[272,128]{1,0:T(8,128)(2,1)S(1)} %get-tuple-element.79), channel_id=1, source_target_pairs={{0,64},{1,65},{2,66},{3,67},{4,68},{5,69},{6,70},{7,71},{8,72},{9,... | collective-permute-start | bytes 208904 | tf_op jit(solution)/shard_map/ppermute | solution.py:54
  42.1 4.3 %collective-permute-start.12 = (bf16[272,128]{1,0:T(8,128)(2,1)S(1)}, bf16[272,128]{1,0:T(8,128)(2,1)S(1)}, u32[]{:S(2)}, u32[]{:S(2)}) collective-permute-start(bf16[272,128]{1,0:T(8,128)(2,1)S(1)} %get-tuple-element.80), channel_id=1, source_target_pairs={{0,96},{1,97},{2,98},{3,99},{4,100},{5,101},{6,102},{7,103},{8,104... | collective-permute-start | bytes 208904 | tf_op jit(solution)/shard_map/ppermute | solution.py:54
  46.5 1.6 %collective-permute-start.13 = (bf16[512,128]{1,0:T(8,128)(2,1)S(1)}, bf16[512,128]{1,0:T(8,128)(2,1)S(1)}, u32[]{:S(2)}, u32[]{:S(2)}) collective-permute-start(bf16[512,128]{1,0:T(8,128)(2,1)S(1)} %get-tuple-element.81), channel_id=1, source_target_pairs={{0,16},{1,17},{2,18},{3,19},{4,20},{5,21},{6,22},{7,23},{8,24},{9,... | collective-permute-start | bytes 393224 | tf_op jit(solution)/shard_map/ppermute | solution.py:54
  51.2 9.1 %collective-permute-start.16 = (bf16[64,3072]{1,0:T(8,128)(2,1)S(1)}, bf16[64,3072]{1,0:T(8,128)(2,1)S(1)}, u32[]{:S(2)}, u32[]{:S(2)}) collective-permute-start(bf16[64,3072]{1,0:T(8,128)(2,1)S(1)} %get-tuple-element.89), channel_id=1, source_target_pairs={{0,4},{1,5},{2,6},{3,7},{4,8},{5,9},{6,10},{7,11},{8,12},{9,13},{1... | collective-permute-start | bytes 1179656 | tf_op jit(solution)/shard_map/ppermute | solution.py:54
  53.9 8.6 %collective-permute-start.15 = (bf16[64,3072]{1,0:T(8,128)(2,1)S(1)}, bf16[64,3072]{1,0:T(8,128)(2,1)S(1)}, u32[]{:S(2)}, u32[]{:S(2)}) collective-permute-start(bf16[64,3072]{1,0:T(8,128)(2,1)S(1)} %get-tuple-element.87), channel_id=1, source_target_pairs={{0,12},{1,13},{2,14},{3,15},{4,0},{5,1},{6,2},{7,3},{8,4},{9,5},{1... | collective-permute-start | bytes 1179656 | tf_op jit(solution)/shard_map/ppermute | solution.py:54
  57.2 9.5 %collective-permute-start.18 = (bf16[64,3072]{1,0:T(8,128)(2,1)S(1)}, bf16[64,3072]{1,0:T(8,128)(2,1)S(1)}, u32[]{:S(2)}, u32[]{:S(2)}) collective-permute-start(bf16[64,3072]{1,0:T(8,128)(2,1)S(1)} %get-tuple-element.90), channel_id=1, source_target_pairs={{0,12},{1,13},{2,14},{3,15},{4,0},{5,1},{6,2},{7,3},{8,4},{9,5},{1... | collective-permute-start | bytes 1179656 | tf_op jit(solution)/shard_map/ppermute | solution.py:54
  57.3 13.3 %collective-permute-start.14 = (bf16[64,3072]{1,0:T(8,128)(2,1)S(1)}, bf16[64,3072]{1,0:T(8,128)(2,1)S(1)}, u32[]{:S(2)}, u32[]{:S(2)}) collective-permute-start(bf16[64,3072]{1,0:T(8,128)(2,1)S(1)} %get-tuple-element.85), channel_id=1, source_target_pairs={{0,4},{1,5},{2,6},{3,7},{4,8},{5,9},{6,10},{7,11},{8,12},{9,13},{1... | collective-permute-start | bytes 1179656 | tf_op jit(solution)/shard_map/ppermute | solution.py:54
  60.3 10.2 %collective-permute-start.19 = (bf16[64,3072]{1,0:T(8,128)(2,1)S(1)}, bf16[64,3072]{1,0:T(8,128)(2,1)S(1)}, u32[]{:S(2)}, u32[]{:S(2)}) collective-permute-start(bf16[64,3072]{1,0:T(8,128)(2,1)S(1)} %relay.2.refs_0_), channel_id=1, source_target_pairs={{0,4},{1,5},{2,6},{3,7},{4,8},{5,9},{6,10},{7,11},{8,12},{9,13},{1... | collective-permute-start | bytes 1179656 | tf_op jit(solution)/shard_map/ppermute | solution.py:54
  62.6 9.1 %collective-permute-start.17 = (bf16[64,3072]{1,0:T(8,128)(2,1)S(1)}, bf16[64,3072]{1,0:T(8,128)(2,1)S(1)}, u32[]{:S(2)}, u32[]{:S(2)}) collective-permute-start(bf16[64,3072]{1,0:T(8,128)(2,1)S(1)} %relay.3), channel_id=1, source_target_pairs={{0,12},{1,13},{2,14},{3,15},{4,0},{5,1},{6,2},{7,3},{8,4},{9,5},{1... | collective-permute-start | bytes 1179656 | tf_op jit(solution)/shard_map/ppermute | solution.py:54
  71.8 6.9 %collective-permute-start.20 = (bf16[16,6144]{1,0:T(8,128)(2,1)S(1)}, bf16[16,6144]{1,0:T(8,128)(2,1)S(1)}, u32[]{:S(2)}, u32[]{:S(2)}) collective-permute-start(bf16[16,6144]{1,0:T(8,128)(2,1)S(1)} %get-tuple-element.96), channel_id=1, source_target_pairs={{0,1},{1,2},{2,3},{3,0},{4,5},{5,6},{6,7},{7,4},{8,9},{9,10},{10,1... | collective-permute-start | bytes 589832 | tf_op jit(solution)/shard_map/ppermute | solution.py:54
  71.8 8.5 %collective-permute-start.21 = (bf16[16,6144]{1,0:T(8,128)(2,1)S(1)}, bf16[16,6144]{1,0:T(8,128)(2,1)S(1)}, u32[]{:S(2)}, u32[]{:S(2)}) collective-permute-start(bf16[16,6144]{1,0:T(8,128)(2,1)S(1)} %get-tuple-element.97), channel_id=1, source_target_pairs={{0,3},{1,0},{2,1},{3,2},{4,7},{5,4},{6,5},{7,6},{8,11},{9,8},{10,9... | collective-permute-start | bytes 589832 | tf_op jit(solution)/shard_map/ppermute | solution.py:54
  75.1 7.2 %collective-permute-start.22 = (bf16[16,6144]{1,0:T(8,128)(2,1)S(1)}, bf16[16,6144]{1,0:T(8,128)(2,1)S(1)}, u32[]{:S(2)}, u32[]{:S(2)}) collective-permute-start(bf16[16,6144]{1,0:T(8,128)(2,1)S(1)} %get-tuple-element.98), channel_id=1, source_target_pairs={{0,2},{1,3},{2,0},{3,1},{4,6},{5,7},{6,4},{7,5},{8,10},{9,11},{10,... | collective-permute-start | bytes 589832 | tf_op jit(solution)/shard_map/ppermute | solution.py:54

commit v5 on v3

--- a/solution.py
+++ b/solution.py
@@ -439,7 +439,7 @@
 def output(d, weights, start, width, kinds, after=()):
     rows = d.shape[0]
     return pl.pallas_call(
-        functools.partial(output_kernel, start, 512),
+        functools.partial(output_kernel, start, 1024),
         out_shape=tuple(pltpu.VMEM((rows // SIDE, width), kind) for kind in kinds),
         in_specs=[VMEM] * (4 + len(after)),
         out_specs=(VMEM,) * SIDE,

time: 83.2 us -> 83.2 us (level)
  no operation moved by 1% of the time
where the time goes in v5:
time: 83.2 us; the launch traced here: 83.1 us
  starting transfers between devices  34.9 us (42%)
  waiting for transfers between devices  27.1 us (33%)
  Pallas kernels  20.8 us (25%)
    ppermute x23, starting transfers between devices, move(): return lax.ppermute(array, AXES, pairs)  34.9 us
    ppermute x23, waiting for transfers between devices, move(): return lax.ppermute(array, AXES, pairs)  27.1 us
    pallas_call x4, Pallas kernels, project(): pl.pallas_call(functools.partial(project_kernel, slots, has_sum), out_sha...  5.54 us
    pallas_call x2, Pallas kernels, output(): pl.pallas_call(functools.partial(output_kernel, start, 1024), out_shape=t...  5.26 us
    pallas_call x1, Pallas kernels, load(): pl.pallas_call(load_kernel, out_shape=tuple((pltpu.VMEM(a.shape, a.dtype)...  4.84 us
  transfers between devices with their start and end apart: 23, of which 16 were waited for; matrix products, arithmetic and copies ran while one was open for 0% of the time, Pallas kernels for 18%

profile of v5, /device:TPU:0, one launch (start us, length us, event | category | flops | bytes accessed | tf_op | source)
XLA Modules:
  0.0 83.1 jit_solution(9462344108066069601)
XLA Ops:
  0.0 3.1 %collective-permute-start = (bf16[256,384]{1,0:T(8,128)(2,1)}, bf16[256,384]{1,0:T(8,128)(2,1)S(1)}, u32[]{:S(2)}, u32[]{:S(2)}) collective-permute-start(bf16[256,384]{1,0:T(8,128)(2,1)} %refs_0_.1), channel_id=1, source_target_pairs={{0,3},{1,0},{2,1},{3,2},{4,7},{5,4},{6,5},{7,6},{8,11},{9,8},{10,9... | collective-permute-start | bytes 589832 | tf_op jit(solution)/shard_map/ppermute | solution.py:54
  3.1 0.0 collective-permute-start.1
  3.1 2.2 %collective-permute-start.2 = (bf16[256,384]{1,0:T(8,128)(2,1)}, bf16[256,384]{1,0:T(8,128)(2,1)S(1)}, u32[]{:S(2)}, u32[]{:S(2)}) collective-permute-start(bf16[256,384]{1,0:T(8,128)(2,1)} %refs_0_.1), channel_id=1, source_target_pairs={{0,2},{1,3},{2,0},{3,1},{4,6},{5,7},{6,4},{7,5},{8,10},{9,11},{10,... | collective-permute-start | bytes 589832 | tf_op jit(solution)/shard_map/ppermute | solution.py:54
  5.3 4.8 %load.1 = (bf16[256,384]{1,0:T(8,128)(2,1)S(1)}, bf16[6144,512]{1,0:T(8,128)(2,1)S(1)}, bf16[6144,512]{1,0:T(8,128)(2,1)S(1)}) custom-call(bf16[256,384]{1,0:T(8,128)(2,1)} %refs_0_.1, bf16[6144,512]{1,0:T(8,128)(2,1)} %refs_1_.1, bf16[6144,512]{1,0:T(8,128)(2,1)} %refs_2_.1), custom_call_target="tpu_custom_call" | custom-call | bytes 25559040 | tf_op jit(solution)/shard_map/load/pallas_call | solution.py:147
  10.2 0.0 copy-start.2
  10.2 0.0 copy-start
  10.2 0.0 collective-permute-done.refs_1_
  10.2 2.1 %collective-permute-done.1.refs_2_ = bf16[256,384]{1,0:T(8,128)(2,1)S(1)} collective-permute-done((bf16[256,384]{1,0:T(8,128)(2,1)}, bf16[256,384]{1,0:T(8,128)(2,1)S(1)}, u32[]{:S(2)}, u32[]{:S(2)}) %collective-permute-start.1) | collective-permute-done | bytes 196640 | tf_op jit(solution)/shard_map/ppermute | solution.py:54
  12.3 0.0 collective-permute-done.2.refs_3_
  12.3 0.1 join.1
  12.4 4.1 %collective-permute-start.3 = (bf16[128,1536]{1,0:T(8,128)(2,1)S(1)}, bf16[128,1536]{1,0:T(8,128)(2,1)S(1)}, u32[]{:S(2)}, u32[]{:S(2)}) collective-permute-start(bf16[128,1536]{1,0:T(8,128)(2,1)S(1)} %get-tuple-element.54.refs_0_), channel_id=1, source_target_pairs={{0,12},{1,13},{2,14},{3,15},{4,0},{5,1},{6,2},{7,3},{8,4},{9,5},{1... | collective-permute-start | bytes 1179656 | tf_op jit(solution)/shard_map/ppermute | solution.py:54
  16.5 0.0 collective-permute-start.5
  16.5 3.2 %collective-permute-start.8 = (bf16[128,1536]{1,0:T(8,128)(2,1)S(1)}, bf16[128,1536]{1,0:T(8,128)(2,1)S(1)}, u32[]{:S(2)}, u32[]{:S(2)}) collective-permute-start(bf16[128,1536]{1,0:T(8,128)(2,1)S(1)} %get-tuple-element.55.refs_1_), channel_id=1, source_target_pairs={{0,12},{1,13},{2,14},{3,15},{4,0},{5,1},{6,2},{7,3},{8,4},{9,5},{1... | collective-permute-start | bytes 1179656 | tf_op jit(solution)/shard_map/ppermute | solution.py:54
  19.7 0.0 collective-permute-start.7
  19.7 2.1 %collective-permute-done.3.refs_0_ = bf16[128,1536]{1,0:T(8,128)(2,1)S(1)} collective-permute-done((bf16[128,1536]{1,0:T(8,128)(2,1)S(1)}, bf16[128,1536]{1,0:T(8,128)(2,1)S(1)}, u32[]{:S(2)}, u32[]{:S(2)}) %collective-permute-start.3) | collective-permute-done | bytes 393248 | tf_op jit(solution)/shard_map/ppermute | solution.py:54
  21.8 3.7 %collective-permute-start.4 = (bf16[128,1536]{1,0:T(8,128)(2,1)S(1)}, bf16[128,1536]{1,0:T(8,128)(2,1)S(1)}, u32[]{:S(2)}, u32[]{:S(2)}) collective-permute-start(bf16[128,1536]{1,0:T(8,128)(2,1)S(1)} %collective-permute-done.3.refs_0_), channel_id=1, source_target_pairs={{0,12},{1,13},{2,14},{3,15},{4,0},{5,1},{6,2},{7,3},{8,4},{9,5},{1... | collective-permute-start | bytes 1179656 | tf_op jit(solution)/shard_map/ppermute | solution.py:54
  25.5 0.0 collective-permute-done.5.refs_1_
  25.5 0.0 collective-permute-start.6
  25.5 1.3 %decay.1 = (f32[4,256,256]{2,1,0:T(8,128)S(1)}, f32[256,512]{1,0:T(8,128)S(1)}, f32[256,512]{1,0:T(8,128)S(1)}) custom-call(f32[4,256]{1,0:T(4,128)S(1)} %copy-done.2), custom_call_target="tpu_custom_call" | custom-call | flops 2000000 | bytes 2000000 | tf_op jit(solution)/shard_map/decay/pallas_call | solution.py:116
  26.8 1.4 %project.4 = (f32[256,512]{1,0:T(8,128)S(1)}, f32[256,512]{1,0:T(8,128)S(1)}, f32[256,512]{1,0:T(8,128)S(1)}) custom-call(bf16[128,1536]{1,0:T(8,128)(2,1)S(1)} %get-tuple-element.54.refs_0_, bf16[128,1536]{1,0:T(8,128)(2,1)S(1)} %get-tuple-element.55.refs_1_, bf16[6144,512]{1,0:T(8,128)(2,1)S(1)} %get-tuple-element.53.refs_4_.refs_2_.refs_5_.wq_ref, ...), custom_call_target="tpu_custom_call" | custom-call | flops 1207959552 | bytes 6144000 | tf_op jit(solution)/shard_map/project/pallas_call | solution.py:202
  28.2 0.0 collective-permute-done.8.refs_1_
  28.2 1.4 %project.5 = (f32[256,512]{1,0:T(8,128)S(1)}, f32[256,512]{1,0:T(8,128)S(1)}, f32[256,512]{1,0:T(8,128)S(1)}) custom-call(bf16[128,1536]{1,0:T(8,128)(2,1)S(1)} %collective-permute-done.3.refs_0_, bf16[128,1536]{1,0:T(8,128)(2,1)S(1)} %collective-permute-done.8.refs_1_, f32[256,512]{1,0:T(8,128)S(1)} %get-tuple-element.58.refs_2_, ...), custom_call_target="tpu_custom_call" | custom-call | flops 1207959552 | bytes 6144000 | tf_op jit(solution)/shard_map/project/pallas_call | solution.py:202
  29.6 0.1 collective-permute-done.7.refs_0_
  29.7 1.4 %project.6 = (f32[256,512]{1,0:T(8,128)S(1)}, f32[256,512]{1,0:T(8,128)S(1)}, f32[256,512]{1,0:T(8,128)S(1)}) custom-call(bf16[128,1536]{1,0:T(8,128)(2,1)S(1)} %collective-permute-done.7.refs_0_, bf16[128,1536]{1,0:T(8,128)(2,1)S(1)} %collective-permute-done.5.refs_1_, f32[256,512]{1,0:T(8,128)S(1)} %get-tuple-element.61.refs_2_, ...), custom_call_target="tpu_custom_call" | custom-call | flops 1207959552 | bytes 6144000 | tf_op jit(solution)/shard_map/project/pallas_call | solution.py:202
  31.1 0.0 collective-permute-done.4.refs_0_
  31.1 3.4 %collective-permute-done.6.refs_1_ = bf16[128,1536]{1,0:T(8,128)(2,1)S(1)} collective-permute-done((bf16[128,1536]{1,0:T(8,128)(2,1)S(1)}, bf16[128,1536]{1,0:T(8,128)(2,1)S(1)}, u32[]{:S(2)}, u32[]{:S(2)}) %collective-permute-start.6) | collective-permute-done | bytes 393248 | tf_op jit(solution)/shard_map/ppermute | solution.py:54
  34.5 1.4 %project.7 = (bf16[256,512]{1,0:T(8,128)(2,1)S(1)}, bf16[256,512]{1,0:T(8,128)(2,1)S(1)}, bf16[256,512]{1,0:T(8,128)(2,1)S(1)}) custom-call(bf16[128,1536]{1,0:T(8,128)(2,1)S(1)} %collective-permute-done.4.refs_0_, bf16[128,1536]{1,0:T(8,128)(2,1)S(1)} %collective-permute-done.6.refs_1_, f32[256,512]{1,0:T(8,128)S(1)} %get-tuple-element.64.refs_2_, ...), custom_call_target="tpu_custom_call" | custom-call | flops 1207959552 | bytes 6144000 | tf_op jit(solution)/shard_map/project/pallas_call | solution.py:202
  35.9 0.4 states.1
  36.3 0.1 collective-permute-start.9
  36.3 1.3 %collective-permute-done.9.peer_ref = bf16[528,128]{1,0:T(8,128)(2,1)S(1)} collective-permute-done((bf16[528,128]{1,0:T(8,128)(2,1)S(1)}, bf16[528,128]{1,0:T(8,128)(2,1)S(1)}, u32[]{:S(2)}, u32[]{:S(2)}) %collective-permute-start.9) | collective-permute-done | bytes 135200 | tf_op jit(solution)/shard_map/ppermute | solution.py:54
  37.7 0.1 chip_states.1
  37.8 1.6 %collective-permute-start.10 = (bf16[272,128]{1,0:T(8,128)(2,1)S(1)}, bf16[272,128]{1,0:T(8,128)(2,1)S(1)}, u32[]{:S(2)}, u32[]{:S(2)}) collective-permute-start(bf16[272,128]{1,0:T(8,128)(2,1)S(1)} %get-tuple-element.74), channel_id=1, source_target_pairs={{0,32},{1,33},{2,34},{3,35},{4,36},{5,37},{6,38},{7,39},{8,40},{9,... | collective-permute-start | bytes 208904 | tf_op jit(solution)/shard_map/ppermute | solution.py:54
  39.3 2.7 %collective-permute-start.11 = (bf16[272,128]{1,0:T(8,128)(2,1)S(1)}, bf16[272,128]{1,0:T(8,128)(2,1)S(1)}, u32[]{:S(2)}, u32[]{:S(2)}) collective-permute-start(bf16[272,128]{1,0:T(8,128)(2,1)S(1)} %get-tuple-element.75), channel_id=1, source_target_pairs={{0,64},{1,65},{2,66},{3,67},{4,68},{5,69},{6,70},{7,71},{8,72},{9,... | collective-permute-start | bytes 208904 | tf_op jit(solution)/shard_map/ppermute | solution.py:54
  42.1 1.4 %collective-permute-start.12 = (bf16[272,128]{1,0:T(8,128)(2,1)S(1)}, bf16[272,128]{1,0:T(8,128)(2,1)S(1)}, u32[]{:S(2)}, u32[]{:S(2)}) collective-permute-start(bf16[272,128]{1,0:T(8,128)(2,1)S(1)} %get-tuple-element.76), channel_id=1, source_target_pairs={{0,96},{1,97},{2,98},{3,99},{4,100},{5,101},{6,102},{7,103},{8,104... | collective-permute-start | bytes 208904 | tf_op jit(solution)/shard_map/ppermute | solution.py:54
  43.5 1.5 %intra.1 = (f32[256,512]{1,0:T(8,128)S(1)}, f32[256,512]{1,0:T(8,128)S(1)}, f32[256,512]{1,0:T(8,128)S(1)}) custom-call(bf16[256,512]{1,0:T(8,128)(2,1)S(1)} %get-tuple-element.67.q_ref, bf16[256,512]{1,0:T(8,128)(2,1)S(1)} %get-tuple-element.68.k_ref, bf16[256,512]{1,0:T(8,128)(2,1)S(1)} %get-tuple-element.69.v_ref, bf16[256,512]{1,0:T(8,128)(2,1)S(1)} %copy-done.1, ...), custom_call_target="tpu_custom_call" | custom-call | flops 340000000 | bytes 4000000 | tf_op jit(solution)/shard_map/intra/pallas_call | solution.py:276
  45.0 0.7 collective-permute-done.11.two_ref
  45.8 0.6 collective-permute-done.12.three_ref
  46.4 0.1 outer_states.1
  46.5 0.3 collective-permute-start.13
  46.8 1.3 %collective-permute-done.13.theirs_ref = bf16[512,128]{1,0:T(8,128)(2,1)S(1)} collective-permute-done((bf16[512,128]{1,0:T(8,128)(2,1)S(1)}, bf16[512,128]{1,0:T(8,128)(2,1)S(1)}, u32[]{:S(2)}, u32[]{:S(2)}) %collective-permute-start.13) | collective-permute-done | bytes 131104 | tf_op jit(solution)/shard_map/ppermute | solution.py:54
  48.1 0.5 inter.1.d_ref
  48.7 2.6 %output.2 = (f32[64,3072]{1,0:T(8,128)S(1)}, f32[64,3072]{1,0:T(8,128)S(1)}, bf16[64,3072]{1,0:T(8,128)(2,1)S(1)}, bf16[64,3072]{1,0:T(8,128)(2,1)S(1)}) custom-call(bf16[256,1536]{1,0:T(8,128)(2,1)S(1)} %inter.1.d_ref, bf16[6144,512]{1,0:T(8,128)(2,1)S(1)} %get-tuple-element.53.refs_4_.refs_2_.refs_5_.wq_ref, ...), custom_call_target="tpu_custom_call" | custom-call | flops 2415919104 | bytes 6000000 | tf_op jit(solution)/shard_map/output/pallas_call | solution.py:441
  51.3 0.1 collective-permute-start.16
  51.4 2.6 %output.3 = (f32[64,3072]{1,0:T(8,128)S(1)}, bf16[64,3072]{1,0:T(8,128)(2,1)S(1)}, f32[64,3072]{1,0:T(8,128)S(1)}, bf16[64,3072]{1,0:T(8,128)(2,1)S(1)}) custom-call(bf16[256,1536]{1,0:T(8,128)(2,1)S(1)} %inter.1.d_ref, bf16[6144,512]{1,0:T(8,128)(2,1)S(1)} %get-tuple-element.53.refs_4_.refs_2_.refs_5_.wq_ref, ...), custom_call_target="tpu_custom_call" | custom-call | flops 2415919104 | bytes 6000000 | tf_op jit(solution)/shard_map/output/pallas_call | solution.py:441
  54.0 3.3 %collective-permute-start.15 = (bf16[64,3072]{1,0:T(8,128)(2,1)S(1)}, bf16[64,3072]{1,0:T(8,128)(2,1)S(1)}, u32[]{:S(2)}, u32[]{:S(2)}) collective-permute-start(bf16[64,3072]{1,0:T(8,128)(2,1)S(1)} %get-tuple-element.87), channel_id=1, source_target_pairs={{0,12},{1,13},{2,14},{3,15},{4,0},{5,1},{6,2},{7,3},{8,4},{9,5},{1... | collective-permute-start | bytes 1179656 | tf_op jit(solution)/shard_map/ppermute | solution.py:54
  57.3 0.1 collective-permute-start.18
  57.4 1.9 %collective-permute-start.14 = (bf16[64,3072]{1,0:T(8,128)(2,1)S(1)}, bf16[64,3072]{1,0:T(8,128)(2,1)S(1)}, u32[]{:S(2)}, u32[]{:S(2)}) collective-permute-start(bf16[64,3072]{1,0:T(8,128)(2,1)S(1)} %get-tuple-element.85), channel_id=1, source_target_pairs={{0,4},{1,5},{2,6},{3,7},{4,8},{5,9},{6,10},{7,11},{8,12},{9,13},{1... | collective-permute-start | bytes 1179656 | tf_op jit(solution)/shard_map/ppermute | solution.py:54
  59.4 1.0 %collective-permute-done.16.other_ref = bf16[64,3072]{1,0:T(8,128)(2,1)S(1)} collective-permute-done((bf16[64,3072]{1,0:T(8,128)(2,1)S(1)}, bf16[64,3072]{1,0:T(8,128)(2,1)S(1)}, u32[]{:S(2)}, u32[]{:S(2)}) %collective-permute-start.16) | collective-permute-done | bytes 393248 | tf_op jit(solution)/shard_map/ppermute | solution.py:54
  60.4 0.1 relay.2.refs_0_
  60.4 0.1 collective-permute-start.19
  60.5 2.1 %collective-permute-done.15.other_ref = bf16[64,3072]{1,0:T(8,128)(2,1)S(1)} collective-permute-done((bf16[64,3072]{1,0:T(8,128)(2,1)S(1)}, bf16[64,3072]{1,0:T(8,128)(2,1)S(1)}, u32[]{:S(2)}, u32[]{:S(2)}) %collective-permute-start.15) | collective-permute-done | bytes 393248 | tf_op jit(solution)/shard_map/ppermute | solution.py:54
  62.6 0.1 relay.3
  62.7 3.8 %collective-permute-start.17 = (bf16[64,3072]{1,0:T(8,128)(2,1)S(1)}, bf16[64,3072]{1,0:T(8,128)(2,1)S(1)}, u32[]{:S(2)}, u32[]{:S(2)}) collective-permute-start(bf16[64,3072]{1,0:T(8,128)(2,1)S(1)} %relay.3), channel_id=1, source_target_pairs={{0,12},{1,13},{2,14},{3,15},{4,0},{5,1},{6,2},{7,3},{8,4},{9,5},{1... | collective-permute-start | bytes 1179656 | tf_op jit(solution)/shard_map/ppermute | solution.py:54
  66.5 0.4 collective-permute-done.18.refs_1_
  66.8 3.8 %collective-permute-done.19.refs_2_ = bf16[64,3072]{1,0:T(8,128)(2,1)S(1)} collective-permute-done((bf16[64,3072]{1,0:T(8,128)(2,1)S(1)}, bf16[64,3072]{1,0:T(8,128)(2,1)S(1)}, u32[]{:S(2)}, u32[]{:S(2)}) %collective-permute-start.19) | collective-permute-done | bytes 393248 | tf_op jit(solution)/shard_map/ppermute | solution.py:54
  70.6 0.1 add.2
  70.7 1.0 %collective-permute-done.17.refs_2_ = bf16[64,3072]{1,0:T(8,128)(2,1)S(1)} collective-permute-done((bf16[64,3072]{1,0:T(8,128)(2,1)S(1)}, bf16[64,3072]{1,0:T(8,128)(2,1)S(1)}, u32[]{:S(2)}, u32[]{:S(2)}) %collective-permute-start.17) | collective-permute-done | bytes 393248 | tf_op jit(solution)/shard_map/ppermute | solution.py:54
  71.8 0.1 add.3
  71.9 0.1 collective-permute-start.20
  72.0 3.2 %collective-permute-start.21 = (bf16[16,6144]{1,0:T(8,128)(2,1)S(1)}, bf16[16,6144]{1,0:T(8,128)(2,1)S(1)}, u32[]{:S(2)}, u32[]{:S(2)}) collective-permute-start(bf16[16,6144]{1,0:T(8,128)(2,1)S(1)} %get-tuple-element.97), channel_id=1, source_target_pairs={{0,3},{1,0},{2,1},{3,2},{4,7},{5,4},{6,5},{7,6},{8,11},{9,8},{10,9... | collective-permute-start | bytes 589832 | tf_op jit(solution)/shard_map/ppermute | solution.py:54
  75.2 3.6 %collective-permute-done.20.a_ref = bf16[16,6144]{1,0:T(8,128)(2,1)S(1)} collective-permute-done((bf16[16,6144]{1,0:T(8,128)(2,1)S(1)}, bf16[16,6144]{1,0:T(8,128)(2,1)S(1)}, u32[]{:S(2)}, u32[]{:S(2)}) %collective-permute-start.20) | collective-permute-done | bytes 196640 | tf_op jit(solution)/shard_map/ppermute | solution.py:54
  78.8 1.7 %collective-permute-done.21.b_ref = bf16[16,6144]{1,0:T(8,128)(2,1)S(1)} collective-permute-done((bf16[16,6144]{1,0:T(8,128)(2,1)S(1)}, bf16[16,6144]{1,0:T(8,128)(2,1)S(1)}, u32[]{:S(2)}, u32[]{:S(2)}) %collective-permute-start.21) | collective-permute-done | bytes 196640 | tf_op jit(solution)/shard_map/ppermute | solution.py:54
  80.5 1.9 %collective-permute-done.22.c_ref = bf16[16,6144]{1,0:T(8,128)(2,1)S(1)} collective-permute-done((bf16[16,6144]{1,0:T(8,128)(2,1)S(1)}, bf16[16,6144]{1,0:T(8,128)(2,1)S(1)}, u32[]{:S(2)}, u32[]{:S(2)}) %collective-permute-start.22) | collective-permute-done | bytes 196640 | tf_op jit(solution)/shard_map/ppermute | solution.py:54
  82.4 0.8 finish.1
  (7 shorter events, 0.0 us)
Async XLA Ops:
  0.0 10.2 %collective-permute-start = (bf16[256,384]{1,0:T(8,128)(2,1)}, bf16[256,384]{1,0:T(8,128)(2,1)S(1)}, u32[]{:S(2)}, u32[]{:S(2)}) collective-permute-start(bf16[256,384]{1,0:T(8,128)(2,1)} %refs_0_.1), channel_id=1, source_target_pairs={{0,3},{1,0},{2,1},{3,2},{4,7},{5,4},{6,5},{7,6},{8,11},{9,8},{10,9... | collective-permute-start | bytes 589832 | tf_op jit(solution)/shard_map/ppermute | solution.py:54
  3.1 9.2 %collective-permute-start.1 = (bf16[256,384]{1,0:T(8,128)(2,1)}, bf16[256,384]{1,0:T(8,128)(2,1)S(1)}, u32[]{:S(2)}, u32[]{:S(2)}) collective-permute-start(bf16[256,384]{1,0:T(8,128)(2,1)} %refs_0_.1), channel_id=1, source_target_pairs={{0,1},{1,2},{2,3},{3,0},{4,5},{5,6},{6,7},{7,4},{8,9},{9,10},{10,1... | collective-permute-start | bytes 589832 | tf_op jit(solution)/shard_map/ppermute | solution.py:54
  3.1 9.2 %collective-permute-start.2 = (bf16[256,384]{1,0:T(8,128)(2,1)}, bf16[256,384]{1,0:T(8,128)(2,1)S(1)}, u32[]{:S(2)}, u32[]{:S(2)}) collective-permute-start(bf16[256,384]{1,0:T(8,128)(2,1)} %refs_0_.1), channel_id=1, source_target_pairs={{0,2},{1,3},{2,0},{3,1},{4,6},{5,7},{6,4},{7,5},{8,10},{9,11},{10,... | collective-permute-start | bytes 589832 | tf_op jit(solution)/shard_map/ppermute | solution.py:54
  10.2 15.3 %copy-start.2 = (f32[4,256]{1,0:T(4,128)S(1)}, f32[4,256]{1,0:T(4,128)}, u32[]{:S(2)}) copy-start(f32[4,256]{1,0:T(4,128)} %decay_ref.1) | copy-start | bytes 12292
  10.2 16.6 %copy-start = (bf16[6144,512]{1,0:T(8,128)(2,1)S(1)}, bf16[6144,512]{1,0:T(8,128)(2,1)}, u32[]{:S(2)}) copy-start(bf16[6144,512]{1,0:T(8,128)(2,1)} %wv_ref.3) | copy-start | bytes 18874372
  12.4 9.4 %collective-permute-start.3 = (bf16[128,1536]{1,0:T(8,128)(2,1)S(1)}, bf16[128,1536]{1,0:T(8,128)(2,1)S(1)}, u32[]{:S(2)}, u32[]{:S(2)}) collective-permute-start(bf16[128,1536]{1,0:T(8,128)(2,1)S(1)} %get-tuple-element.54.refs_0_), channel_id=1, source_target_pairs={{0,12},{1,13},{2,14},{3,15},{4,0},{5,1},{6,2},{7,3},{8,4},{9,5},{1... | collective-permute-start | bytes 1179656 | tf_op jit(solution)/shard_map/ppermute | solution.py:54
  16.5 9.0 %collective-permute-start.5 = (bf16[128,1536]{1,0:T(8,128)(2,1)S(1)}, bf16[128,1536]{1,0:T(8,128)(2,1)S(1)}, u32[]{:S(2)}, u32[]{:S(2)}) collective-permute-start(bf16[128,1536]{1,0:T(8,128)(2,1)S(1)} %get-tuple-element.55.refs_1_), channel_id=1, source_target_pairs={{0,4},{1,5},{2,6},{3,7},{4,8},{5,9},{6,10},{7,11},{8,12},{9,13},{1... | collective-permute-start | bytes 1179656 | tf_op jit(solution)/shard_map/ppermute | solution.py:54
  16.5 11.7 %collective-permute-start.8 = (bf16[128,1536]{1,0:T(8,128)(2,1)S(1)}, bf16[128,1536]{1,0:T(8,128)(2,1)S(1)}, u32[]{:S(2)}, u32[]{:S(2)}) collective-permute-start(bf16[128,1536]{1,0:T(8,128)(2,1)S(1)} %get-tuple-element.55.refs_1_), channel_id=1, source_target_pairs={{0,12},{1,13},{2,14},{3,15},{4,0},{5,1},{6,2},{7,3},{8,4},{9,5},{1... | collective-permute-start | bytes 1179656 | tf_op jit(solution)/shard_map/ppermute | solution.py:54
  19.7 10.0 %collective-permute-start.7 = (bf16[128,1536]{1,0:T(8,128)(2,1)S(1)}, bf16[128,1536]{1,0:T(8,128)(2,1)S(1)}, u32[]{:S(2)}, u32[]{:S(2)}) collective-permute-start(bf16[128,1536]{1,0:T(8,128)(2,1)S(1)} %get-tuple-element.54.refs_0_), channel_id=1, source_target_pairs={{0,4},{1,5},{2,6},{3,7},{4,8},{5,9},{6,10},{7,11},{8,12},{9,13},{1... | collective-permute-start | bytes 1179656 | tf_op jit(solution)/shard_map/ppermute | solution.py:54
  21.8 9.3 %collective-permute-start.4 = (bf16[128,1536]{1,0:T(8,128)(2,1)S(1)}, bf16[128,1536]{1,0:T(8,128)(2,1)S(1)}, u32[]{:S(2)}, u32[]{:S(2)}) collective-permute-start(bf16[128,1536]{1,0:T(8,128)(2,1)S(1)} %collective-permute-done.3.refs_0_), channel_id=1, source_target_pairs={{0,12},{1,13},{2,14},{3,15},{4,0},{5,1},{6,2},{7,3},{8,4},{9,5},{1... | collective-permute-start | bytes 1179656 | tf_op jit(solution)/shard_map/ppermute | solution.py:54
  25.5 9.0 %collective-permute-start.6 = (bf16[128,1536]{1,0:T(8,128)(2,1)S(1)}, bf16[128,1536]{1,0:T(8,128)(2,1)S(1)}, u32[]{:S(2)}, u32[]{:S(2)}) collective-permute-start(bf16[128,1536]{1,0:T(8,128)(2,1)S(1)} %collective-permute-done.5.refs_1_), channel_id=1, source_target_pairs={{0,4},{1,5},{2,6},{3,7},{4,8},{5,9},{6,10},{7,11},{8,12},{9,13},{1... | collective-permute-start | bytes 1179656 | tf_op jit(solution)/shard_map/ppermute | solution.py:54
  34.5 1.4 %copy-start.1 = (bf16[256,512]{1,0:T(8,128)(2,1)S(1)}, bf16[256,512]{1,0:T(8,128)(2,1)}, u32[]{:S(2)}) copy-start(bf16[256,512]{1,0:T(8,128)(2,1)} %g_ref.5) | copy-start | bytes 786436
  36.3 1.4 %collective-permute-start.9 = (bf16[528,128]{1,0:T(8,128)(2,1)S(1)}, bf16[528,128]{1,0:T(8,128)(2,1)S(1)}, u32[]{:S(2)}, u32[]{:S(2)}) collective-permute-start(bf16[528,128]{1,0:T(8,128)(2,1)S(1)} %get-tuple-element.73), channel_id=1, source_target_pairs={{0,16},{1,17},{2,18},{3,19},{4,20},{5,21},{6,22},{7,23},{8,24},{9,... | collective-permute-start | bytes 405512 | tf_op jit(solution)/shard_map/ppermute | solution.py:54
  37.8 7.2 %collective-permute-start.10 = (bf16[272,128]{1,0:T(8,128)(2,1)S(1)}, bf16[272,128]{1,0:T(8,128)(2,1)S(1)}, u32[]{:S(2)}, u32[]{:S(2)}) collective-permute-start(bf16[272,128]{1,0:T(8,128)(2,1)S(1)} %get-tuple-element.74), channel_id=1, source_target_pairs={{0,32},{1,33},{2,34},{3,35},{4,36},{5,37},{6,38},{7,39},{8,40},{9,... | collective-permute-start | bytes 208904 | tf_op jit(solution)/shard_map/ppermute | solution.py:54
  39.3 6.4 %collective-permute-start.11 = (bf16[272,128]{1,0:T(8,128)(2,1)S(1)}, bf16[272,128]{1,0:T(8,128)(2,1)S(1)}, u32[]{:S(2)}, u32[]{:S(2)}) collective-permute-start(bf16[272,128]{1,0:T(8,128)(2,1)S(1)} %get-tuple-element.75), channel_id=1, source_target_pairs={{0,64},{1,65},{2,66},{3,67},{4,68},{5,69},{6,70},{7,71},{8,72},{9,... | collective-permute-start | bytes 208904 | tf_op jit(solution)/shard_map/ppermute | solution.py:54
  42.1 4.3 %collective-permute-start.12 = (bf16[272,128]{1,0:T(8,128)(2,1)S(1)}, bf16[272,128]{1,0:T(8,128)(2,1)S(1)}, u32[]{:S(2)}, u32[]{:S(2)}) collective-permute-start(bf16[272,128]{1,0:T(8,128)(2,1)S(1)} %get-tuple-element.76), channel_id=1, source_target_pairs={{0,96},{1,97},{2,98},{3,99},{4,100},{5,101},{6,102},{7,103},{8,104... | collective-permute-start | bytes 208904 | tf_op jit(solution)/shard_map/ppermute | solution.py:54
  46.5 1.6 %collective-permute-start.13 = (bf16[512,128]{1,0:T(8,128)(2,1)S(1)}, bf16[512,128]{1,0:T(8,128)(2,1)S(1)}, u32[]{:S(2)}, u32[]{:S(2)}) collective-permute-start(bf16[512,128]{1,0:T(8,128)(2,1)S(1)} %get-tuple-element.80), channel_id=1, source_target_pairs={{0,16},{1,17},{2,18},{3,19},{4,20},{5,21},{6,22},{7,23},{8,24},{9,... | collective-permute-start | bytes 393224 | tf_op jit(solution)/shard_map/ppermute | solution.py:54
  51.3 9.1 %collective-permute-start.16 = (bf16[64,3072]{1,0:T(8,128)(2,1)S(1)}, bf16[64,3072]{1,0:T(8,128)(2,1)S(1)}, u32[]{:S(2)}, u32[]{:S(2)}) collective-permute-start(bf16[64,3072]{1,0:T(8,128)(2,1)S(1)} %get-tuple-element.89), channel_id=1, source_target_pairs={{0,4},{1,5},{2,6},{3,7},{4,8},{5,9},{6,10},{7,11},{8,12},{9,13},{1... | collective-permute-start | bytes 1179656 | tf_op jit(solution)/shard_map/ppermute | solution.py:54
  54.0 8.6 %collective-permute-start.15 = (bf16[64,3072]{1,0:T(8,128)(2,1)S(1)}, bf16[64,3072]{1,0:T(8,128)(2,1)S(1)}, u32[]{:S(2)}, u32[]{:S(2)}) collective-permute-start(bf16[64,3072]{1,0:T(8,128)(2,1)S(1)} %get-tuple-element.87), channel_id=1, source_target_pairs={{0,12},{1,13},{2,14},{3,15},{4,0},{5,1},{6,2},{7,3},{8,4},{9,5},{1... | collective-permute-start | bytes 1179656 | tf_op jit(solution)/shard_map/ppermute | solution.py:54
  57.3 9.5 %collective-permute-start.18 = (bf16[64,3072]{1,0:T(8,128)(2,1)S(1)}, bf16[64,3072]{1,0:T(8,128)(2,1)S(1)}, u32[]{:S(2)}, u32[]{:S(2)}) collective-permute-start(bf16[64,3072]{1,0:T(8,128)(2,1)S(1)} %get-tuple-element.90), channel_id=1, source_target_pairs={{0,12},{1,13},{2,14},{3,15},{4,0},{5,1},{6,2},{7,3},{8,4},{9,5},{1... | collective-permute-start | bytes 1179656 | tf_op jit(solution)/shard_map/ppermute | solution.py:54
  57.4 13.3 %collective-permute-start.14 = (bf16[64,3072]{1,0:T(8,128)(2,1)S(1)}, bf16[64,3072]{1,0:T(8,128)(2,1)S(1)}, u32[]{:S(2)}, u32[]{:S(2)}) collective-permute-start(bf16[64,3072]{1,0:T(8,128)(2,1)S(1)} %get-tuple-element.85), channel_id=1, source_target_pairs={{0,4},{1,5},{2,6},{3,7},{4,8},{5,9},{6,10},{7,11},{8,12},{9,13},{1... | collective-permute-start | bytes 1179656 | tf_op jit(solution)/shard_map/ppermute | solution.py:54
  60.4 10.2 %collective-permute-start.19 = (bf16[64,3072]{1,0:T(8,128)(2,1)S(1)}, bf16[64,3072]{1,0:T(8,128)(2,1)S(1)}, u32[]{:S(2)}, u32[]{:S(2)}) collective-permute-start(bf16[64,3072]{1,0:T(8,128)(2,1)S(1)} %relay.2.refs_0_), channel_id=1, source_target_pairs={{0,4},{1,5},{2,6},{3,7},{4,8},{5,9},{6,10},{7,11},{8,12},{9,13},{1... | collective-permute-start | bytes 1179656 | tf_op jit(solution)/shard_map/ppermute | solution.py:54
  62.7 9.1 %collective-permute-start.17 = (bf16[64,3072]{1,0:T(8,128)(2,1)S(1)}, bf16[64,3072]{1,0:T(8,128)(2,1)S(1)}, u32[]{:S(2)}, u32[]{:S(2)}) collective-permute-start(bf16[64,3072]{1,0:T(8,128)(2,1)S(1)} %relay.3), channel_id=1, source_target_pairs={{0,12},{1,13},{2,14},{3,15},{4,0},{5,1},{6,2},{7,3},{8,4},{9,5},{1... | collective-permute-start | bytes 1179656 | tf_op jit(solution)/shard_map/ppermute | solution.py:54
  71.9 6.9 %collective-permute-start.20 = (bf16[16,6144]{1,0:T(8,128)(2,1)S(1)}, bf16[16,6144]{1,0:T(8,128)(2,1)S(1)}, u32[]{:S(2)}, u32[]{:S(2)}) collective-permute-start(bf16[16,6144]{1,0:T(8,128)(2,1)S(1)} %get-tuple-element.96), channel_id=1, source_target_pairs={{0,1},{1,2},{2,3},{3,0},{4,5},{5,6},{6,7},{7,4},{8,9},{9,10},{10,1... | collective-permute-start | bytes 589832 | tf_op jit(solution)/shard_map/ppermute | solution.py:54
  72.0 8.5 %collective-permute-start.21 = (bf16[16,6144]{1,0:T(8,128)(2,1)S(1)}, bf16[16,6144]{1,0:T(8,128)(2,1)S(1)}, u32[]{:S(2)}, u32[]{:S(2)}) collective-permute-start(bf16[16,6144]{1,0:T(8,128)(2,1)S(1)} %get-tuple-element.97), channel_id=1, source_target_pairs={{0,3},{1,0},{2,1},{3,2},{4,7},{5,4},{6,5},{7,6},{8,11},{9,8},{10,9... | collective-permute-start | bytes 589832 | tf_op jit(solution)/shard_map/ppermute | solution.py:54
  75.2 7.2 %collective-permute-start.22 = (bf16[16,6144]{1,0:T(8,128)(2,1)S(1)}, bf16[16,6144]{1,0:T(8,128)(2,1)S(1)}, u32[]{:S(2)}, u32[]{:S(2)}) collective-permute-start(bf16[16,6144]{1,0:T(8,128)(2,1)S(1)} %get-tuple-element.98), channel_id=1, source_target_pairs={{0,2},{1,3},{2,0},{3,1},{4,6},{5,7},{6,4},{7,5},{8,10},{9,11},{10,... | collective-permute-start | bytes 589832 | tf_op jit(solution)/shard_map/ppermute | solution.py:54
